TPU v7x, 128 devices: a whole 4x4x4 slice. The times are simulated.
128 devices in a mesh: dp: 16 (over z, y_lo, core), block: 8 (over x, y_hi).
Axes of the slice: x: 4, y: 4 (y_hi: 2, y_lo: 2; y = y_hi * 2 + y_lo), z: 4, core: 2. Of those that a mesh axis runs over, the one named last changes fastest.
Arguments:
- activations: bfloat16 [16384, 7168], P('dp', 'block'), may hold values from -6 to 6
- out_grads: bfloat16 [16384, 2112], P('dp', 'block'), may hold values from -6 to 6
- act_basis: bfloat16 [7168, 7168], P('block', 'dp'), may hold values from -0.0625 to 0.0625
- grad_basis: bfloat16 [2112, 2112], P('block', 'dp'), may hold values from -0.125 to 0.125
- query_acts: bfloat16 [512, 7168], P(None, 'block'), may hold values from -6 to 6
- query_grads: bfloat16 [512, 2112], P(None, 'block'), may hold values from -6 to 6
Outputs:
- act_cov: float32 [7168, 7168], P('dp', 'block')
- grad_cov: float32 [2112, 2112], P('dp', 'block')
- rot_act: float32 [512, 7168], P(None, 'dp')
- rot_grad: float32 [512, 2112], P(None, 'dp')
All inputs are finite; a program needn't handle non-finite values.
Results may differ from a plain program's by a relative error of at most 0.0003.
Values may be sent and summed in bfloat16 or wider, within the bound.
No kernel may reach another device: no remote copies, remote signals or barrier semaphores. Data moves between devices by JAX's collectives and lax.ppermute only.
A program may use at most 192 MiB of HBM per device.

v0:
```python
import jax
import jax.numpy as jnp
from jax import lax
from jax.sharding import PartitionSpec as P


def transposed_product(left, right):
    return lax.dot_general(
        left, right, (((0,), (0,)), ((), ())), preferred_element_type=jnp.float32
    )


def on_device(activations, out_grads, act_basis, grad_basis, query_acts, query_grads):
    n_data = lax.axis_size("dp")
    tokens_total = activations.shape[0] * n_data
    act_part = jnp.dot(query_acts, act_basis, preferred_element_type=jnp.float32)
    rot_act = lax.psum(act_part, "block")
    act_whole = lax.all_gather(activations, "block", axis=1, tiled=True)
    picked = act_whole
    act_cov = (
        lax.psum_scatter(
            transposed_product(picked, activations), "dp", scatter_dimension=0, tiled=True
        )
        / tokens_total
    )
    grad_whole = lax.all_gather(out_grads, "block", axis=1, tiled=True)
    picked = grad_whole
    grad_cov = (
        lax.psum_scatter(
            transposed_product(picked, out_grads), "dp", scatter_dimension=0, tiled=True
        )
        / tokens_total
    )
    grad_part = jnp.dot(query_grads, grad_basis, preferred_element_type=jnp.float32)
    rot_grad = lax.psum(grad_part, "block")
    return (act_cov, grad_cov, rot_act, rot_grad)


def solution(mesh):
    return jax.shard_map(
        on_device,
        mesh=mesh,
        in_specs=(
            P("dp", "block"),
            P("dp", "block"),
            P("block", "dp"),
            P("block", "dp"),
            P(None, "block"),
            P(None, "block"),
        ),
        out_specs=(P("dp", "block"), P("dp", "block"), P(None, "dp"), P(None, "dp")),
        check_vma=False,
    )
```

profile of v0, /device:TPU:16, one launch (start us, length us, event | category | flops | bytes accessed | tf_op | source)
XLA Modules:
  0.0 661.5 jit_solution(3554861510246401239)
XLA Ops:
  7.2 0.7 all-gather.3.cloned.1.call-update
  7.9 0.0 all-gather.5.cloned.1.call-start
  8.0 0.7 all-gather.5.cloned.1.call-update
  8.7 0.0 reduce-scatter.4.cloned.1.call-start
  8.7 165.9 %all-gather.3.cloned.1.call-done = bf16[1024,7168]{1,0:T(8,128)(2,1)} async-done(((bf16[1024,896]{1,0:T(8,128)(2,1)}), bf16[1024,7168]{1,0:T(8,128)(2,1)}) %all-gather.3.cloned.1.call-update) | async-done | bytes 14680080 | tf_op jit(solution)/shard_map/all_gather | solution.py:18
  174.6 22.6 %fusion.1 = f32[7168,896]{1,0:T(8,128)} fusion(bf16[1024,7168]{1,0:T(8,128)(2,1)} %all-gather.3.cloned.1.call-done, bf16[1024,896]{1,0:T(8,128)(2,1)} %param.6), kind=kOutput, calls=%fused_computation.2 | convolution fusion | flops 13153337344 | bytes 42205184 | tf_op jit(solution)/shard_map/dot_general | solution.py:8
  197.2 0.0 all-reduce.5.cloned.1.call-start
  197.2 0.9 copy-done.3
  198.1 0.9 fusion.4
  199.1 1.6 fusion.3
  200.7 46.7 %all-gather.5.cloned.1.call-done = bf16[1024,2112]{0,1:T(8,128)(2,1)} async-done(((bf16[1024,264]{0,1:T(8,128)(2,1)}), bf16[1024,2112]{0,1:T(8,128)(2,1)}) %all-gather.5.cloned.1.call-update) | async-done | bytes 4325392 | tf_op jit(solution)/shard_map/all_gather | solution.py:26
  247.5 6.3 fusion.2
  253.8 82.9 %fusion = f32[144,264]{1,0:T(8,128)S(1)} fusion(f32[2112,264]{1,0:T(8,128)} %fusion.2), kind=kCustom, calls=%all-reduce-scatter | all-reduce-scatter fusion | flops 608257 | bytes 2382848
  336.7 1.3 collective-permute-start
  338.0 1.3 collective-permute-start.1
  339.3 0.6 dynamic-slice.4
  340.6 2.6 collective-permute-done.1
  343.2 0.6 concatenate
  343.8 0.7 dynamic-slice_multiply_fusion
  344.5 213.5 %reduce-scatter.4.cloned.1.call-done = f32[448,896]{1,0:T(8,128)} async-done(((f32[7168,896]{1,0:T(8,128)}), f32[448,896]{1,0:T(8,128)}) %reduce-scatter.4.cloned.1.call-update) | async-done | bytes 1605648 | tf_op jit(solution)/shard_map/reduce_scatter | solution.py:21
  558.0 2.7 broadcast_multiply_fusion
  560.7 90.4 %all-reduce.5.cloned.1.call-done = (f32[512,448]{0,1:T(8,128)}, f32[512,132]{0,1:T(8,128)}) async-done(((f32[512,448]{0,1:T(8,128)}, f32[512,132]{0,1:T(8,128)}), (f32[512,448]{0,1:T(8,128)}, f32[512,132]{0,1:T(8,128)})) %all-reduce.5.cloned.1.call-update) | async-done | bytes 1187856 | tf_op jit(solution)/shard_map/psum | solution.py:17
  651.1 2.2 copy.12
  653.2 1.7 copy.13
  (16 shorter events, 0.1 us)
Async XLA Ops:
  7.2 191.9 %copy-start = (bf16[512,896]{1,0:T(8,128)(2,1)S(1)}, bf16[512,896]{1,0:T(8,128)(2,1)}, u32[]{:S(2)}) copy-start(bf16[512,896]{1,0:T(8,128)(2,1)} %param.10) | copy-start | bytes 2752516
  7.2 167.4 %all-gather.3.cloned.1.call-start = ((), (), s32[]{:S(2)}) async-start(), calls=%async_computation.1 | async-start | bytes 16515072 | tf_op jit(solution)/shard_map/all_gather | solution.py:18
  7.9 239.5 %all-gather.5.cloned.1.call-start = ((), (), s32[]{:S(2)}) async-start(), calls=%async_computation.3 | async-start | bytes 4866048 | tf_op jit(solution)/shard_map/all_gather | solution.py:26
  8.7 549.3 %reduce-scatter.4.cloned.1.call-start = ((), (), s32[]{:S(2)}) async-start(), calls=%async_computation.2 | async-start | bytes 27295744 | tf_op jit(solution)/shard_map/reduce_scatter | solution.py:21
  197.2 1.0 copy-start.3
  197.2 1.0 copy-start.4
  197.2 1.9 copy-start.1
  197.2 50.3 %copy-start.2 = (bf16[1024,264]{0,1:T(8,128)(2,1)S(1)}, bf16[1024,264]{0,1:T(8,128)(2,1)}, u32[]{:S(2)}) copy-start(bf16[1024,264]{0,1:T(8,128)(2,1)} %param.7) | copy-start | bytes 1622020
  197.2 453.9 %all-reduce.5.cloned.1.call-start = ((), (), s32[]{:S(2)}) async-start(), calls=%async_computation.4 | async-start | bytes 2392064 | tf_op jit(solution)/shard_map/psum | solution.py:17
  253.8 85.6 %copy-start.5 = (u32[128]{0:T(128)S(1)}, u32[128]{0:T(128)}, u32[]{:S(2)}) copy-start(u32[128]{0:T(128)} %constant.8) | copy-start | bytes 1540
  336.7 6.5 collective-permute-start
  338.0 5.2 collective-permute-start.1
Sparse Core Ops, SparseCore 0:
  10.3 164.1 all-gather.2
  176.9 70.5 all-gather.4
  249.9 308.0 reduce-scatter.3
  561.0 90.0 all-reduce.4
where the time goes:
time: 664 us; the launch traced here: 661 us
  waiting for transfers between devices  521 us (78%)
  blocking collectives  82.9 us (12%)
  matrix products  31.4 us (5%)
  between operations  14.5 us (2%)
    reduce_scatter x1, waiting for transfers between devices, on_device(): lax.psum_scatter(transposed_product(picked, activations), 'dp', scatter_d...  214 us
    all_gather x1, waiting for transfers between devices, on_device(): act_whole = lax.all_gather(activations, 'block', axis=1, tiled=True)  166 us
    psum x1, waiting for transfers between devices, on_device(): rot_act = lax.psum(act_part, 'block')  90.4 us
    unnamed x1, blocking collectives  82.9 us
    all_gather x1, waiting for transfers between devices, on_device(): grad_whole = lax.all_gather(out_grads, 'block', axis=1, tiled=True)  46.7 us
    dot_general x2, matrix products, transposed_product(): lax.dot_general(left, right, (((0,), (0,)), ((), ())), preferred_element_...  28.9 us
  transfers between devices with their start and end apart: 6, of which 5 were waited for; matrix products, arithmetic and copies ran while one was open for 18% of the time, Pallas kernels for 0%

commit v1 on v0

v1 whole, which is shorter than its diff:
```python
import itertools

import jax
import jax.numpy as jnp
from jax import lax
from jax.sharding import PartitionSpec as P

AXES = ("dp", "block")
HALF = jnp.float16


def place(x, y, z, core):
    return ((z * 2 + y % 2) * 2 + core) * 8 + x * 2 + y // 2


def pairs(move):
    out = []
    for at in itertools.product(range(4), range(4), range(4), range(2)):
        x, y, z, core = move(*at)
        out.append((place(*at), place(x % 4, y % 4, z % 4, core % 2)))
    return out


SIBLING = pairs(lambda x, y, z, c: (x, y, z, c + 1))
OTHER_COLUMN = pairs(lambda x, y, z, c: (x, y + 2, z, c))
X_DOWN = pairs(lambda x, y, z, c: (x - 1, y, z, c))
X_UP = pairs(lambda x, y, z, c: (x + 1, y, z, c))
X_FAR = pairs(lambda x, y, z, c: (x + 2, y, z, c))
Z_ALONG = pairs(lambda x, y, z, c: (x, y, z + 1 - 2 * c, c))
Z_AGAINST = pairs(lambda x, y, z, c: (x, y, z - 1 + 2 * c, c))
Y_PARTNER = pairs(lambda x, y, z, c: (x, y ^ 1, z, c))
Y_MIDDLE = [p for p in pairs(lambda x, y, z, c: (x, (0, 2, 1, 3)[y], z, c)) if p[0] != p[1]]


def send(value, to):
    return lax.ppermute(value, AXES, to)


def transposed_product(left, right):
    return lax.dot_general(
        left, right, (((0,), (0,)), ((), ())), preferred_element_type=jnp.float32
    )


def covariance(own, tokens_total, where):
    x, y_hi, z, y_lo, core = where
    width = own.shape[1]
    half = width // 2

    largest = lax.pmax(jnp.max(jnp.abs(own)).astype(jnp.float32), AXES)
    largest = jnp.maximum(largest, 1e-18)
    down = 2.0 / (largest * largest)
    up = largest * largest * (0.5 / tokens_total)

    other = send(own, OTHER_COLUMN)
    sibling = send(own, SIBLING)
    other_sibling = send(other, SIBLING)

    def my_rows(block):
        return jnp.where(core == 0, block[:, :half], block[:, half:])

    rows = jnp.concatenate([my_rows(own), my_rows(sibling)], axis=0)
    rows_of = [rows, send(rows, X_DOWN), send(rows, X_FAR), send(rows, X_UP)]
    columns = jnp.concatenate(
        [
            jnp.concatenate([own, sibling], axis=0),
            jnp.concatenate([other, other_sibling], axis=0),
        ],
        axis=1,
    )
    partial = jnp.stack([transposed_product(r, columns) * down for r in rows_of])

    def toward(offset):
        return lax.dynamic_index_in_dim(partial, (z + offset - x) % 4, 0, keepdims=False)

    along = 1 - 2 * core
    first = send(toward(2).astype(HALF), Z_ALONG).astype(jnp.float32)
    third = send(toward(-along).astype(HALF), Z_AGAINST).astype(jnp.float32)
    second = send((toward(along) + first).astype(HALF), Z_ALONG).astype(jnp.float32)
    total = toward(0) + second + third

    total_own, total_other = total[:, :width], total[:, width:]
    stays = y_lo == y_hi
    near = send(jnp.where(stays, total_other, total_own).astype(HALF), Y_PARTNER)
    near = near.astype(jnp.float32)
    cross = send((total_other + near).astype(HALF), Y_MIDDLE).astype(jnp.float32)
    return jnp.where(stays, total_own + near, cross) * up


def on_device(activations, out_grads, act_basis, grad_basis, query_acts, query_grads):
    dp, block = lax.axis_index("dp"), lax.axis_index("block")
    where = (block // 2, block % 2, dp // 4, dp // 2 % 2, dp % 2)
    tokens_total = activations.shape[0] * lax.axis_size("dp")
    rot_act = lax.psum(
        jnp.dot(query_acts, act_basis, preferred_element_type=jnp.float32), "block"
    )
    rot_grad = lax.psum(
        jnp.dot(query_grads, grad_basis, preferred_element_type=jnp.float32), "block"
    )
    act_cov = covariance(activations, tokens_total, where)
    grad_cov = covariance(out_grads, tokens_total, where)
    return (act_cov, grad_cov, rot_act, rot_grad)


def solution(mesh):
    return jax.shard_map(
        on_device,
        mesh=mesh,
        in_specs=(
            P("dp", "block"),
            P("dp", "block"),
            P("block", "dp"),
            P("block", "dp"),
            P(None, "block"),
            P(None, "block"),
        ),
        out_specs=(P("dp", "block"), P("dp", "block"), P(None, "dp"), P(None, "dp")),
        check_vma=False,
    )
```

time: 664 us -> 402 us (0.61)
  waiting for transfers between devices: 521 us -> 179 us
  matrix products: 31.4 us -> 66.5 us
  starting transfers between devices: 2.75 us -> 31 us
  other arithmetic: 3.39 us -> 27.7 us
  blocking collectives: 82.9 us -> 67.2 us
    reduce_scatter x1 -> x0, waiting for transfers between devices: 214 us -> none  [on_device(): lax.psum_scatter(transposed_product(picked, activations), 'dp', scatter_d...]
    all_gather x2 -> x0, waiting for transfers between devices: 213 us -> none  [the longest x1 166 us: on_device(): act_whole = lax.all_gather(activations, 'block', axis=1, tiled=True)]
    ppermute x0 -> x22, waiting for transfers between devices: none -> 149 us  [send(): return lax.ppermute(value, AXES, to)]
    unnamed x1 -> x0, blocking collectives: 82.9 us -> none
    pmax x0 -> x1, blocking collectives: none -> 67.2 us  [covariance(): largest = lax.pmax(jnp.max(jnp.abs(own)).astype(jnp.float32), AXES)]
    psum x1, waiting for transfers between devices: 90.4 us -> 30.5 us  [on_device(): lax.psum(jnp.dot(query_acts, act_basis, preferred_element_type=jnp.float3...]
    dot_general x2 -> x8, matrix products: 28.9 us -> 64 us  [transposed_product(): lax.dot_general(left, right, (((0,), (0,)), ((), ())), preferred_element_...]
    ppermute x0 -> x22, starting transfers between devices: none -> 31 us  [send(): return lax.ppermute(value, AXES, to)]
  transfers between devices with their start and end apart: 6 -> 23, of which waited for: 5 -> 14; matrix products, arithmetic and copies ran while one was open for 18% -> 19% of each run, Pallas kernels for 0% -> 0%
where the time goes in v1:
time: 402 us; the launch traced here: 399 us
  waiting for transfers between devices  179 us (45%)
  blocking collectives  67.2 us (17%)
  matrix products  66.5 us (17%)
  starting transfers between devices  31 us (8%)
  other arithmetic  27.7 us (7%)
  between operations  15.6 us (4%)
  local copies, waits for them, and re-layouts  11.5 us (3%)
    ppermute x22, waiting for transfers between devices, send(): return lax.ppermute(value, AXES, to)  149 us
    pmax x1, blocking collectives, covariance(): largest = lax.pmax(jnp.max(jnp.abs(own)).astype(jnp.float32), AXES)  67.2 us
    dot_general x8, matrix products, transposed_product(): lax.dot_general(left, right, (((0,), (0,)), ((), ())), preferred_element_...  64 us
    ppermute x22, starting transfers between devices, send(): return lax.ppermute(value, AXES, to)  31 us
    psum x1, waiting for transfers between devices, on_device(): lax.psum(jnp.dot(query_acts, act_basis, preferred_element_type=jnp.float3...  30.5 us
    unnamed x33, local copies, waits for them, and re-layouts  11.5 us
  transfers between devices with their start and end apart: 23, of which 14 were waited for; matrix products, arithmetic and copies ran while one was open for 19% of the time, Pallas kernels for 0%

profile of v1, /device:TPU:16, one launch (start us, length us, event | category | flops | bytes accessed | tf_op | source)
XLA Modules:
  0.0 398.9 jit_solution(3584684812272791106)
XLA Ops:
  10.8 3.4 collective-permute-done
  18.7 35.6 %collective-permute-done.1 = bf16[1024,896]{0,1:T(8,128)(2,1)} collective-permute-done((bf16[1024,896]{0,1:T(8,128)(2,1)S(1)}, bf16[1024,896]{0,1:T(8,128)(2,1)}, u32[]{:S(2)}, u32[]{:S(2)}) %collective-permute-start.1) | collective-permute-done | bytes 1835040 | tf_op jit(solution)/shard_map/ppermute | solution.py:36
  55.9 67.2 %all-reduce = (f32[]{:T(128)}, f32[]{:T(128)}) all-reduce(bf16[]{:T(256)} %abs_reduce_fusion, bf16[]{:T(256)} %abs_reduce_fusion.1), channel_id=1, replica_groups=mesh['dp'=16,'block'=8] {'dp','block'}, use_global_device_ids=true, to_apply=%region_1.2 | all-reduce | flops 2 | bytes 12 | tf_op jit(solution)/shard_map/pmax | solution.py:50
  126.9 13.4 %multiply_bitcast_fusion = f32[1,448,1792]{2,1,0:T(8,128)S(1)} fusion(bf16[2048,448]{0,1:T(8,128)(2,1)} %collective-permute-done.5, f32[]{:T(128)S(6)} %div.31, bf16[1024,896]{0,1:T(8,128)(2,1)} %collective-permute-done.2, bf16[1024,896]{0,1:T(8,128)(2,1)} %collective-permute-done.1, bf16[1024,896]{0,1:T(8,128)(2,1)} %collective-permute-done, ...), kind=kOutput, calls=%fused_computation.8 | convolution fusion | flops 3318497280 | bytes 12386308 | tf_op jit(solution)/shard_map/dot_general | solution.py:40
  140.4 12.9 %multiply_bitcast_fusion.3 = f32[1,448,1792]{2,1,0:T(8,128)S(1)} fusion(f32[]{:T(128)S(6)} %div.31, bf16[1024,448]{0,1:T(8,128)(2,1)S(1)} %copy-done.7, bf16[1024,448]{0,1:T(8,128)(2,1)S(1)} %copy-done.5, bf16[1024,896]{0,1:T(8,128)(2,1)} %collective-permute-done.2, bf16[1024,896]{0,1:T(8,128)(2,1)} %collective-permute-done.1, ...), kind=kOutput, calls=%fused_computation.11 | convolution fusion | flops 3322167296 | bytes 12386308 | tf_op jit(solution)/shard_map/dot_general | solution.py:40
  153.3 13.6 %collective-permute-done.4 = bf16[2048,448]{0,1:T(8,128)(2,1)S(1)} collective-permute-done((bf16[2048,448]{0,1:T(8,128)(2,1)}, bf16[2048,448]{0,1:T(8,128)(2,1)S(1)}, u32[]{:S(2)}, u32[]{:S(2)}) %collective-permute-start.4) | collective-permute-done | bytes 1835040 | tf_op jit(solution)/shard_map/ppermute | solution.py:36
  167.0 14.1 %multiply_bitcast_fusion.1 = f32[1,448,1792]{2,1,0:T(8,128)S(1)} fusion(bf16[2048,448]{0,1:T(8,128)(2,1)S(1)} %collective-permute-done.4, f32[]{:T(128)S(6)} %div.31, bf16[1024,896]{0,1:T(8,128)(2,1)} %collective-permute-done.2, bf16[1024,896]{0,1:T(8,128)(2,1)} %collective-permute-done.1, bf16[1024,896]{0,1:T(8,128)(2,1)} %collective-permute-done, ...), kind=kOutput, calls=%fused_computation.9 | convolution fusion | flops 3318497280 | bytes 12386308 | tf_op jit(solution)/shard_map/dot_general | solution.py:40
  181.0 24.5 %collective-permute-done.3 = bf16[2048,448]{0,1:T(8,128)(2,1)S(1)} collective-permute-done((bf16[2048,448]{0,1:T(8,128)(2,1)}, bf16[2048,448]{0,1:T(8,128)(2,1)S(1)}, u32[]{:S(2)}, u32[]{:S(2)}) %collective-permute-start.3) | collective-permute-done | bytes 1835040 | tf_op jit(solution)/shard_map/ppermute | solution.py:36
  205.5 14.1 %multiply_bitcast_fusion.2 = f32[1,448,1792]{2,1,0:T(8,128)S(1)} fusion(bf16[2048,448]{0,1:T(8,128)(2,1)S(1)} %collective-permute-done.3, f32[]{:T(128)S(6)} %div.31, bf16[1024,896]{0,1:T(8,128)(2,1)} %collective-permute-done.2, bf16[1024,896]{0,1:T(8,128)(2,1)} %collective-permute-done.1, bf16[1024,896]{0,1:T(8,128)(2,1)} %collective-permute-done, ...), kind=kOutput, calls=%fused_computation.10 | convolution fusion | flops 3318497280 | bytes 12386308 | tf_op jit(solution)/shard_map/dot_general | solution.py:40
  220.7 4.6 %copy-done.1 = f32[4,448,1792]{2,1,0:T(8,128)} copy-done((f32[4,448,1792]{2,1,0:T(8,128)}, f32[4,448,1792]{2,1,0:T(8,128)S(1)}, u32[]{:S(2)}) %copy-start.1) | copy-done | bytes 12845080
  235.4 7.9 %collective-permute-done.12 = bf16[1024,264]{0,1:T(8,128)(2,1)} collective-permute-done((bf16[1024,264]{0,1:T(8,128)(2,1)S(1)}, bf16[1024,264]{0,1:T(8,128)(2,1)}, u32[]{:S(2)}, u32[]{:S(2)}) %collective-permute-start.12) | collective-permute-done | bytes 540704 | tf_op jit(solution)/shard_map/ppermute | solution.py:36
  243.3 3.1 collective-permute-start.8
  246.4 3.3 collective-permute-done.6
  249.7 3.9 fusion
  263.2 5.4 %collective-permute-done.15 = bf16[2048,132]{0,1:T(8,128)(2,1)S(1)} collective-permute-done((bf16[2048,132]{0,1:T(8,128)(2,1)}, bf16[2048,132]{0,1:T(8,128)(2,1)S(1)}, u32[]{:S(2)}, u32[]{:S(2)}) %collective-permute-start.15) | collective-permute-done | bytes 540704 | tf_op jit(solution)/shard_map/ppermute | solution.py:36
  271.0 10.3 %collective-permute-done.14 = bf16[2048,132]{0,1:T(8,128)(2,1)S(1)} collective-permute-done((bf16[2048,132]{0,1:T(8,128)(2,1)}, bf16[2048,132]{0,1:T(8,128)(2,1)S(1)}, u32[]{:S(2)}, u32[]{:S(2)}) %collective-permute-start.14) | collective-permute-done | bytes 540704 | tf_op jit(solution)/shard_map/ppermute | solution.py:36
  284.7 3.3 fusion.1
  299.4 3.3 collective-permute-done.18
  303.8 4.2 %collective-permute-done.9 = f16[448,896]{1,0:T(8,128)(2,1)S(1)} collective-permute-done((f16[448,896]{1,0:T(8,128)(2,1)}, f16[448,896]{1,0:T(8,128)(2,1)S(1)}, u32[]{:S(2)}, u32[]{:S(2)}) %collective-permute-start.9) | collective-permute-done | bytes 802848 | tf_op jit(solution)/shard_map/ppermute | solution.py:36
  309.6 7.3 %collective-permute-start.10 = (f16[448,896]{1,0:T(8,128)(2,1)S(1)}, f16[448,896]{1,0:T(8,128)(2,1)}, u32[]{:S(2)}, u32[]{:S(2)}) collective-permute-start(f16[448,896]{1,0:T(8,128)(2,1)S(1)} %fusion.4), channel_id=1, source_target_pairs={{16,1},{24,9},{48,33},{56,41},{80,65},{88,73},{112,97},{120,105},{... | collective-permute-start | bytes 2408456 | tf_op jit(solution)/shard_map/ppermute | solution.py:36
  317.1 8.5 %collective-permute-done.20 = f16[132,264]{1,0:T(8,128)(2,1)S(1)} collective-permute-done((f16[132,264]{1,0:T(8,128)(2,1)S(1)}, f16[132,264]{1,0:T(8,128)(2,1)S(1)}, u32[]{:S(2)}, u32[]{:S(2)}) %collective-permute-start.20) | collective-permute-done | bytes 69728 | tf_op jit(solution)/shard_map/ppermute | solution.py:36
  327.9 26.0 %collective-permute-done.21 = f16[132,264]{1,0:T(8,128)(2,1)S(1)} collective-permute-done((f16[132,264]{1,0:T(8,128)(2,1)S(1)}, f16[132,264]{1,0:T(8,128)(2,1)S(1)}, u32[]{:S(2)}, u32[]{:S(2)}) %collective-permute-start.21) | collective-permute-done | bytes 69728 | tf_op jit(solution)/shard_map/ppermute | solution.py:36
  354.6 3.2 fusion.3
  357.8 30.5 %all-reduce.4.cloned.1.call-done = (f32[512,448]{0,1:T(8,128)}, f32[512,132]{0,1:T(8,128)}) async-done(((f32[512,448]{0,1:T(8,128)}, f32[512,132]{0,1:T(8,128)}), (f32[512,448]{0,1:T(8,128)}, f32[512,132]{0,1:T(8,128)})) %all-reduce.4.cloned.1.call-update) | async-done | bytes 1187856 | tf_op jit(solution)/shard_map/psum | solution.py:94
  (89 shorter events, 59.5 us)
Async XLA Ops:
  7.2 283.3 %copy-start = (bf16[512,896]{1,0:T(8,128)(2,1)S(1)}, bf16[512,896]{1,0:T(8,128)(2,1)}, u32[]{:S(2)}) copy-start(bf16[512,896]{1,0:T(8,128)(2,1)} %param.10) | copy-start | bytes 2752516
  7.2 381.1 %all-reduce.4.cloned.1.call-start = ((), (), s32[]{:S(2)}) async-start(), calls=%async_computation | async-start | bytes 2392064 | tf_op jit(solution)/shard_map/psum | solution.py:94
  10.2 4.0 %collective-permute-start = (bf16[1024,896]{0,1:T(8,128)(2,1)S(1)}, bf16[1024,896]{0,1:T(8,128)(2,1)}, u32[]{:S(2)}, u32[]{:S(2)}) collective-permute-start(bf16[1024,896]{0,1:T(8,128)(2,1)S(1)} %copy.10), channel_id=1, source_target_pairs={{0,8},{8,0},{32,40},{40,32},{64,72},{72,64},{96,104},{104,96},{16,... | collective-permute-start | bytes 5505032 | tf_op jit(solution)/shard_map/ppermute | solution.py:36
  10.3 44.0 %collective-permute-start.1 = (bf16[1024,896]{0,1:T(8,128)(2,1)S(1)}, bf16[1024,896]{0,1:T(8,128)(2,1)}, u32[]{:S(2)}, u32[]{:S(2)}) collective-permute-start(bf16[1024,896]{0,1:T(8,128)(2,1)S(1)} %copy.10), channel_id=1, source_target_pairs={{0,1},{8,9},{32,33},{40,41},{64,65},{72,73},{96,97},{104,105},{16,... | collective-permute-start | bytes 5505032 | tf_op jit(solution)/shard_map/ppermute | solution.py:36
  17.2 109.7 %collective-permute-start.5 = (bf16[2048,448]{0,1:T(8,128)(2,1)}, bf16[2048,448]{0,1:T(8,128)(2,1)}, u32[]{:S(2)}, u32[]{:S(2)}) collective-permute-start(bf16[2048,448]{0,1:T(8,128)(2,1)} %pad_maximum_fusion.1), channel_id=1, source_target_pairs={{0,2},{8,10},{32,34},{40,42},{64,66},{72,74},{96,98},{104,106},{16... | collective-permute-start | bytes 5505032 | tf_op jit(solution)/shard_map/ppermute | solution.py:36
  54.3 72.6 %collective-permute-start.2 = (bf16[1024,896]{0,1:T(8,128)(2,1)}, bf16[1024,896]{0,1:T(8,128)(2,1)}, u32[]{:S(2)}, u32[]{:S(2)}) collective-permute-start(bf16[1024,896]{0,1:T(8,128)(2,1)} %collective-permute-done.1), channel_id=1, source_target_pairs={{0,8},{8,0},{32,40},{40,32},{64,72},{72,64},{96,104},{104,96},{16,... | collective-permute-start | bytes 5505032 | tf_op jit(solution)/shard_map/ppermute | solution.py:36
  123.7 43.3 %collective-permute-start.4 = (bf16[2048,448]{0,1:T(8,128)(2,1)}, bf16[2048,448]{0,1:T(8,128)(2,1)S(1)}, u32[]{:S(2)}, u32[]{:S(2)}) collective-permute-start(bf16[2048,448]{0,1:T(8,128)(2,1)} %pad_maximum_fusion.1), channel_id=1, source_target_pairs={{0,4},{8,12},{32,36},{40,44},{64,68},{72,76},{96,100},{104,108},{1... | collective-permute-start | bytes 5505032 | tf_op jit(solution)/shard_map/ppermute | solution.py:36
  124.9 80.6 %collective-permute-start.3 = (bf16[2048,448]{0,1:T(8,128)(2,1)}, bf16[2048,448]{0,1:T(8,128)(2,1)S(1)}, u32[]{:S(2)}, u32[]{:S(2)}) collective-permute-start(bf16[2048,448]{0,1:T(8,128)(2,1)} %pad_maximum_fusion.1), channel_id=1, source_target_pairs={{0,6},{8,14},{32,38},{40,46},{64,70},{72,78},{96,102},{104,110},{1... | collective-permute-start | bytes 5505032 | tf_op jit(solution)/shard_map/ppermute | solution.py:36
  226.9 22.9 %collective-permute-start.6 = (f16[448,1792]{1,0:T(8,128)(2,1)S(1)}, f16[448,1792]{1,0:T(8,128)(2,1)}, u32[]{:S(2)}, u32[]{:S(2)}) collective-permute-start(f16[448,1792]{1,0:T(8,128)(2,1)S(1)} %get-tuple-element.8), channel_id=1, source_target_pairs={{0,32},{8,104},{32,64},{40,8},{64,96},{72,40},{96,0},{104,72},{16,... | collective-permute-start | bytes 4816904 | tf_op jit(solution)/shard_map/ppermute | solution.py:36
  227.0 3.0 collective-permute-start.11
  227.0 16.3 %collective-permute-start.12 = (bf16[1024,264]{0,1:T(8,128)(2,1)S(1)}, bf16[1024,264]{0,1:T(8,128)(2,1)}, u32[]{:S(2)}, u32[]{:S(2)}) collective-permute-start(bf16[1024,264]{0,1:T(8,128)(2,1)S(1)} %copy-done.8), channel_id=1, source_target_pairs={{0,1},{8,9},{32,33},{40,41},{64,65},{72,73},{96,97},{104,105},{16,... | collective-permute-start | bytes 1622024 | tf_op jit(solution)/shard_map/ppermute | solution.py:36
  233.0 23.4 %collective-permute-start.16 = (bf16[2048,132]{0,1:T(8,128)(2,1)}, bf16[2048,132]{0,1:T(8,128)(2,1)}, u32[]{:S(2)}, u32[]{:S(2)}) collective-permute-start(bf16[2048,132]{0,1:T(8,128)(2,1)} %pad_maximum_fusion.3), channel_id=1, source_target_pairs={{0,2},{8,10},{32,34},{40,42},{64,66},{72,74},{96,98},{104,106},{16... | collective-permute-start | bytes 1622024 | tf_op jit(solution)/shard_map/ppermute | solution.py:36
  243.3 15.1 %collective-permute-start.13 = (bf16[1024,264]{0,1:T(8,128)(2,1)}, bf16[1024,264]{0,1:T(8,128)(2,1)}, u32[]{:S(2)}, u32[]{:S(2)}) collective-permute-start(bf16[1024,264]{0,1:T(8,128)(2,1)} %collective-permute-done.12), channel_id=1, source_target_pairs={{0,8},{8,0},{32,40},{40,32},{64,72},{72,64},{96,104},{104,96},{16,... | collective-permute-start | bytes 1622024 | tf_op jit(solution)/shard_map/ppermute | solution.py:36
  243.3 41.4 %collective-permute-start.8 = (f16[448,1792]{1,0:T(8,128)(2,1)}, f16[448,1792]{1,0:T(8,128)(2,1)}, u32[]{:S(2)}, u32[]{:S(2)}) collective-permute-start(f16[448,1792]{1,0:T(8,128)(2,1)} %get-tuple-element.9), channel_id=1, source_target_pairs={{0,96},{8,40},{32,0},{40,72},{64,32},{72,104},{96,64},{104,8},{16,... | collective-permute-start | bytes 4816904 | tf_op jit(solution)/shard_map/ppermute | solution.py:36
  253.7 31.0 %collective-permute-start.7 = (f16[448,1792]{1,0:T(8,128)(2,1)}, f16[448,1792]{1,0:T(8,128)(2,1)}, u32[]{:S(2)}, u32[]{:S(2)}) collective-permute-start(f16[448,1792]{1,0:T(8,128)(2,1)} %fusion), channel_id=1, source_target_pairs={{0,32},{8,104},{32,64},{40,8},{64,96},{72,40},{96,0},{104,72},{16,... | collective-permute-start | bytes 4816904 | tf_op jit(solution)/shard_map/ppermute | solution.py:36
  254.3 14.3 %collective-permute-start.15 = (bf16[2048,132]{0,1:T(8,128)(2,1)}, bf16[2048,132]{0,1:T(8,128)(2,1)S(1)}, u32[]{:S(2)}, u32[]{:S(2)}) collective-permute-start(bf16[2048,132]{0,1:T(8,128)(2,1)} %pad_maximum_fusion.3), channel_id=1, source_target_pairs={{0,4},{8,12},{32,36},{40,44},{64,68},{72,76},{96,100},{104,108},{1... | collective-permute-start | bytes 1622024 | tf_op jit(solution)/shard_map/ppermute | solution.py:36
  256.4 24.8 %collective-permute-start.14 = (bf16[2048,132]{0,1:T(8,128)(2,1)}, bf16[2048,132]{0,1:T(8,128)(2,1)S(1)}, u32[]{:S(2)}, u32[]{:S(2)}) collective-permute-start(bf16[2048,132]{0,1:T(8,128)(2,1)} %pad_maximum_fusion.3), channel_id=1, source_target_pairs={{0,6},{8,14},{32,38},{40,46},{64,70},{72,78},{96,102},{104,110},{1... | collective-permute-start | bytes 1622024 | tf_op jit(solution)/shard_map/ppermute | solution.py:36
  284.4 10.6 %collective-permute-start.17 = (f16[132,528]{1,0:T(8,128)(2,1)S(1)}, f16[132,528]{1,0:T(8,128)(2,1)S(1)}, u32[]{:S(2)}, u32[]{:S(2)}) collective-permute-start(f16[132,528]{1,0:T(8,128)(2,1)S(1)} %get-tuple-element.10), channel_id=1, source_target_pairs={{0,32},{8,104},{32,64},{40,8},{64,96},{72,40},{96,0},{104,72},{16,... | collective-permute-start | bytes 418184 | tf_op jit(solution)/shard_map/ppermute | solution.py:36
  289.1 18.8 %collective-permute-start.9 = (f16[448,896]{1,0:T(8,128)(2,1)}, f16[448,896]{1,0:T(8,128)(2,1)S(1)}, u32[]{:S(2)}, u32[]{:S(2)}) collective-permute-start(f16[448,896]{1,0:T(8,128)(2,1)} %select_convert_fusion), channel_id=1, source_target_pairs={{0,16},{8,24},{32,48},{40,56},{64,80},{72,88},{96,112},{104,120},{... | collective-permute-start | bytes 2408456 | tf_op jit(solution)/shard_map/ppermute | solution.py:36
  292.1 7.3 %collective-permute-start.19 = (f16[132,528]{1,0:T(8,128)(2,1)}, f16[132,528]{1,0:T(8,128)(2,1)}, u32[]{:S(2)}, u32[]{:S(2)}) collective-permute-start(f16[132,528]{1,0:T(8,128)(2,1)} %get-tuple-element.11), channel_id=1, source_target_pairs={{0,96},{8,40},{32,0},{40,72},{64,32},{72,104},{96,64},{104,8},{16,... | collective-permute-start | bytes 418184 | tf_op jit(solution)/shard_map/ppermute | solution.py:36
  295.7 7.0 %collective-permute-start.18 = (f16[132,528]{1,0:T(8,128)(2,1)}, f16[132,528]{1,0:T(8,128)(2,1)}, u32[]{:S(2)}, u32[]{:S(2)}) collective-permute-start(f16[132,528]{1,0:T(8,128)(2,1)} %fusion.11), channel_id=1, source_target_pairs={{0,32},{8,104},{32,64},{40,8},{64,96},{72,40},{96,0},{104,72},{16,... | collective-permute-start | bytes 418184 | tf_op jit(solution)/shard_map/ppermute | solution.py:36
  309.6 45.0 %collective-permute-start.10 = (f16[448,896]{1,0:T(8,128)(2,1)S(1)}, f16[448,896]{1,0:T(8,128)(2,1)}, u32[]{:S(2)}, u32[]{:S(2)}) collective-permute-start(f16[448,896]{1,0:T(8,128)(2,1)S(1)} %fusion.4), channel_id=1, source_target_pairs={{16,1},{24,9},{48,33},{56,41},{80,65},{88,73},{112,97},{120,105},{... | collective-permute-start | bytes 2408456 | tf_op jit(solution)/shard_map/ppermute | solution.py:36
  317.0 8.6 %collective-permute-start.20 = (f16[132,264]{1,0:T(8,128)(2,1)S(1)}, f16[132,264]{1,0:T(8,128)(2,1)S(1)}, u32[]{:S(2)}, u32[]{:S(2)}) collective-permute-start(f16[132,264]{1,0:T(8,128)(2,1)S(1)} %select_convert_fusion.1), channel_id=1, source_target_pairs={{0,16},{8,24},{32,48},{40,56},{64,80},{72,88},{96,112},{104,120},{... | collective-permute-start | bytes 209096 | tf_op jit(solution)/shard_map/ppermute | solution.py:36
  325.8 28.1 %collective-permute-start.21 = (f16[132,264]{1,0:T(8,128)(2,1)S(1)}, f16[132,264]{1,0:T(8,128)(2,1)S(1)}, u32[]{:S(2)}, u32[]{:S(2)}) collective-permute-start(f16[132,264]{1,0:T(8,128)(2,1)S(1)} %fusion.15), channel_id=1, source_target_pairs={{16,1},{24,9},{48,33},{56,41},{80,65},{88,73},{112,97},{120,105},{... | collective-permute-start | bytes 209096 | tf_op jit(solution)/shard_map/ppermute | solution.py:36
  (14 other events, 214.2 us)
Sparse Core Ops, SparseCore 0:
  296.8 91.3 all-reduce.3

commit v2 on v0

v2 whole, which is shorter than its diff:
```python
import functools
import itertools

import jax
import jax.numpy as jnp
from jax import lax
from jax.experimental import pallas as pl
from jax.experimental.pallas import tpu as pltpu
from jax.sharding import PartitionSpec as P

AXES = ("dp", "block")
HALF = jnp.float16
MARK = 8


def place(x, y, z, core):
    return ((z * 2 + y % 2) * 2 + core) * 8 + x * 2 + y // 2


def pairs(move):
    out = []
    for at in itertools.product(range(4), range(4), range(4), range(2)):
        x, y, z, core = move(*at)
        out.append((place(*at), place(x % 4, y % 4, z % 4, core % 2)))
    return out


SIBLING = pairs(lambda x, y, z, c: (x, y, z, c + 1))
OTHER_COLUMN = pairs(lambda x, y, z, c: (x, y + 2, z, c))
X_FAR = pairs(lambda x, y, z, c: (x + 2, y, z, c))
X_FLIP = pairs(lambda x, y, z, c: (x ^ 1, y, z, c))
Z_ALONG = pairs(lambda x, y, z, c: (x, y, z + 1 - 2 * c, c))
Z_AGAINST = pairs(lambda x, y, z, c: (x, y, z - 1 + 2 * c, c))
X_RINGS = [
    [place(x, y, z, c) for x in range(4)]
    for y, z, c in itertools.product(range(4), range(4), range(2))
]
CHUNKS = ((0, 224), (224, 448))
Y_PARTNER = pairs(lambda x, y, z, c: (x, y ^ 1, z, c))
Y_MIDDLE = [p for p in pairs(lambda x, y, z, c: (x, (0, 2, 1, 3)[y], z, c)) if p[0] != p[1]]


def send(value, to):
    return lax.ppermute(value, AXES, to)


def turn_kernel(core, own, mine, theirs, turned):
    half = mine.shape[0]
    turned[...] = own[...].T
    mine[...] = turned[pl.ds(pl.multiple_of(core[0] * half, 16), half), :]
    theirs[...] = turned[pl.ds(pl.multiple_of((1 - core[0]) * half, 16), half), :]


def turn(own, core):
    tokens, width = own.shape
    vmem = pl.BlockSpec(memory_space=pltpu.VMEM)
    half = jax.ShapeDtypeStruct((width // 2, tokens), own.dtype)
    return pl.pallas_call(
        turn_kernel,
        out_shape=(half, half),
        in_specs=[pl.BlockSpec(memory_space=pltpu.SMEM), vmem],
        out_specs=(vmem, vmem),
        scratch_shapes=[pltpu.VMEM((width, tokens), own.dtype)],
        compiler_params=pltpu.CompilerParams(vmem_limit_bytes=24 << 20),
    )(core.reshape(1).astype(jnp.int32), own)


def product_kernel(turned, slot, rows, own, sib, oth, oth_sib, out, top, held, sem):
    blocks, _, n, _ = rows.shape
    step = pl.program_id(0)
    contract = (((1,), (1 if turned else 0,)), ((), ()))
    dot = functools.partial(
        lax.dot_general, dimension_numbers=contract, preferred_element_type=jnp.float32
    )

    @pl.when(step == 0)
    def _():
        copies = [
            pltpu.make_async_copy(
                rows.at[d],
                held.at[:, pl.ds(pl.multiple_of(slot[d] * n, 16), n), :],
                sem.at[d],
            )
            for d in range(blocks)
        ]
        for copy in copies:
            copy.start()
        for copy in copies:
            copy.wait()
        top[...] = jnp.zeros_like(top)

    def product(left, right):
        value = dot(held[0], left[...]) + dot(held[1], right[...])
        out[0] = value.reshape(out.shape[1:])
        top[...] = jnp.maximum(top[...], jnp.max(jnp.abs(value)))

    @pl.when(step == 0)
    def _():
        product(own, sib)

    @pl.when(step == 1)
    def _():
        product(oth, oth_sib)


def products(slot, rows, columns, turned=False):
    blocks, _, n, tokens = rows.shape
    width = columns[0].shape[0 if turned else 1]
    whole = pl.BlockSpec(columns[0].shape, lambda step, slot: (0, 0))
    out, top = pl.pallas_call(
        functools.partial(product_kernel, turned),
        out_shape=(
            jax.ShapeDtypeStruct((2, blocks, n, width), jnp.float32),
            jax.ShapeDtypeStruct((8, 128), jnp.float32),
        ),
        grid_spec=pltpu.PrefetchScalarGridSpec(
            num_scalar_prefetch=1,
            grid=(2,),
            in_specs=[pl.BlockSpec(memory_space=pl.ANY)] + [whole] * 4,
            out_specs=(
                pl.BlockSpec((1, blocks, n, width), lambda step, slot: (step, 0, 0, 0)),
                pl.BlockSpec((8, 128), lambda step, slot: (0, 0)),
            ),
            scratch_shapes=[
                pltpu.VMEM((2, blocks * n, tokens), rows.dtype),
                pltpu.SemaphoreType.DMA((blocks,)),
            ],
        ),
        compiler_params=pltpu.CompilerParams(vmem_limit_bytes=50 << 20),
        cost_estimate=pl.CostEstimate(
            flops=4 * blocks * n * tokens * width,
            bytes_accessed=4 * blocks * n * tokens,
            transcendentals=0,
        ),
    )(slot, rows, *columns)
    return out, jnp.clip(jnp.ceil(jnp.log2(top[0, 0])), -100.0, 100.0) - 15.0


def message(value, exponent):
    marks = value.shape[:-2] + (MARK, value.shape[-1])
    return jnp.concatenate(
        [
            (value * jnp.exp2(-exponent)).astype(HALF),
            jnp.broadcast_to(exponent, marks).astype(HALF),
        ],
        axis=-2,
    )


def read(got):
    n = got.shape[-2] - MARK
    exponent = got[..., n : n + 1, :].astype(jnp.float32)
    return got[..., :n, :].astype(jnp.float32) * jnp.exp2(exponent), exponent


def far(p):
    a = send(message(p["partial"][:, 2], p["exponent"]), Z_ALONG)
    c = send(message(p["partial"][:, 3], p["exponent"]), Z_AGAINST)
    return {**p, "a": a, "c": c}


def along(p):
    first, first_exp = read(p.pop("a"))
    exponent = jnp.maximum(first_exp, p["exponent"]) + 1.0
    return {**p, "b": send(message(p["partial"][:, 1] + first, exponent), Z_ALONG)}


def near(p):
    second, second_exp = read(p["b"])
    third, third_exp = read(p["c"])
    total = p["partial"][:, 0] + second + third
    top = jnp.maximum(jnp.maximum(second_exp, third_exp), p["exponent"]) + 2.0
    value = jnp.where(p["stays"], total[1], total[0])
    n = send(message(value, jnp.where(p["stays"], top[1], top[0])), Y_PARTNER)
    return {"total": total, "top": top, "stays": p["stays"], "n": n}


def cross(p):
    value, exponent = read(p["n"])
    exponent = jnp.maximum(p["top"][1], exponent) + 1.0
    return {**p, "m": send(message(p["total"][1] + value, exponent), Y_MIDDLE)}


def result(p):
    near, _ = read(p["n"])
    cross, _ = read(p["m"])
    return jnp.where(p["stays"], p["total"][0] + near, cross)


def halve(value, bit, to):
    rows = value.shape[0] // 2
    keep = lax.dynamic_slice_in_dim(value, bit * rows, rows, 0)
    give = lax.dynamic_slice_in_dim(value, (1 - bit) * rows, rows, 0)
    return keep + send(give, to)


def double(value, bit, to):
    got = send(value, to)
    return jnp.where(
        bit == 0,
        jnp.concatenate([value, got], axis=0),
        jnp.concatenate([got, value], axis=0),
    )


def round_x(rows):
    return lax.all_gather(rows, AXES, axis_index_groups=X_RINGS)


def on_device(activations, out_grads, act_basis, grad_basis, query_acts, query_grads):
    dp, block = lax.axis_index("dp"), lax.axis_index("block")
    x, y_hi, z, y_lo, core = block // 2, block % 2, dp // 4, dp // 2 % 2, dp % 2
    up = 1.0 / (activations.shape[0] * lax.axis_size("dp"))
    slot = jnp.stack([((d - z) * (1 - 2 * core)) % 4 for d in range(4)]).astype(jnp.int32)

    other = send(activations, OTHER_COLUMN)
    mine, theirs = turn(activations, core)
    got = send(theirs, SIBLING)
    rows = []
    for start, end in CHUNKS:
        rows.append(round_x(jnp.stack([mine[start:end], got[start:end]])))
    half = out_grads.shape[1] // 2
    grads = out_grads.T
    mine = lax.dynamic_slice_in_dim(grads, core * half, half, 0)
    theirs = lax.dynamic_slice_in_dim(grads, (1 - core) * half, half, 0)
    grad_rows = jnp.stack([mine, send(theirs, SIBLING)])
    rows.append(round_x(jnp.pad(grad_rows, ((0, 0), (0, -half % 16), (0, 0)))))
    sibling = send(activations, SIBLING)
    grad_sibling = send(grads, SIBLING)
    act_part = jnp.dot(query_acts, act_basis, preferred_element_type=jnp.float32)
    grad_part = jnp.dot(query_grads, grad_basis, preferred_element_type=jnp.float32)
    part = jnp.concatenate([act_part, grad_part], axis=1)

    rows[0], other, sibling, grad_sibling, part = lax.optimization_barrier(
        (rows[0], other, sibling, grad_sibling, part)
    )
    columns = [activations, sibling, other, send(other, SIBLING)]
    grad_other = send(grads, OTHER_COLUMN)
    grad_columns = [grads, grad_sibling, grad_other, send(grad_other, SIBLING)]

    def multiply(i):
        if i < len(CHUNKS):
            partial, exponent = products(slot, rows[i], columns)
        else:
            partial, exponent = products(slot, rows[i], grad_columns, turned=True)
            partial = partial[:, :, :half]
        return {"partial": partial, "exponent": exponent, "stays": y_lo == y_hi}

    rotate = [
        functools.partial(halve, bit=y_hi, to=OTHER_COLUMN),
        functools.partial(halve, bit=x // 2, to=X_FAR),
        functools.partial(halve, bit=x % 2, to=X_FLIP),
        functools.partial(double, bit=x % 2, to=X_FLIP),
        functools.partial(double, bit=x // 2, to=X_FAR),
        functools.partial(double, bit=y_hi, to=OTHER_COLUMN),
    ]
    steps = (far, along, near, cross)
    parts, done = [None] * len(rows), [None] * len(rows)
    for stage in range(len(rows) + len(steps)):
        for i in reversed(range(len(rows))):
            step = stage - i - 1
            if 0 <= step < len(steps):
                parts[i] = steps[step](parts[i])
        if stage < len(rotate):
            part = rotate[stage](part)
        if stage < len(rows):
            parts[stage] = multiply(stage)
        parts, part = lax.optimization_barrier((parts, part))
        i = stage - len(steps)
        if i >= 0:
            done[i] = result(parts[i]) * up
            parts[i] = None
    act_cov = jnp.concatenate(done[:-1], axis=0)
    split = act_part.shape[1]
    return (act_cov, done[-1], part[:, :split], part[:, split:])


def solution(mesh):
    return jax.shard_map(
        on_device,
        mesh=mesh,
        in_specs=(
            P("dp", "block"),
            P("dp", "block"),
            P("block", "dp"),
            P("block", "dp"),
            P(None, "block"),
            P(None, "block"),
        ),
        out_specs=(P("dp", "block"), P("dp", "block"), P(None, "dp"), P(None, "dp")),
        check_vma=False,
    )
```

time: 664 us -> 254 us (0.38)
  waiting for transfers between devices: 521 us -> 87.2 us
  blocking collectives: 82.9 us -> 0 us
  other arithmetic: 3.39 us -> 48.8 us
  Pallas kernels: 0 us -> 36.6 us
  starting transfers between devices: 2.75 us -> 35.6 us
  matrix products: 31.4 us -> 2.98 us
  local copies, waits for them, and re-layouts: 5.91 us -> 22.3 us
    reduce_scatter x1 -> x0, waiting for transfers between devices: 214 us -> none  [on_device(): lax.psum_scatter(transposed_product(picked, activations), 'dp', scatter_d...]
    all_gather x2 -> x3, waiting for transfers between devices: 213 us -> 0.01 us  [round_x(): return lax.all_gather(rows, AXES, axis_index_groups=X_RINGS)]
    psum x1 -> x0, waiting for transfers between devices: 90.4 us -> none  [on_device(): rot_act = lax.psum(act_part, 'block')]
    ppermute x0 -> x29, waiting for transfers between devices: none -> 87.1 us  [send(): return lax.ppermute(value, AXES, to)]
    unnamed x1 -> x0, blocking collectives: 82.9 us -> none
    pallas_call x0 -> x4, Pallas kernels: none -> 36.6 us  [the longest x3 35.9 us: products(): pl.pallas_call(functools.partial(product_kernel, turned), out_shape=(jax....]
    ppermute x0 -> x29, starting transfers between devices: none -> 35.5 us  [send(): return lax.ppermute(value, AXES, to)]
    dot_general x2 -> x0, matrix products: 28.9 us -> none  [transposed_product(): lax.dot_general(left, right, (((0,), (0,)), ((), ())), preferred_element_...]
  transfers between devices with their start and end apart: 6 -> 32, of which waited for: 5 -> 15; matrix products, arithmetic and copies ran while one was open for 18% -> 23% of each run, Pallas kernels for 0% -> 14%
where the time goes in v2:
time: 254 us; the launch traced here: 250 us
  waiting for transfers between devices  87.2 us (34%)
  other arithmetic  48.8 us (19%)
  Pallas kernels  36.6 us (14%)
  starting transfers between devices  35.6 us (14%)
  local copies, waits for them, and re-layouts  22.3 us (9%)
  between operations  16.7 us (7%)
  matrix products  2.98 us (1%)
    ppermute x29, waiting for transfers between devices, send(): return lax.ppermute(value, AXES, to)  87.1 us
    pallas_call x3, Pallas kernels, products(): pl.pallas_call(functools.partial(product_kernel, turned), out_shape=(jax....  35.9 us
    ppermute x29, starting transfers between devices, send(): return lax.ppermute(value, AXES, to)  35.5 us
    convert_element_type x12, other arithmetic, message(): (value * jnp.exp2(-exponent)).astype(HALF)  12.8 us
    unnamed x48, local copies, waits for them, and re-layouts  8.02 us
    exp2 x12, other arithmetic, read(): return (got[..., :n, :].astype(jnp.float32) * jnp.exp2(exponent), exponent)  6.19 us
    add x3, other arithmetic, near(): total = p['partial'][:, 0] + second + third  5.68 us
    concatenate x9, other arithmetic, message(): jnp.concatenate([(value * jnp.exp2(-exponent)).astype(HALF), jnp.broadcas...  5.67 us
  transfers between devices with their start and end apart: 32, of which 15 were waited for; matrix products, arithmetic and copies ran while one was open for 23% of the time, Pallas kernels for 14%

profile of v2, /device:TPU:16, one launch (start us, length us, event | category | flops | bytes accessed | tf_op | source)
XLA Modules:
  0.0 250.2 jit_solution(9417161962353691847)
XLA Ops:
  14.0 2.3 pad_maximum_fusion.3
  22.2 37.9 %collective-permute-done.1.oth = bf16[1024,896]{1,0:T(8,128)(2,1)S(1)} collective-permute-done((bf16[1024,896]{1,0:T(8,128)(2,1)S(1)}, bf16[1024,896]{1,0:T(8,128)(2,1)S(1)}, u32[]{:S(2)}, u32[]{:S(2)}) %collective-permute-start.1) | collective-permute-done | bytes 1835040 | tf_op jit(solution)/shard_map/ppermute | solution.py:44
  65.2 3.2 %collective-permute-start.13 = (bf16[264,1024]{1,0:T(8,128)(2,1)S(1)}, bf16[264,1024]{1,0:T(8,128)(2,1)}, u32[]{:S(2)}, u32[]{:S(2)}) collective-permute-start(bf16[264,1024]{1,0:T(8,128)(2,1)S(1)} %bitcast.194), channel_id=1, source_target_pairs={{0,1},{8,9},{32,33},{40,41},{64,65},{72,73},{96,97},{104,105},{16,... | collective-permute-start | bytes 1622024 | tf_op jit(solution)/shard_map/ppermute | solution.py:44
  69.4 13.1 %collective-permute-done.5 = f32[256,580]{0,1:T(8,128)} collective-permute-done((f32[256,580]{0,1:T(8,128)}, f32[256,580]{0,1:T(8,128)}, u32[]{:S(2)}, u32[]{:S(2)}) %collective-permute-start.5) | collective-permute-done | bytes 593952 | tf_op jit(solution)/shard_map/ppermute | solution.py:44
  82.6 2.2 dynamic-slice_add_fusion
  86.3 14.6 %shard_map.94 = (f32[2,4,224,896]{3,2,1,0:T(8,128)}, f32[8,128]{1,0:T(8,128)S(1)}) custom-call(s32[4]{0:T(128)S(1)} %pad_add_fusion.slot, bf16[4,2,224,1024]{3,2,1,0:T(8,128)(2,1)} %bitcast.212, bf16[1024,896]{1,0:T(8,128)(2,1)S(1)} %copy-done.4, bf16[1024,896]{1,0:T(8,128)(2,1)S(1)} %copy-done.8, bf16[1024,896]{1,0:T(8,128)(2,1)} %copy-done.16, ...), custom_call_target="tpu_custom_call" | custom-call | flops 3288334336 | bytes 3670016 | tf_op jit(solution)/shard_map/pallas_call | solution.py:110
  102.2 2.2 fusion.16
  105.5 4.0 %collective-permute-start.7 = (f16[2,232,896]{2,1,0:T(8,128)(2,1)}, f16[2,232,896]{2,1,0:T(8,128)(2,1)}, u32[]{:S(2)}, u32[]{:S(2)}) collective-permute-start(f16[2,232,896]{2,1,0:T(8,128)(2,1)} %concatenate.71), channel_id=1, source_target_pairs={{0,96},{8,40},{32,0},{40,72},{64,32},{72,104},{96,64},{104,8},{16,... | collective-permute-start | bytes 2494472 | tf_op jit(solution)/shard_map/ppermute | solution.py:44
  111.5 3.3 %collective-permute-start.8 = (f32[128,580]{0,1:T(8,128)S(1)}, f32[128,580]{0,1:T(8,128)S(1)}, u32[]{:S(2)}, u32[]{:S(2)}) collective-permute-start(f32[128,580]{0,1:T(8,128)S(1)} %constant_dynamic-slice_fusion.1), channel_id=1, source_target_pairs={{0,4},{8,12},{32,36},{40,44},{64,68},{72,76},{96,100},{104,108},{1... | collective-permute-start | bytes 890888 | tf_op jit(solution)/shard_map/ppermute | solution.py:44
  116.4 14.9 %shard_map.95 = (f32[2,4,224,896]{3,2,1,0:T(8,128)}, f32[8,128]{1,0:T(8,128)S(1)}) custom-call(s32[4]{0:T(128)S(1)} %pad_add_fusion.slot, bf16[4,2,224,1024]{3,2,1,0:T(8,128)(2,1)} %bitcast.211, bf16[1024,896]{1,0:T(8,128)(2,1)S(1)} %copy-done.4, bf16[1024,896]{1,0:T(8,128)(2,1)S(1)} %copy-done.9, bf16[1024,896]{1,0:T(8,128)(2,1)} %copy-done.16, ...), custom_call_target="tpu_custom_call" | custom-call | flops 3288334336 | bytes 3670016 | tf_op jit(solution)/shard_map/pallas_call | solution.py:110
  132.6 2.2 fusion.18
  135.9 3.1 %collective-permute-start.11 = (f16[2,232,896]{2,1,0:T(8,128)(2,1)}, f16[2,232,896]{2,1,0:T(8,128)(2,1)}, u32[]{:S(2)}, u32[]{:S(2)}) collective-permute-start(f16[2,232,896]{2,1,0:T(8,128)(2,1)} %concatenate.74), channel_id=1, source_target_pairs={{0,96},{8,40},{32,0},{40,72},{64,32},{72,104},{96,64},{104,8},{16,... | collective-permute-start | bytes 2494472 | tf_op jit(solution)/shard_map/ppermute | solution.py:44
  145.6 6.4 %shard_map.96 = (f32[2,4,144,264]{3,2,1,0:T(8,128)S(1)}, f32[8,128]{1,0:T(8,128)S(1)}) custom-call(s32[4]{0:T(128)S(1)} %pad_add_fusion.slot, bf16[4,2,144,1024]{3,2,1,0:T(8,128)(2,1)} %bitcast.196, bf16[264,1024]{1,0:T(8,128)(2,1)S(1)} %bitcast.195, bf16[264,1024]{1,0:T(8,128)(2,1)S(1)} %copy-done.6, bf16[264,1024]{1,0:T(8,128)(2,1)} %collective-permute-done.13.oth, ...), custom_call_target="tpu_custom_call" | custom-call | flops 622854144 | bytes 2359296 | tf_op jit(solution)/shard_map/pallas_call | solution.py:110
  158.2 8.9 %collective-permute-done.9 = f16[2,232,896]{2,1,0:T(8,128)(2,1)} collective-permute-done((f16[2,232,896]{2,1,0:T(8,128)(2,1)}, f16[2,232,896]{2,1,0:T(8,128)(2,1)}, u32[]{:S(2)}, u32[]{:S(2)}) %collective-permute-start.9) | collective-permute-done | bytes 831520 | tf_op jit(solution)/shard_map/ppermute | solution.py:44
  171.9 2.2 fusion.4
  179.1 3.5 %collective-permute-start.19 = (f16[2,140,264]{2,1,0:T(8,128)(2,1)S(1)}, f16[2,140,264]{2,1,0:T(8,128)(2,1)S(1)}, u32[]{:S(2)}, u32[]{:S(2)}) collective-permute-start(f16[2,140,264]{2,1,0:T(8,128)(2,1)S(1)} %concatenate.78), channel_id=1, source_target_pairs={{0,96},{8,40},{32,0},{40,72},{64,32},{72,104},{96,64},{104,8},{16,... | collective-permute-start | bytes 443528 | tf_op jit(solution)/shard_map/ppermute | solution.py:44
  187.1 3.5 %collective-permute-done.18 = f16[2,140,264]{2,1,0:T(8,128)(2,1)S(1)} collective-permute-done((f16[2,140,264]{2,1,0:T(8,128)(2,1)S(1)}, f16[2,140,264]{2,1,0:T(8,128)(2,1)S(1)}, u32[]{:S(2)}, u32[]{:S(2)}) %collective-permute-start.18) | collective-permute-done | bytes 147872 | tf_op jit(solution)/shard_map/ppermute | solution.py:44
  193.5 2.2 fusion.12
  200.1 2.3 collective-permute-start.21
  205.5 6.3 %collective-permute-done.23 = f16[2,140,264]{2,1,0:T(8,128)(2,1)} collective-permute-done((f16[2,140,264]{2,1,0:T(8,128)(2,1)}, f16[2,140,264]{2,1,0:T(8,128)(2,1)}, u32[]{:S(2)}, u32[]{:S(2)}) %collective-permute-start.23) | collective-permute-done | bytes 147872 | tf_op jit(solution)/shard_map/ppermute | solution.py:44
  214.0 3.7 %collective-permute-start.26 = (f16[140,264]{1,0:T(8,128)(2,1)S(1)}, f16[140,264]{1,0:T(8,128)(2,1)S(1)}, u32[]{:S(2)}, u32[]{:S(2)}) collective-permute-start(f16[140,264]{1,0:T(8,128)(2,1)S(1)} %pad_maximum_fusion.11), channel_id=1, source_target_pairs={{0,16},{8,24},{32,48},{40,56},{64,80},{72,88},{96,112},{104,120},{... | collective-permute-start | bytes 221768 | tf_op jit(solution)/shard_map/ppermute | solution.py:44
  219.8 2.3 collective-permute-start.25
  227.2 7.2 %collective-permute-done.25 = f16[232,896]{1,0:T(8,128)(2,1)S(1)} collective-permute-done((f16[232,896]{1,0:T(8,128)(2,1)S(1)}, f16[232,896]{1,0:T(8,128)(2,1)S(1)}, u32[]{:S(2)}, u32[]{:S(2)}) %collective-permute-start.25) | collective-permute-done | bytes 415776 | tf_op jit(solution)/shard_map/ppermute | solution.py:44
  234.5 2.7 %collective-permute-start.28 = (f16[140,264]{1,0:T(8,128)(2,1)S(1)}, f16[140,264]{1,0:T(8,128)(2,1)S(1)}, u32[]{:S(2)}, u32[]{:S(2)}) collective-permute-start(f16[140,264]{1,0:T(8,128)(2,1)S(1)} %pad_maximum_fusion.12), channel_id=1, source_target_pairs={{16,1},{24,9},{48,33},{56,41},{80,65},{88,73},{112,97},{120,105},{... | collective-permute-start | bytes 221768 | tf_op jit(solution)/shard_map/ppermute | solution.py:44
  (187 shorter events, 79.0 us)
Async XLA Ops:
  7.2 55.3 %all-gather.7.cloned.1.call-start = ((), (), s32[]{:S(2)}) async-start(), calls=%async_computation | async-start | bytes 4587520 | tf_op jit(solution)/shard_map/all_gather | solution.py:207
  14.0 100.9 %all-gather.9.cloned.1.call-start = ((), (), s32[]{:S(2)}) async-start(), calls=%async_computation.1 | async-start | bytes 4587520 | tf_op jit(solution)/shard_map/all_gather | solution.py:207
  16.3 129.3 %all-gather.11.cloned.1.call-start = ((), (), s32[]{:S(2)}) async-start(), calls=%async_computation.2 | async-start | bytes 2949120 | tf_op jit(solution)/shard_map/all_gather | solution.py:207
  16.4 43.6 %collective-permute-start.1 = (bf16[1024,896]{1,0:T(8,128)(2,1)S(1)}, bf16[1024,896]{1,0:T(8,128)(2,1)S(1)}, u32[]{:S(2)}, u32[]{:S(2)}) collective-permute-start(bf16[1024,896]{1,0:T(8,128)(2,1)S(1)} %copy-done.4), channel_id=1, source_target_pairs={{0,1},{8,9},{32,33},{40,41},{64,65},{72,73},{96,97},{104,105},{16,... | collective-permute-start | bytes 5505032 | tf_op jit(solution)/shard_map/ppermute | solution.py:44
  16.7 44.5 %collective-permute-start.2 = (bf16[1024,896]{1,0:T(8,128)(2,1)S(1)}, bf16[1024,896]{1,0:T(8,128)(2,1)S(1)}, u32[]{:S(2)}, u32[]{:S(2)}) collective-permute-start(bf16[1024,896]{1,0:T(8,128)(2,1)S(1)} %copy-done.4), channel_id=1, source_target_pairs={{0,8},{8,0},{32,40},{40,32},{64,72},{72,64},{96,104},{104,96},{16,... | collective-permute-start | bytes 5505032 | tf_op jit(solution)/shard_map/ppermute | solution.py:44
  62.5 22.3 %collective-permute-start.4 = (bf16[1024,896]{1,0:T(8,128)(2,1)}, bf16[1024,896]{1,0:T(8,128)(2,1)}, u32[]{:S(2)}, u32[]{:S(2)}) collective-permute-start(bf16[1024,896]{1,0:T(8,128)(2,1)} %copy-done.16), channel_id=1, source_target_pairs={{0,8},{8,0},{32,40},{40,32},{64,72},{72,64},{96,104},{104,96},{16,... | collective-permute-start | bytes 5505032 | tf_op jit(solution)/shard_map/ppermute | solution.py:44
  64.5 18.1 %collective-permute-start.5 = (f32[256,580]{0,1:T(8,128)}, f32[256,580]{0,1:T(8,128)}, u32[]{:S(2)}, u32[]{:S(2)}) collective-permute-start(f32[256,580]{0,1:T(8,128)} %constant_dynamic-slice_fusion.2), channel_id=1, source_target_pairs={{0,1},{8,9},{32,33},{40,41},{64,65},{72,73},{96,97},{104,105},{16,... | collective-permute-start | bytes 1781768 | tf_op jit(solution)/shard_map/ppermute | solution.py:44
  65.2 45.3 %collective-permute-start.13 = (bf16[264,1024]{1,0:T(8,128)(2,1)S(1)}, bf16[264,1024]{1,0:T(8,128)(2,1)}, u32[]{:S(2)}, u32[]{:S(2)}) collective-permute-start(bf16[264,1024]{1,0:T(8,128)(2,1)S(1)} %bitcast.194), channel_id=1, source_target_pairs={{0,1},{8,9},{32,33},{40,41},{64,65},{72,73},{96,97},{104,105},{16,... | collective-permute-start | bytes 1622024 | tf_op jit(solution)/shard_map/ppermute | solution.py:44
  105.5 27.0 %collective-permute-start.7 = (f16[2,232,896]{2,1,0:T(8,128)(2,1)}, f16[2,232,896]{2,1,0:T(8,128)(2,1)}, u32[]{:S(2)}, u32[]{:S(2)}) collective-permute-start(f16[2,232,896]{2,1,0:T(8,128)(2,1)} %concatenate.71), channel_id=1, source_target_pairs={{0,96},{8,40},{32,0},{40,72},{64,32},{72,104},{96,64},{104,8},{16,... | collective-permute-start | bytes 2494472 | tf_op jit(solution)/shard_map/ppermute | solution.py:44
  110.5 22.0 %collective-permute-start.6 = (f16[2,232,896]{2,1,0:T(8,128)(2,1)}, f16[2,232,896]{2,1,0:T(8,128)(2,1)}, u32[]{:S(2)}, u32[]{:S(2)}) collective-permute-start(f16[2,232,896]{2,1,0:T(8,128)(2,1)} %concatenate.70), channel_id=1, source_target_pairs={{0,32},{8,104},{32,64},{40,8},{64,96},{72,40},{96,0},{104,72},{16,... | collective-permute-start | bytes 2494472 | tf_op jit(solution)/shard_map/ppermute | solution.py:44
  110.5 35.1 %collective-permute-start.14 = (bf16[264,1024]{1,0:T(8,128)(2,1)}, bf16[264,1024]{1,0:T(8,128)(2,1)}, u32[]{:S(2)}, u32[]{:S(2)}) collective-permute-start(bf16[264,1024]{1,0:T(8,128)(2,1)} %collective-permute-done.13.oth), channel_id=1, source_target_pairs={{0,8},{8,0},{32,40},{40,32},{64,72},{72,64},{96,104},{104,96},{16,... | collective-permute-start | bytes 1622024 | tf_op jit(solution)/shard_map/ppermute | solution.py:44
  111.5 20.9 %collective-permute-start.8 = (f32[128,580]{0,1:T(8,128)S(1)}, f32[128,580]{0,1:T(8,128)S(1)}, u32[]{:S(2)}, u32[]{:S(2)}) collective-permute-start(f32[128,580]{0,1:T(8,128)S(1)} %constant_dynamic-slice_fusion.1), channel_id=1, source_target_pairs={{0,4},{8,12},{32,36},{40,44},{64,68},{72,76},{96,100},{104,108},{1... | collective-permute-start | bytes 890888 | tf_op jit(solution)/shard_map/ppermute | solution.py:44
  135.9 22.1 %collective-permute-start.11 = (f16[2,232,896]{2,1,0:T(8,128)(2,1)}, f16[2,232,896]{2,1,0:T(8,128)(2,1)}, u32[]{:S(2)}, u32[]{:S(2)}) collective-permute-start(f16[2,232,896]{2,1,0:T(8,128)(2,1)} %concatenate.74), channel_id=1, source_target_pairs={{0,96},{8,40},{32,0},{40,72},{64,32},{72,104},{96,64},{104,8},{16,... | collective-permute-start | bytes 2494472 | tf_op jit(solution)/shard_map/ppermute | solution.py:44
  140.1 18.2 %collective-permute-start.10 = (f16[2,232,896]{2,1,0:T(8,128)(2,1)}, f16[2,232,896]{2,1,0:T(8,128)(2,1)}, u32[]{:S(2)}, u32[]{:S(2)}) collective-permute-start(f16[2,232,896]{2,1,0:T(8,128)(2,1)} %concatenate.73), channel_id=1, source_target_pairs={{0,32},{8,104},{32,64},{40,8},{64,96},{72,40},{96,0},{104,72},{16,... | collective-permute-start | bytes 2494472 | tf_op jit(solution)/shard_map/ppermute | solution.py:44
  144.0 23.2 %collective-permute-start.9 = (f16[2,232,896]{2,1,0:T(8,128)(2,1)}, f16[2,232,896]{2,1,0:T(8,128)(2,1)}, u32[]{:S(2)}, u32[]{:S(2)}) collective-permute-start(f16[2,232,896]{2,1,0:T(8,128)(2,1)} %pad_maximum_fusion.4), channel_id=1, source_target_pairs={{0,32},{8,104},{32,64},{40,8},{64,96},{72,40},{96,0},{104,72},{16,... | collective-permute-start | bytes 2494472 | tf_op jit(solution)/shard_map/ppermute | solution.py:44
  144.8 9.9 %collective-permute-start.15 = (f32[64,580]{0,1:T(8,128)}, f32[64,580]{0,1:T(8,128)}, u32[]{:S(2)}, u32[]{:S(2)}) collective-permute-start(f32[64,580]{0,1:T(8,128)} %constant_dynamic-slice_fusion), channel_id=1, source_target_pairs={{0,2},{8,10},{32,34},{40,42},{64,66},{72,74},{96,98},{104,106},{16... | collective-permute-start | bytes 445448 | tf_op jit(solution)/shard_map/ppermute | solution.py:44
  171.1 19.5 %collective-permute-start.17 = (f16[2,232,896]{2,1,0:T(8,128)(2,1)}, f16[2,232,896]{2,1,0:T(8,128)(2,1)}, u32[]{:S(2)}, u32[]{:S(2)}) collective-permute-start(f16[2,232,896]{2,1,0:T(8,128)(2,1)} %pad_maximum_fusion.5), channel_id=1, source_target_pairs={{0,32},{8,104},{32,64},{40,8},{64,96},{72,40},{96,0},{104,72},{16,... | collective-permute-start | bytes 2494472 | tf_op jit(solution)/shard_map/ppermute | solution.py:44
  175.2 15.4 %collective-permute-start.16 = (f16[232,896]{1,0:T(8,128)(2,1)}, f16[232,896]{1,0:T(8,128)(2,1)}, u32[]{:S(2)}, u32[]{:S(2)}) collective-permute-start(f16[232,896]{1,0:T(8,128)(2,1)} %pad_maximum_fusion.6), channel_id=1, source_target_pairs={{0,16},{8,24},{32,48},{40,56},{64,80},{72,88},{96,112},{104,120},{... | collective-permute-start | bytes 1247240 | tf_op jit(solution)/shard_map/ppermute | solution.py:44
  190.6 13.8 %collective-permute-start.24 = (f32[128,580]{0,1:T(8,128)S(1)}, f32[128,580]{0,1:T(8,128)}, u32[]{:S(2)}, u32[]{:S(2)}) collective-permute-start(f32[128,580]{0,1:T(8,128)S(1)} %maximum_select_fusion.2), channel_id=1, source_target_pairs={{0,4},{8,12},{32,36},{40,44},{64,68},{72,76},{96,100},{104,108},{1... | collective-permute-start | bytes 890888 | tf_op jit(solution)/shard_map/ppermute | solution.py:44
  196.6 15.2 %collective-permute-start.22 = (f16[232,896]{1,0:T(8,128)(2,1)}, f16[232,896]{1,0:T(8,128)(2,1)}, u32[]{:S(2)}, u32[]{:S(2)}) collective-permute-start(f16[232,896]{1,0:T(8,128)(2,1)} %pad_maximum_fusion.8), channel_id=1, source_target_pairs={{0,16},{8,24},{32,48},{40,56},{64,80},{72,88},{96,112},{104,120},{... | collective-permute-start | bytes 1247240 | tf_op jit(solution)/shard_map/ppermute | solution.py:44
  200.1 11.7 %collective-permute-start.21 = (f16[232,896]{1,0:T(8,128)(2,1)}, f16[232,896]{1,0:T(8,128)(2,1)}, u32[]{:S(2)}, u32[]{:S(2)}) collective-permute-start(f16[232,896]{1,0:T(8,128)(2,1)} %pad_maximum_fusion.7), channel_id=1, source_target_pairs={{16,1},{24,9},{48,33},{56,41},{80,65},{88,73},{112,97},{120,105},{... | collective-permute-start | bytes 1247240 | tf_op jit(solution)/shard_map/ppermute | solution.py:44
  211.8 14.9 %collective-permute-start.27 = (f32[256,580]{0,1:T(8,128)S(1)}, f32[256,580]{0,1:T(8,128)S(1)}, u32[]{:S(2)}, u32[]{:S(2)}) collective-permute-start(f32[256,580]{0,1:T(8,128)S(1)} %maximum_select_fusion.1), channel_id=1, source_target_pairs={{0,1},{8,9},{32,33},{40,41},{64,65},{72,73},{96,97},{104,105},{16,... | collective-permute-start | bytes 1781768 | tf_op jit(solution)/shard_map/ppermute | solution.py:44
  214.0 13.2 %collective-permute-start.26 = (f16[140,264]{1,0:T(8,128)(2,1)S(1)}, f16[140,264]{1,0:T(8,128)(2,1)S(1)}, u32[]{:S(2)}, u32[]{:S(2)}) collective-permute-start(f16[140,264]{1,0:T(8,128)(2,1)S(1)} %pad_maximum_fusion.11), channel_id=1, source_target_pairs={{0,16},{8,24},{32,48},{40,56},{64,80},{72,88},{96,112},{104,120},{... | collective-permute-start | bytes 221768 | tf_op jit(solution)/shard_map/ppermute | solution.py:44
  219.8 14.6 %collective-permute-start.25 = (f16[232,896]{1,0:T(8,128)(2,1)S(1)}, f16[232,896]{1,0:T(8,128)(2,1)S(1)}, u32[]{:S(2)}, u32[]{:S(2)}) collective-permute-start(f16[232,896]{1,0:T(8,128)(2,1)S(1)} %pad_maximum_fusion.9), channel_id=1, source_target_pairs={{16,1},{24,9},{48,33},{56,41},{80,65},{88,73},{112,97},{120,105},{... | collective-permute-start | bytes 1247240 | tf_op jit(solution)/shard_map/ppermute | solution.py:44
  (25 other events, 141.2 us)
Sparse Core Ops, SparseCore 0:
  14.0 46.0 all-gather.6
  62.4 44.1 all-gather.8
  108.2 34.0 all-gather.10

commit v3 on v1

v3 whole, which is shorter than its diff:
```python
import functools
import itertools

import jax
import jax.numpy as jnp
from jax import lax
from jax.experimental import pallas as pl
from jax.experimental.pallas import tpu as pltpu
from jax.sharding import PartitionSpec as P

AXES = ("dp", "block")
HALF = jnp.float16


def place(x, y, z, core):
    return ((z * 2 + y % 2) * 2 + core) * 8 + x * 2 + y // 2


def pairs(move):
    out = []
    for at in itertools.product(range(4), range(4), range(4), range(2)):
        x, y, z, core = move(*at)
        out.append((place(*at), place(x % 4, y % 4, z % 4, core % 2)))
    return out


SIBLING = pairs(lambda x, y, z, c: (x, y, z, c + 1))
OTHER_COLUMN = pairs(lambda x, y, z, c: (x, y + 2, z, c))
X_DOWN = pairs(lambda x, y, z, c: (x - 1, y, z, c))
X_UP = pairs(lambda x, y, z, c: (x + 1, y, z, c))
X_FAR = pairs(lambda x, y, z, c: (x + 2, y, z, c))
X_FLIP = pairs(lambda x, y, z, c: (x ^ 1, y, z, c))
Z_ALONG = pairs(lambda x, y, z, c: (x, y, z + 1 - 2 * c, c))
Z_AGAINST = pairs(lambda x, y, z, c: (x, y, z - 1 + 2 * c, c))
X_RINGS = [
    [place(x, y, z, c) for x in range(4)]
    for y, z, c in itertools.product(range(4), range(4), range(2))
]
FIRST = 272
Y_PARTNER = pairs(lambda x, y, z, c: (x, y ^ 1, z, c))
Y_ROUND = pairs(lambda x, y, z, c: (x, (2, 0, 3, 1)[y], z, c))
Y_MIDDLE = [p for p in pairs(lambda x, y, z, c: (x, (0, 2, 1, 3)[y], z, c)) if p[0] != p[1]]


def send(value, to):
    return lax.ppermute(value, AXES, to)


def turn_kernel(core, own, mine, theirs, turned):
    half = mine.shape[0]
    turned[...] = own[...].T
    mine[...] = turned[pl.ds(pl.multiple_of(core[0] * half, 16), half), :]
    theirs[...] = turned[pl.ds(pl.multiple_of((1 - core[0]) * half, 16), half), :]


def turn(own, core):
    tokens, width = own.shape
    vmem = pl.BlockSpec(memory_space=pltpu.VMEM)
    half = jax.ShapeDtypeStruct((width // 2, tokens), own.dtype)
    return pl.pallas_call(
        turn_kernel,
        out_shape=(half, half),
        in_specs=[pl.BlockSpec(memory_space=pltpu.SMEM), vmem],
        out_specs=(vmem, vmem),
        scratch_shapes=[pltpu.VMEM((width, tokens), own.dtype)],
        compiler_params=pltpu.CompilerParams(vmem_limit_bytes=24 << 20),
    )(core.reshape(1).astype(jnp.int32), own)


def product_kernel(turned, slot, rows, own, sib, oth, oth_sib, *refs):
    *outs, held, columns, sem = refs
    tokens = held.shape[2] // 2
    block, at = pl.program_id(0), pl.program_id(1)

    def row_copy(d, half, i):
        place = held.at[i, :, pl.ds(half * tokens, tokens)]
        return pltpu.make_async_copy(rows.at[d, half], place, sem.at[half, i])

    def column_copies(i):
        copies = []
        for half, ref in enumerate(((own, sib), (oth, oth_sib))[i]):
            part = pl.ds(half * tokens, tokens)
            place = columns.at[i, :, part] if turned else columns.at[i, part, :]
            copies.append(pltpu.make_async_copy(ref, place, sem.at[half, 4 + i]))
        return copies

    @pl.when((block == 0) & (at == 0))
    def _():
        for copy in column_copies(0):
            copy.start()
        for d in range(4):
            for half in (0, 1):
                row_copy(d, half, slot[d]).start()
        for copy in column_copies(1):
            copy.start()

    for i in (0, 1):

        @pl.when((block == i) & (at == 0))
        def _(i=i):
            for copy in column_copies(i):
                copy.wait()

    for i in range(4):

        @pl.when((block == 0) & (at == i))
        def _(i=i):
            for half in (0, 1):
                row_copy(0, half, i).wait()

    for i, out in enumerate(outs):

        @pl.when(at == i)
        def _(i=i, out=out):
            out[0] = lax.dot_general(
                held[i],
                columns[block],
                (((1,), (1 if turned else 0,)), ((), ())),
                preferred_element_type=jnp.float32,
            )


def products(slot, rows, columns, turned=False):
    _, _, n, tokens = rows.shape
    width = columns[0].shape[0 if turned else 1]
    anywhere = pl.BlockSpec(memory_space=pl.ANY)
    smem = pl.BlockSpec(memory_space=pltpu.SMEM)
    held_columns = (2, width, 2 * tokens) if turned else (2, 2 * tokens, width)
    return pl.pallas_call(
        functools.partial(product_kernel, turned),
        out_shape=[jax.ShapeDtypeStruct((2, n, width), jnp.float32)] * 4,
        grid=(2, 4),
        in_specs=[smem] + [anywhere] * 5,
        out_specs=[pl.BlockSpec((1, n, width), lambda block, at: (block, 0, 0))] * 4,
        scratch_shapes=[
            pltpu.VMEM((4, n, 2 * tokens), columns[0].dtype),
            pltpu.VMEM(held_columns, columns[0].dtype),
            pltpu.SemaphoreType.DMA((2, 6)),
        ],
        compiler_params=pltpu.CompilerParams(vmem_limit_bytes=60 << 20),
        cost_estimate=pl.CostEstimate(
            flops=16 * n * tokens * width, bytes_accessed=16 * n * tokens, transcendentals=0
        ),
    )(slot, rows, *columns)


def largest_over(largest, *moves):
    for move in moves:
        largest = jnp.maximum(largest, send(largest, pairs(move)))
    return largest


def scales(largest, tokens_total):
    largest = jnp.maximum(largest, 1e-18)
    most = largest * largest * tokens_total
    return 32768.0 / most, most / (32768.0 * tokens_total)


def far(p):
    _, _, second, third = p["partial"]
    a = send((second * p["down"]).astype(HALF), Z_ALONG)
    return {**p, "a": a, "c": send((third * p["down"]).astype(HALF), Z_AGAINST)}


def along(p):
    b = p["partial"][1] * p["down"] + p["a"].astype(jnp.float32)
    return {**p, "a": None, "b": send(b.astype(HALF), Z_ALONG)}


def summed(p):
    b, c = p["b"].astype(jnp.float32), p["c"].astype(jnp.float32)
    return p["partial"][0] * p["down"] + b + c


def near(p):
    total = summed(p)
    value = jnp.where(p["stays"], total[1], total[0])
    return {"total": total, "stays": p["stays"], "n": send(value.astype(HALF), Y_PARTNER)}


def cross(p):
    value = p["total"][1] + p["n"].astype(jnp.float32)
    return {**p, "m": send(value.astype(HALF), Y_MIDDLE)}


def result(p):
    own = p["total"][0] + p["n"].astype(jnp.float32)
    return jnp.where(p["stays"], own, p["m"].astype(jnp.float32))


def direct(p):
    total = summed(p)
    value = jnp.where(p["stays"], total[1], total[0])
    n, m = send(value.astype(HALF), Y_ROUND), send(total[1].astype(HALF), Y_MIDDLE)
    return {"total": total[0], "stays": p["stays"], "n": n, "m": m}


def direct_result(p):
    other = jnp.where(p["stays"], p["total"], p["m"].astype(jnp.float32))
    return p["n"].astype(jnp.float32) + other


def turned_product(basis, queries):
    return lax.dot_general(
        basis, queries, (((0,), (1,)), ((), ())), preferred_element_type=jnp.float32
    )


def give(value, bit, to):
    rows = value.shape[0] // 2
    return (value, send(lax.dynamic_slice_in_dim(value, (1 - bit) * rows, rows, 0), to))


def add(value, got, bit):
    rows = got.shape[0]
    return lax.dynamic_slice_in_dim(value, bit * rows, rows, 0) + got


def join(value, to, bit, axis):
    got = send(value, to)
    return jnp.where(
        bit == 0,
        jnp.concatenate([value, got], axis=axis),
        jnp.concatenate([got, value], axis=axis),
    )


def round_x(rows):
    return lax.all_gather(rows, AXES, axis_index_groups=X_RINGS)


def on_device(activations, out_grads, act_basis, grad_basis, query_acts, query_grads):
    dp, block = lax.axis_index("dp"), lax.axis_index("block")
    x, y_hi, z, y_lo, core = block // 2, block % 2, dp // 4, dp // 2 % 2, dp % 2
    tokens_total = activations.shape[0] * lax.axis_size("dp")
    along_z = 1 - 2 * core
    slot = jnp.stack([((d - z) * along_z) % 4 for d in range(4)]).astype(jnp.int32)
    half = out_grads.shape[1] // 2

    mine, theirs = turn(activations, core)
    other = send(activations, OTHER_COLUMN)
    got = send(theirs, SIBLING)
    rows_1 = round_x(jnp.stack([mine[:FIRST], got[:FIRST]]))
    rows_2 = round_x(jnp.stack([mine[FIRST:], got[FIRST:]]))
    sibling = send(activations, SIBLING)
    grads = jnp.pad(out_grads.T, ((0, -out_grads.shape[1] % 16), (0, 0)))
    grad_mine = lax.dynamic_slice_in_dim(grads, core * half, half, 0)
    grad_theirs = lax.dynamic_slice_in_dim(grads, (1 - core) * half, half, 0)
    grad_rows = jnp.stack([grad_mine, send(grad_theirs, SIBLING)])
    grad_rows = round_x(jnp.pad(grad_rows, ((0, 0), (0, -half % 16), (0, 0))))
    grad_sibling = send(grads, SIBLING)
    part = jnp.concatenate(
        [turned_product(act_basis, query_acts), turned_product(grad_basis, query_grads)], axis=0
    )
    part = jnp.pad(part, ((0, -part.shape[0] % 64), (0, 0)))
    largest = largest_over(
        jnp.where(
            lax.broadcasted_iota(jnp.int32, (8, 128), 0) < 4,
            jnp.max(jnp.abs(activations)).astype(jnp.float32),
            jnp.max(jnp.abs(out_grads)).astype(jnp.float32),
        ),
        lambda x, y, z, c: (x, y, z, c + 1),
        lambda x, y, z, c: (x, y, z ^ 1, c),
        lambda x, y, z, c: (x, y, z + 2, c),
        lambda x, y, z, c: (x ^ 1, y, z, c),
        lambda x, y, z, c: (x + 2, y, z, c),
    )
    largest, other, sibling, grads, grad_sibling, part = lax.optimization_barrier(
        (largest, other, sibling, grads, grad_sibling, part)
    )
    largest = largest_over(
        largest, lambda x, y, z, c: (x, y ^ 1, z, c), lambda x, y, z, c: (x, y + 2, z, c)
    )
    act_down, act_up = scales(largest[0, 0], tokens_total)
    grad_down, grad_up = scales(largest[4, 0], tokens_total)
    columns = [activations, sibling, other, send(other, SIBLING)]
    columns, rows_1, grads, grad_sibling, part, act_down, act_up, grad_down, grad_up = (
        lax.optimization_barrier(
            (columns, rows_1, grads, grad_sibling, part, act_down, act_up, grad_down, grad_up)
        )
    )

    parts, done, beside = [None] * 3, [None] * 3, ()
    steps = [(far, along, near, cross)] * 2 + [(far, along, direct)]
    for stage in range(6):
        for i in reversed(range(len(parts))):
            step = stage - i - 1
            if 0 <= step < len(steps[i]):
                down = grad_down if i == 2 else act_down
                parts[i] = steps[i][step]({**parts[i], "down": down})
        if stage == 0:
            part = give(part, y_hi, OTHER_COLUMN)
            partial = products(slot, rows_1, columns)
            beside = send(grads, OTHER_COLUMN)
        elif stage == 1:
            part = give(add(*part, y_hi), x // 2, X_FAR)
            partial = products(slot, rows_2, columns)
            beside = [grads, grad_sibling, beside, send(beside, SIBLING)]
        elif stage == 2:
            part = give(add(*part, x // 2), x % 2, X_FLIP)
            partial = products(slot, grad_rows, beside, turned=True)
            beside = ()
        elif stage == 3:
            part = add(*part, x % 2)
            part = part.reshape((1, 1, 1, *part.shape))
            part = join(join(part, OTHER_COLUMN, y_hi, 0), X_FLIP, x % 2, 2)
        elif stage == 4:
            part = join(part, X_FAR, x // 2, 1)
        if stage < len(parts):
            parts[stage] = {"partial": partial, "stays": y_lo == y_hi}
        if stage < 5:
            parts, part, beside = lax.optimization_barrier((parts, part, beside))
    act_cov = jnp.concatenate([result(parts[0]), result(parts[1])], axis=0) * act_up
    grad_cov = direct_result(parts[2])[:half, : out_grads.shape[1]] * grad_up
    part = part.reshape(-1, query_acts.shape[0])
    split, end = act_basis.shape[1], act_basis.shape[1] + grad_basis.shape[1]
    return (act_cov, grad_cov, part[:split].T, part[split:end].T)


def solution(mesh):
    return jax.shard_map(
        on_device,
        mesh=mesh,
        in_specs=(
            P("dp", "block"),
            P("dp", "block"),
            P("block", "dp"),
            P("block", "dp"),
            P(None, "block"),
            P(None, "block"),
        ),
        out_specs=(P("dp", "block"), P("dp", "block"), P(None, "dp"), P(None, "dp")),
        check_vma=False,
    )
```

time: 402 us -> 229 us (0.57)
  waiting for transfers between devices: 179 us -> 74.5 us
  blocking collectives: 67.2 us -> 0 us
  matrix products: 66.5 us -> 2.09 us
  Pallas kernels: 0 us -> 39.6 us
  starting transfers between devices: 31 us -> 50.1 us
  other arithmetic: 27.7 us -> 33.1 us
    ppermute x22 -> x36, waiting for transfers between devices: 149 us -> 71 us  [send(): return lax.ppermute(value, AXES, to)]
    pmax x1 -> x0, blocking collectives: 67.2 us -> none  [covariance(): largest = lax.pmax(jnp.max(jnp.abs(own)).astype(jnp.float32), AXES)]
    dot_general x10 -> x2, matrix products: 66.5 us -> 2.09 us  [turned_product(): lax.dot_general(basis, queries, (((0,), (1,)), ((), ())), preferred_eleme...]
    pallas_call x0 -> x4, Pallas kernels: none -> 39.6 us  [the longest x3 38.9 us: products(): pl.pallas_call(functools.partial(product_kernel, turned), out_shape=[jax....]
    psum x1 -> x0, waiting for transfers between devices: 30.5 us -> none  [on_device(): lax.psum(jnp.dot(query_acts, act_basis, preferred_element_type=jnp.float3...]
    ppermute x22 -> x36, starting transfers between devices: 31 us -> 50 us  [send(): return lax.ppermute(value, AXES, to)]
    unnamed x33 -> x60, local copies, waits for them, and re-layouts: 11.5 us -> 2.84 us
    convert_element_type x8 -> x15, other arithmetic: 9.85 us -> 14.2 us  [the longest x3 5.27 us: along(): return {**p, 'a': None, 'b': send(b.astype(HALF), Z_ALONG)}]
  transfers between devices with their start and end apart: 23 -> 39, of which waited for: 14 -> 17; matrix products, arithmetic and copies ran while one was open for 19% -> 17% of each run, Pallas kernels for 0% -> 17%
where the time goes in v3:
time: 229 us; the launch traced here: 227 us
  waiting for transfers between devices  74.5 us (33%)
  starting transfers between devices  50.1 us (22%)
  Pallas kernels  39.6 us (17%)
  other arithmetic  33.1 us (14%)
  between operations  17.1 us (7%)
  local copies, waits for them, and re-layouts  10.9 us (5%)
    ppermute x36, waiting for transfers between devices, send(): return lax.ppermute(value, AXES, to)  71 us
    ppermute x36, starting transfers between devices, send(): return lax.ppermute(value, AXES, to)  50 us
    pallas_call x3, Pallas kernels, products(): pl.pallas_call(functools.partial(product_kernel, turned), out_shape=[jax....  38.9 us
    convert_element_type x3, other arithmetic, along(): return {**p, 'a': None, 'b': send(b.astype(HALF), Z_ALONG)}  5.27 us
    convert_element_type x3, other arithmetic, far(): return {**p, 'a': a, 'c': send((third * p['down']).astype(HALF), Z_AGAINST)}  4.83 us
  transfers between devices with their start and end apart: 39, of which 17 were waited for; matrix products, arithmetic and copies ran while one was open for 17% of the time, Pallas kernels for 17%

profile of v3, /device:TPU:16, one launch (start us, length us, event | category | flops | bytes accessed | tf_op | source)
XLA Modules:
  0.0 227.5 jit_solution(2692703471005601767)
XLA Ops:
  9.6 2.5 %collective-permute-done.9 = bf16[448,1024]{1,0:T(8,128)(2,1)} collective-permute-done((bf16[448,1024]{1,0:T(8,128)(2,1)S(1)}, bf16[448,1024]{1,0:T(8,128)(2,1)}, u32[]{:S(2)}, u32[]{:S(2)}) %collective-permute-start.9) | collective-permute-done | bytes 917536 | tf_op jit(solution)/shard_map/ppermute | solution.py:46
  25.1 4.0 %collective-permute-start.2 = (f32[8,128]{1,0:T(8,128)S(1)}, f32[8,128]{1,0:T(8,128)S(1)}, u32[]{:S(2)}, u32[]{:S(2)}) collective-permute-start(f32[8,128]{1,0:T(8,128)S(1)} %fusion.24), channel_id=1, source_target_pairs={{0,64},{8,72},{32,96},{40,104},{64,0},{72,8},{96,32},{104,40},{16,... | collective-permute-start | bytes 12296 | tf_op jit(solution)/shard_map/ppermute | solution.py:46
  34.7 3.0 %collective-permute-start.4 = (f32[8,128]{1,0:T(8,128)S(1)}, f32[8,128]{1,0:T(8,128)S(1)}, u32[]{:S(2)}, u32[]{:S(2)}) collective-permute-start(f32[8,128]{1,0:T(8,128)S(1)} %max.32), channel_id=1, source_target_pairs={{0,4},{8,12},{32,36},{40,44},{64,68},{72,76},{96,100},{104,108},{1... | collective-permute-start | bytes 12296 | tf_op jit(solution)/shard_map/ppermute | solution.py:46
  39.9 20.5 %collective-permute-done.5.oth = bf16[1024,896]{1,0:T(8,128)(2,1)} collective-permute-done((bf16[1024,896]{1,0:T(8,128)(2,1)S(1)}, bf16[1024,896]{1,0:T(8,128)(2,1)}, u32[]{:S(2)}, u32[]{:S(2)}) %collective-permute-start.5) | collective-permute-done | bytes 1835040 | tf_op jit(solution)/shard_map/ppermute | solution.py:46
  63.1 2.3 %collective-permute-done.10 = f32[8,128]{1,0:T(8,128)S(1)} collective-permute-done((f32[8,128]{1,0:T(8,128)S(1)}, f32[8,128]{1,0:T(8,128)S(1)}, u32[]{:S(2)}, u32[]{:S(2)}) %collective-permute-start.10) | collective-permute-done | bytes 4128 | tf_op jit(solution)/shard_map/ppermute | solution.py:46
  65.7 4.8 %collective-permute-done.11 = f32[8,128]{1,0:T(8,128)S(1)} collective-permute-done((f32[8,128]{1,0:T(8,128)S(1)}, f32[8,128]{1,0:T(8,128)S(1)}, u32[]{:S(2)}, u32[]{:S(2)}) %collective-permute-start.11) | collective-permute-done | bytes 4128 | tf_op jit(solution)/shard_map/ppermute | solution.py:46
  72.6 2.5 %constant_dynamic-slice_fusion.3 = f32[320,512]{1,0:T(8,128)} fusion(f32[640,512]{1,0:T(8,128)} %select_maximum_fusion, s32[]{:T(128)S(6)} %select_n.196), kind=kLoop, calls=%fused_computation.64 | loop fusion | bytes 1310724 | tf_op jit(solution)/shard_map/dynamic_slice | solution.py:211
  75.3 3.2 %collective-permute-start.13 = (bf16[272,1024]{1,0:T(8,128)(2,1)S(1)}, bf16[272,1024]{1,0:T(8,128)(2,1)}, u32[]{:S(2)}, u32[]{:S(2)}) collective-permute-start(bf16[272,1024]{1,0:T(8,128)(2,1)S(1)} %copy-done.7), channel_id=1, source_target_pairs={{0,1},{8,9},{32,33},{40,41},{64,65},{72,73},{96,97},{104,105},{16,... | collective-permute-start | bytes 1671176 | tf_op jit(solution)/shard_map/ppermute | solution.py:46
  81.2 16.7 %shard_map.94 = (f32[2,272,896]{2,1,0:T(8,128)}, f32[2,272,896]{2,1,0:T(8,128)}, f32[2,272,896]{2,1,0:T(8,128)}, f32[2,272,896]{2,1,0:T(8,128)}) custom-call(s32[4]{0:T(128)} %pad_add_fusion.slot, bf16[4,2,272,1024]{3,2,1,0:T(8,128)(2,1)} %bitcast.73, bf16[1024,896]{1,0:T(8,128)(2,1)} %own.3, bf16[1024,896]{1,0:T(8,128)(2,1)} %collective-permute-done.6.sib, ...), custom_call_target="tpu_custom_call" | custom-call | flops 3992977408 | bytes 4456448 | tf_op jit(solution)/shard_map/pallas_call | solution.py:129
  97.9 5.6 %collective-permute-done.13.oth = bf16[272,1024]{1,0:T(8,128)(2,1)} collective-permute-done((bf16[272,1024]{1,0:T(8,128)(2,1)S(1)}, bf16[272,1024]{1,0:T(8,128)(2,1)}, u32[]{:S(2)}, u32[]{:S(2)}) %collective-permute-start.13) | collective-permute-done | bytes 557088 | tf_op jit(solution)/shard_map/ppermute | solution.py:46
  104.4 2.8 %multiply_convert_fusion = f16[2,272,896]{2,1,0:T(8,128)(2,1)} fusion(f32[2,272,896]{2,1,0:T(8,128)} %get-tuple-element.122, f32[]{:T(128)} %bitcast.5), kind=kLoop, calls=%fused_computation.2 | loop fusion | flops 974848 | bytes 2924548 | tf_op jit(solution)/shard_map/convert_element_type | solution.py:162
  107.2 4.0 %collective-permute-start.15 = (f16[2,272,896]{2,1,0:T(8,128)(2,1)}, f16[2,272,896]{2,1,0:T(8,128)(2,1)S(1)}, u32[]{:S(2)}, u32[]{:S(2)}) collective-permute-start(f16[2,272,896]{2,1,0:T(8,128)(2,1)} %multiply_convert_fusion), channel_id=1, source_target_pairs={{0,96},{8,40},{32,0},{40,72},{64,32},{72,104},{96,64},{104,8},{16,... | collective-permute-start | bytes 2924552 | tf_op jit(solution)/shard_map/ppermute | solution.py:46
  113.7 3.3 %collective-permute-start.16 = (f32[160,512]{1,0:T(8,128)S(1)}, f32[160,512]{1,0:T(8,128)S(1)}, u32[]{:S(2)}, u32[]{:S(2)}) collective-permute-start(f32[160,512]{1,0:T(8,128)S(1)} %constant_dynamic-slice_fusion.2), channel_id=1, source_target_pairs={{0,4},{8,12},{32,36},{40,44},{64,68},{72,76},{96,100},{104,108},{1... | collective-permute-start | bytes 983048 | tf_op jit(solution)/shard_map/ppermute | solution.py:46
  117.0 13.2 %shard_map.95 = (f32[2,176,896]{2,1,0:T(8,128)}, f32[2,176,896]{2,1,0:T(8,128)}, f32[2,176,896]{2,1,0:T(8,128)}, f32[2,176,896]{2,1,0:T(8,128)}) custom-call(s32[4]{0:T(128)} %pad_add_fusion.slot, bf16[4,2,176,1024]{3,2,1,0:T(8,128)(2,1)} %bitcast.70, bf16[1024,896]{1,0:T(8,128)(2,1)} %own.3, bf16[1024,896]{1,0:T(8,128)(2,1)} %collective-permute-done.6.sib, ...), custom_call_target="tpu_custom_call" | custom-call | flops 2583691264 | bytes 2883584 | tf_op jit(solution)/shard_map/pallas_call | solution.py:129
  131.1 3.2 %add_convert_fusion = f16[2,272,896]{2,1,0:T(8,128)(2,1)} fusion(f16[2,272,896]{2,1,0:T(8,128)(2,1)} %collective-permute-done.14, f32[2,272,896]{2,1,0:T(8,128)} %get-tuple-element.134, f32[]{:T(128)} %bitcast.5), kind=kLoop, calls=%fused_computation.1 | loop fusion | flops 1949696 | bytes 3899396 | tf_op jit(solution)/shard_map/convert_element_type | solution.py:167
  141.8 3.4 %all-gather.11.cloned.1.call-done = bf16[8,144,1024]{2,1,0:T(8,128)(2,1)} async-done(((bf16[2,144,1024]{2,1,0:T(8,128)(2,1)}), bf16[8,144,1024]{2,1,0:T(8,128)(2,1)}) %all-gather.11.cloned.1.call-update) | async-done | bytes 2359312 | tf_op jit(solution)/shard_map/all_gather | solution.py:229
  145.2 9.0 %shard_map.96 = (f32[2,144,272]{2,1,0:T(8,128)}, f32[2,144,272]{2,1,0:T(8,128)}, f32[2,144,272]{2,1,0:T(8,128)}, f32[2,144,272]{2,1,0:T(8,128)}) custom-call(s32[4]{0:T(128)} %pad_add_fusion.slot, bf16[4,2,144,1024]{3,2,1,0:T(8,128)(2,1)} %bitcast.71, bf16[272,1024]{1,0:T(8,128)(2,1)} %copy-done.6, bf16[272,1024]{1,0:T(8,128)(2,1)} %copy-done.19, ...), custom_call_target="tpu_custom_call" | custom-call | flops 641728512 | bytes 2359296 | tf_op jit(solution)/shard_map/pallas_call | solution.py:129
  154.6 9.1 %collective-permute-done.19 = f16[2,176,896]{2,1,0:T(8,128)(2,1)} collective-permute-done((f16[2,176,896]{2,1,0:T(8,128)(2,1)}, f16[2,176,896]{2,1,0:T(8,128)(2,1)}, u32[]{:S(2)}, u32[]{:S(2)}) %collective-permute-start.19) | collective-permute-done | bytes 630816 | tf_op jit(solution)/shard_map/ppermute | solution.py:46
  174.7 7.1 %collective-permute-done.28 = f32[2,1,1,80,512]{4,3,2,1,0:T(8,128)S(1)} collective-permute-done((f32[2,1,1,80,512]{4,3,2,1,0:T(8,128)S(1)}, f32[2,1,1,80,512]{4,3,2,1,0:T(8,128)S(1)}, u32[]{:S(2)}, u32[]{:S(2)}) %collective-permute-start.28) | collective-permute-done | bytes 327712 | tf_op jit(solution)/shard_map/ppermute | solution.py:46
  186.3 4.1 %collective-permute-start.29 = (f16[272,896]{1,0:T(8,128)(2,1)}, f16[272,896]{1,0:T(8,128)(2,1)}, u32[]{:S(2)}, u32[]{:S(2)}) collective-permute-start(f16[272,896]{1,0:T(8,128)(2,1)} %fusion.4), channel_id=1, source_target_pairs={{16,1},{24,9},{48,33},{56,41},{80,65},{88,73},{112,97},{120,105},{... | collective-permute-start | bytes 1462280 | tf_op jit(solution)/shard_map/ppermute | solution.py:46
  193.6 7.6 %collective-permute-done.32 = f32[2,1,2,80,512]{4,3,2,1,0:T(8,128)} collective-permute-done((f32[2,1,2,80,512]{4,3,2,1,0:T(8,128)}, f32[2,1,2,80,512]{4,3,2,1,0:T(8,128)}, u32[]{:S(2)}, u32[]{:S(2)}) %collective-permute-start.32) | collective-permute-done | bytes 655392 | tf_op jit(solution)/shard_map/ppermute | solution.py:46
  206.0 3.6 %collective-permute-start.35 = (f16[144,272]{1,0:T(8,128)(2,1)S(1)}, f16[144,272]{1,0:T(8,128)(2,1)S(1)}, u32[]{:S(2)}, u32[]{:S(2)}) collective-permute-start(f16[144,272]{1,0:T(8,128)(2,1)S(1)} %get-tuple-element.202), channel_id=1, source_target_pairs={{16,1},{24,9},{48,33},{56,41},{80,65},{88,73},{112,97},{120,105},{... | collective-permute-start | bytes 235016 | tf_op jit(solution)/shard_map/ppermute | solution.py:46
  209.8 2.3 %collective-permute-start.33 = (f16[176,896]{1,0:T(8,128)(2,1)S(1)}, f16[176,896]{1,0:T(8,128)(2,1)S(1)}, u32[]{:S(2)}, u32[]{:S(2)}) collective-permute-start(f16[176,896]{1,0:T(8,128)(2,1)S(1)} %fusion.6), channel_id=1, source_target_pairs={{16,1},{24,9},{48,33},{56,41},{80,65},{88,73},{112,97},{120,105},{... | collective-permute-start | bytes 946184 | tf_op jit(solution)/shard_map/ppermute | solution.py:46
  215.7 3.8 %collective-permute-done.33 = f16[176,896]{1,0:T(8,128)(2,1)S(1)} collective-permute-done((f16[176,896]{1,0:T(8,128)(2,1)S(1)}, f16[176,896]{1,0:T(8,128)(2,1)S(1)}, u32[]{:S(2)}, u32[]{:S(2)}) %collective-permute-start.33) | collective-permute-done | bytes 315424 | tf_op jit(solution)/shard_map/ppermute | solution.py:46
  (180 shorter events, 68.3 us)
Async XLA Ops:
  7.2 65.4 %all-gather.7.cloned.1.call-start = ((), (), s32[]{:S(2)}) async-start(), calls=%async_computation | async-start | bytes 5570560 | tf_op jit(solution)/shard_map/all_gather | solution.py:229
  14.5 102.5 %all-gather.9.cloned.1.call-start = ((), (), s32[]{:S(2)}) async-start(), calls=%async_computation.1 | async-start | bytes 3604480 | tf_op jit(solution)/shard_map/all_gather | solution.py:229
  16.7 128.5 %all-gather.11.cloned.1.call-start = ((), (), s32[]{:S(2)}) async-start(), calls=%async_computation.2 | async-start | bytes 2949120 | tf_op jit(solution)/shard_map/all_gather | solution.py:229
  16.7 43.7 %collective-permute-start.5 = (bf16[1024,896]{1,0:T(8,128)(2,1)S(1)}, bf16[1024,896]{1,0:T(8,128)(2,1)}, u32[]{:S(2)}, u32[]{:S(2)}) collective-permute-start(bf16[1024,896]{1,0:T(8,128)(2,1)S(1)} %copy-done.3), channel_id=1, source_target_pairs={{0,1},{8,9},{32,33},{40,41},{64,65},{72,73},{96,97},{104,105},{16,... | collective-permute-start | bytes 5505032 | tf_op jit(solution)/shard_map/ppermute | solution.py:46
  17.1 43.4 %collective-permute-start.6 = (bf16[1024,896]{1,0:T(8,128)(2,1)S(1)}, bf16[1024,896]{1,0:T(8,128)(2,1)}, u32[]{:S(2)}, u32[]{:S(2)}) collective-permute-start(bf16[1024,896]{1,0:T(8,128)(2,1)S(1)} %copy-done.3), channel_id=1, source_target_pairs={{0,8},{8,0},{32,40},{40,32},{64,72},{72,64},{96,104},{104,96},{16,... | collective-permute-start | bytes 5505032 | tf_op jit(solution)/shard_map/ppermute | solution.py:46
  23.5 16.5 %collective-permute-start.7 = (bf16[272,1024]{1,0:T(8,128)(2,1)S(1)}, bf16[272,1024]{1,0:T(8,128)(2,1)S(1)}, u32[]{:S(2)}, u32[]{:S(2)}) collective-permute-start(bf16[272,1024]{1,0:T(8,128)(2,1)S(1)} %pad.12.own), channel_id=1, source_target_pairs={{0,8},{8,0},{32,40},{40,32},{64,72},{72,64},{96,104},{104,96},{16,... | collective-permute-start | bytes 1671176 | tf_op jit(solution)/shard_map/ppermute | solution.py:46
  60.5 12.0 %collective-permute-start.8 = (bf16[1024,896]{1,0:T(8,128)(2,1)}, bf16[1024,896]{1,0:T(8,128)(2,1)S(1)}, u32[]{:S(2)}, u32[]{:S(2)}) collective-permute-start(bf16[1024,896]{1,0:T(8,128)(2,1)} %collective-permute-done.5.oth), channel_id=1, source_target_pairs={{0,8},{8,0},{32,40},{40,32},{64,72},{72,64},{96,104},{104,96},{16,... | collective-permute-start | bytes 5505032 | tf_op jit(solution)/shard_map/ppermute | solution.py:46
  61.4 17.2 %collective-permute-start.21 = (bf16[132,1024]{1,0:T(8,128)(2,1)}, bf16[132,1024]{1,0:T(8,128)(2,1)}, u32[]{:S(2)}, u32[]{:S(2)}) collective-permute-start(bf16[132,1024]{1,0:T(8,128)(2,1)} %get-tuple-element.199), channel_id=1, source_target_pairs={{0,8},{8,0},{32,40},{40,32},{64,72},{72,64},{96,104},{104,96},{16,... | collective-permute-start | bytes 811016 | tf_op jit(solution)/shard_map/ppermute | solution.py:46
  75.0 28.5 %collective-permute-start.12 = (f32[320,512]{1,0:T(8,128)}, f32[320,512]{1,0:T(8,128)S(1)}, u32[]{:S(2)}, u32[]{:S(2)}) collective-permute-start(f32[320,512]{1,0:T(8,128)} %constant_dynamic-slice_fusion.3), channel_id=1, source_target_pairs={{0,1},{8,9},{32,33},{40,41},{64,65},{72,73},{96,97},{104,105},{16,... | collective-permute-start | bytes 1966088 | tf_op jit(solution)/shard_map/ppermute | solution.py:46
  75.3 28.2 %collective-permute-start.13 = (bf16[272,1024]{1,0:T(8,128)(2,1)S(1)}, bf16[272,1024]{1,0:T(8,128)(2,1)}, u32[]{:S(2)}, u32[]{:S(2)}) collective-permute-start(bf16[272,1024]{1,0:T(8,128)(2,1)S(1)} %copy-done.7), channel_id=1, source_target_pairs={{0,1},{8,9},{32,33},{40,41},{64,65},{72,73},{96,97},{104,105},{16,... | collective-permute-start | bytes 1671176 | tf_op jit(solution)/shard_map/ppermute | solution.py:46
  107.2 23.8 %collective-permute-start.15 = (f16[2,272,896]{2,1,0:T(8,128)(2,1)}, f16[2,272,896]{2,1,0:T(8,128)(2,1)S(1)}, u32[]{:S(2)}, u32[]{:S(2)}) collective-permute-start(f16[2,272,896]{2,1,0:T(8,128)(2,1)} %multiply_convert_fusion), channel_id=1, source_target_pairs={{0,96},{8,40},{32,0},{40,72},{64,32},{72,104},{96,64},{104,8},{16,... | collective-permute-start | bytes 2924552 | tf_op jit(solution)/shard_map/ppermute | solution.py:46
  112.4 18.7 %collective-permute-start.14 = (f16[2,272,896]{2,1,0:T(8,128)(2,1)}, f16[2,272,896]{2,1,0:T(8,128)(2,1)}, u32[]{:S(2)}, u32[]{:S(2)}) collective-permute-start(f16[2,272,896]{2,1,0:T(8,128)(2,1)} %multiply_convert_fusion.1), channel_id=1, source_target_pairs={{0,32},{8,104},{32,64},{40,8},{64,96},{72,40},{96,0},{104,72},{16,... | collective-permute-start | bytes 2924552 | tf_op jit(solution)/shard_map/ppermute | solution.py:46
  112.4 17.8 %collective-permute-start.17 = (bf16[272,1024]{1,0:T(8,128)(2,1)}, bf16[272,1024]{1,0:T(8,128)(2,1)S(1)}, u32[]{:S(2)}, u32[]{:S(2)}) collective-permute-start(bf16[272,1024]{1,0:T(8,128)(2,1)} %collective-permute-done.13.oth), channel_id=1, source_target_pairs={{0,8},{8,0},{32,40},{40,32},{64,72},{72,64},{96,104},{104,96},{16,... | collective-permute-start | bytes 1671176 | tf_op jit(solution)/shard_map/ppermute | solution.py:46
  113.7 16.5 %collective-permute-start.16 = (f32[160,512]{1,0:T(8,128)S(1)}, f32[160,512]{1,0:T(8,128)S(1)}, u32[]{:S(2)}, u32[]{:S(2)}) collective-permute-start(f32[160,512]{1,0:T(8,128)S(1)} %constant_dynamic-slice_fusion.2), channel_id=1, source_target_pairs={{0,4},{8,12},{32,36},{40,44},{64,68},{72,76},{96,100},{104,108},{1... | collective-permute-start | bytes 983048 | tf_op jit(solution)/shard_map/ppermute | solution.py:46
  134.3 29.3 %collective-permute-start.18 = (f16[2,272,896]{2,1,0:T(8,128)(2,1)}, f16[2,272,896]{2,1,0:T(8,128)(2,1)S(1)}, u32[]{:S(2)}, u32[]{:S(2)}) collective-permute-start(f16[2,272,896]{2,1,0:T(8,128)(2,1)} %add_convert_fusion), channel_id=1, source_target_pairs={{0,32},{8,104},{32,64},{40,8},{64,96},{72,40},{96,0},{104,72},{16,... | collective-permute-start | bytes 2924552 | tf_op jit(solution)/shard_map/ppermute | solution.py:46
  137.1 17.5 %collective-permute-start.20 = (f16[2,176,896]{2,1,0:T(8,128)(2,1)}, f16[2,176,896]{2,1,0:T(8,128)(2,1)}, u32[]{:S(2)}, u32[]{:S(2)}) collective-permute-start(f16[2,176,896]{2,1,0:T(8,128)(2,1)} %multiply_convert_fusion.2), channel_id=1, source_target_pairs={{0,96},{8,40},{32,0},{40,72},{64,32},{72,104},{96,64},{104,8},{16,... | collective-permute-start | bytes 1892360 | tf_op jit(solution)/shard_map/ppermute | solution.py:46
  139.8 23.9 %collective-permute-start.19 = (f16[2,176,896]{2,1,0:T(8,128)(2,1)}, f16[2,176,896]{2,1,0:T(8,128)(2,1)}, u32[]{:S(2)}, u32[]{:S(2)}) collective-permute-start(f16[2,176,896]{2,1,0:T(8,128)(2,1)} %multiply_convert_fusion.3), channel_id=1, source_target_pairs={{0,32},{8,104},{32,64},{40,8},{64,96},{72,40},{96,0},{104,72},{16,... | collective-permute-start | bytes 1892360 | tf_op jit(solution)/shard_map/ppermute | solution.py:46
  140.2 14.0 %collective-permute-start.22 = (f32[80,512]{1,0:T(8,128)S(1)}, f32[80,512]{1,0:T(8,128)S(1)}, u32[]{:S(2)}, u32[]{:S(2)}) collective-permute-start(f32[80,512]{1,0:T(8,128)S(1)} %constant_dynamic-slice_fusion), channel_id=1, source_target_pairs={{0,2},{8,10},{32,34},{40,42},{64,66},{72,74},{96,98},{104,106},{16... | collective-permute-start | bytes 491528 | tf_op jit(solution)/shard_map/ppermute | solution.py:46
  165.2 17.5 %collective-permute-start.26 = (f16[2,144,272]{2,1,0:T(8,128)(2,1)S(1)}, f16[2,144,272]{2,1,0:T(8,128)(2,1)S(1)}, u32[]{:S(2)}, u32[]{:S(2)}) collective-permute-start(f16[2,144,272]{2,1,0:T(8,128)(2,1)S(1)} %multiply_convert_fusion.4), channel_id=1, source_target_pairs={{0,96},{8,40},{32,0},{40,72},{64,32},{72,104},{96,64},{104,8},{16,... | collective-permute-start | bytes 470024 | tf_op jit(solution)/shard_map/ppermute | solution.py:46
  168.6 15.1 %collective-permute-start.24 = (f16[2,176,896]{2,1,0:T(8,128)(2,1)S(1)}, f16[2,176,896]{2,1,0:T(8,128)(2,1)S(1)}, u32[]{:S(2)}, u32[]{:S(2)}) collective-permute-start(f16[2,176,896]{2,1,0:T(8,128)(2,1)S(1)} %add_convert_fusion.1), channel_id=1, source_target_pairs={{0,32},{8,104},{32,64},{40,8},{64,96},{72,40},{96,0},{104,72},{16,... | collective-permute-start | bytes 1892360 | tf_op jit(solution)/shard_map/ppermute | solution.py:46
  170.4 13.3 %collective-permute-start.23 = (f16[272,896]{1,0:T(8,128)(2,1)S(1)}, f16[272,896]{1,0:T(8,128)(2,1)S(1)}, u32[]{:S(2)}, u32[]{:S(2)}) collective-permute-start(f16[272,896]{1,0:T(8,128)(2,1)S(1)} %fusion.9), channel_id=1, source_target_pairs={{0,16},{8,24},{32,48},{40,56},{64,80},{72,88},{96,112},{104,120},{... | collective-permute-start | bytes 1462280 | tf_op jit(solution)/shard_map/ppermute | solution.py:46
  183.7 17.6 %collective-permute-start.32 = (f32[2,1,2,80,512]{4,3,2,1,0:T(8,128)}, f32[2,1,2,80,512]{4,3,2,1,0:T(8,128)}, u32[]{:S(2)}, u32[]{:S(2)}) collective-permute-start(f32[2,1,2,80,512]{4,3,2,1,0:T(8,128)} %maximum_select_fusion.1), channel_id=1, source_target_pairs={{0,4},{8,12},{32,36},{40,44},{64,68},{72,76},{96,100},{104,108},{1... | collective-permute-start | bytes 1966088 | tf_op jit(solution)/shard_map/ppermute | solution.py:46
  186.3 17.1 %collective-permute-start.29 = (f16[272,896]{1,0:T(8,128)(2,1)}, f16[272,896]{1,0:T(8,128)(2,1)}, u32[]{:S(2)}, u32[]{:S(2)}) collective-permute-start(f16[272,896]{1,0:T(8,128)(2,1)} %fusion.4), channel_id=1, source_target_pairs={{16,1},{24,9},{48,33},{56,41},{80,65},{88,73},{112,97},{120,105},{... | collective-permute-start | bytes 1462280 | tf_op jit(solution)/shard_map/ppermute | solution.py:46
  192.6 10.8 %collective-permute-start.30 = (f16[176,896]{1,0:T(8,128)(2,1)}, f16[176,896]{1,0:T(8,128)(2,1)S(1)}, u32[]{:S(2)}, u32[]{:S(2)}) collective-permute-start(f16[176,896]{1,0:T(8,128)(2,1)} %fusion.11), channel_id=1, source_target_pairs={{0,16},{8,24},{32,48},{40,56},{64,80},{72,88},{96,112},{104,120},{... | collective-permute-start | bytes 946184 | tf_op jit(solution)/shard_map/ppermute | solution.py:46
  (45 other events, 327.2 us)
Sparse Core Ops, SparseCore 0:
  14.6 52.6 all-gather.6
  69.6 37.8 all-gather.8
  109.1 36.0 all-gather.10

commit v4 on v3

v4 whole, which is shorter than its diff:
```python
import functools
import itertools

import jax
import jax.numpy as jnp
from jax import lax
from jax.experimental import pallas as pl
from jax.experimental.pallas import tpu as pltpu
from jax.sharding import PartitionSpec as P

AXES = ("dp", "block")
HALF = jnp.float16


def place(x, y, z, core):
    return ((z * 2 + y % 2) * 2 + core) * 8 + x * 2 + y // 2


def pairs(move):
    out = []
    for at in itertools.product(range(4), range(4), range(4), range(2)):
        x, y, z, core = move(*at)
        out.append((place(*at), place(x % 4, y % 4, z % 4, core % 2)))
    return out


SIBLING = pairs(lambda x, y, z, c: (x, y, z, c + 1))
OTHER_COLUMN = pairs(lambda x, y, z, c: (x, y + 2, z, c))
X_DOWN = pairs(lambda x, y, z, c: (x - 1, y, z, c))
X_UP = pairs(lambda x, y, z, c: (x + 1, y, z, c))
X_FAR = pairs(lambda x, y, z, c: (x + 2, y, z, c))
Z_ALONG = pairs(lambda x, y, z, c: (x, y, z + 1 - 2 * c, c))
Z_AGAINST = pairs(lambda x, y, z, c: (x, y, z - 1 + 2 * c, c))
X_RINGS = [
    [place(x, y, z, c) for x in range(4)]
    for y, z, c in itertools.product(range(4), range(4), range(2))
]
FIRST = 304
Y_PARTNER = pairs(lambda x, y, z, c: (x, y ^ 1, z, c))
Y_ROUND = pairs(lambda x, y, z, c: (x, (2, 0, 3, 1)[y], z, c))
Y_MIDDLE = [p for p in pairs(lambda x, y, z, c: (x, (0, 2, 1, 3)[y], z, c)) if p[0] != p[1]]


def send(value, to):
    return lax.ppermute(value, AXES, to)


def turn_kernel(core, own, mine, theirs, turned):
    half = mine.shape[0]
    turned[...] = own[...].T
    mine[...] = turned[pl.ds(pl.multiple_of(core[0] * half, 16), half), :]
    theirs[...] = turned[pl.ds(pl.multiple_of((1 - core[0]) * half, 16), half), :]


def turn(own, core):
    tokens, width = own.shape
    vmem = pl.BlockSpec(memory_space=pltpu.VMEM)
    half = jax.ShapeDtypeStruct((width // 2, tokens), own.dtype)
    return pl.pallas_call(
        turn_kernel,
        out_shape=(half, half),
        in_specs=[pl.BlockSpec(memory_space=pltpu.SMEM), vmem],
        out_specs=(vmem, vmem),
        scratch_shapes=[pltpu.VMEM((width, tokens), own.dtype)],
        compiler_params=pltpu.CompilerParams(vmem_limit_bytes=24 << 20),
    )(core.reshape(1).astype(jnp.int32), own)


def product_kernel(kinds, slots, source, rows, *refs):
    count = len(slots)
    columns_of, refs = refs[: 4 * len(kinds)], refs[4 * len(kinds) :]
    outs, refs = refs[:count], refs[count:]
    *buffers, sem = refs
    block, at = pl.program_id(0), pl.program_id(1)
    start, column_waits, row_waits, work = [], ([], []), [[] for _ in slots], []
    lane = 0
    for kind, (first, turned) in enumerate(kinds):
        held, columns, landing = buffers[3 * kind : 3 * kind + 3]
        n, tokens = held.shape[1], held.shape[2] // 2
        width = columns.shape[2]
        part = [pl.ds(half * tokens, tokens) for half in (0, 1)]
        for i in (0, 1):
            for half in (0, 1):
                ref = columns_of[4 * kind + 2 * i + half]
                if turned:
                    place = landing.at[i, :, part[half]]
                else:
                    place = columns.at[i, part[half], :]
                column_waits[i].append(
                    pltpu.make_async_copy(ref, place, sem.at[kind, half, i])
                )
        for i, slot in enumerate(slots):
            for half in (0, 1):
                row_waits[i].append(
                    pltpu.make_async_copy(
                        rows.at[source[slot], half, pl.ds(first, n), :],
                        held.at[i, :, part[half]],
                        sem.at[kind, half, 2 + i],
                    )
                )
        work.append((held, columns, landing if turned else None, lane, width))
        lane += width

    @pl.when((block == 0) & (at == 0))
    def _():
        for copy in column_waits[0] + sum(row_waits, []) + column_waits[1]:
            copy.start()

    for i in (0, 1):

        @pl.when((block == i) & (at == 0))
        def _(i=i):
            for copy in column_waits[i]:
                copy.wait()
            for _, columns, landing, _, _ in work:
                if landing is not None:
                    columns[i] = landing[i].T

    for i in range(count):

        @pl.when((block == 0) & (at == i))
        def _(i=i):
            for copy in row_waits[i]:
                copy.wait()

    for i, out in enumerate(outs):

        @pl.when(at == i)
        def _(i=i, out=out):
            for held, columns, _, lane, width in work:
                out[0, :, lane : lane + width] = jnp.dot(
                    held[i], columns[block], preferred_element_type=jnp.float32
                )


def products(source, slots, rows, n, columns, grad_columns=()):
    tokens = rows.shape[3]
    dtype = rows.dtype
    count = len(slots)
    kinds, widths, buffers = [(0, False)], [columns[0].shape[1]], []
    if grad_columns:
        kinds.append((n, True))
        widths.append(grad_columns[0].shape[0])
    for (_, turned), width in zip(kinds, widths):
        buffers += [
            pltpu.VMEM((count, n, 2 * tokens), dtype),
            pltpu.VMEM((2, 2 * tokens, width), dtype),
            pltpu.VMEM((2, width, 2 * tokens) if turned else (16, 128), dtype),
        ]
    anywhere = pl.BlockSpec(memory_space=pl.ANY)
    smem = pl.BlockSpec(memory_space=pltpu.SMEM)
    return pl.pallas_call(
        functools.partial(product_kernel, kinds, slots),
        out_shape=[jax.ShapeDtypeStruct((2, n, sum(widths)), jnp.float32)] * count,
        grid=(2, count),
        in_specs=[smem] + [anywhere] * (1 + 4 * len(kinds)),
        out_specs=[pl.BlockSpec((1, n, sum(widths)), lambda block, at: (block, 0, 0))] * count,
        scratch_shapes=[*buffers, pltpu.SemaphoreType.DMA((len(kinds), 2, 2 + count))],
        compiler_params=pltpu.CompilerParams(vmem_limit_bytes=60 << 20),
        cost_estimate=pl.CostEstimate(
            flops=4 * count * n * tokens * sum(widths),
            bytes_accessed=4 * count * n * tokens,
            transcendentals=0,
        ),
    )(source, rows, *columns, *grad_columns)


def largest_over(largest, *moves):
    for move in moves:
        largest = jnp.maximum(largest, send(largest, pairs(move)))
    return largest


def scales(largest, tokens_total):
    largest = jnp.maximum(largest, 1e-18)
    most = largest * largest * tokens_total
    return 32768.0 / most, most / (32768.0 * tokens_total)


def far(p):
    second, third = p.pop("far")
    a = send((second * p["down"]).astype(HALF), Z_ALONG)
    return {**p, "a": a, "c": send((third * p["down"]).astype(HALF), Z_AGAINST)}


def along(p):
    b = p["close"][1] * p["down"] + p["a"].astype(jnp.float32)
    return {**p, "a": None, "b": send(b.astype(HALF), Z_ALONG)}


def summed(p):
    b, c = p["b"].astype(jnp.float32), p["c"].astype(jnp.float32)
    return p["close"][0] * p["down"] + b + c


def near(p, stays):
    total = summed(p)
    value = jnp.where(stays, total[1], total[0])
    return {"total": total, "n": send(value.astype(HALF), Y_PARTNER)}


def cross(p):
    value = p["total"][1] + p["n"].astype(jnp.float32)
    return {**p, "m": send(value.astype(HALF), Y_MIDDLE)}


def crossed(p, stays):
    own = p["total"][0] + p["n"].astype(jnp.float32)
    return jnp.where(stays, own, p["m"].astype(jnp.float32))


def across(p, stays):
    total = summed(p)
    value = jnp.where(stays, total[1], total[0])
    n, m = send(value.astype(HALF), Y_ROUND), send(total[1].astype(HALF), Y_MIDDLE)
    return {"total": total, "n": n, "m": m}


def result(p, stays):
    other = jnp.where(stays, p["total"][0], p["m"].astype(jnp.float32))
    return p["n"].astype(jnp.float32) + other


def turned_product(basis, queries):
    return lax.dot_general(
        basis, queries, (((0,), (1,)), ((), ())), preferred_element_type=jnp.float32
    )


def give(value, bit, to, axis):
    return (value, send(lax.dynamic_slice_in_dim(value, 1 - bit, 1, axis), to))


def add(value, got, bit, axis):
    return lax.dynamic_slice_in_dim(value, bit, 1, axis) + got


def scatter_x(value, x):
    quarter = [
        lax.dynamic_index_in_dim(value[:, 0], (x + d) % 4, 0, keepdims=False) for d in range(4)
    ]
    return [quarter[0]] + [send(q, to) for q, to in zip(quarter[1:], (X_UP, X_FAR, X_DOWN))]


def round_x(rows):
    return lax.all_gather(rows, AXES, axis_index_groups=X_RINGS)


def on_device(activations, out_grads, act_basis, grad_basis, query_acts, query_grads):
    dp, block = lax.axis_index("dp"), lax.axis_index("block")
    x, y_hi, z, y_lo, core = block // 2, block % 2, dp // 4, dp // 2 % 2, dp % 2
    tokens_total = activations.shape[0] * lax.axis_size("dp")
    source = jnp.stack([(z + d * (1 - 2 * core)) % 4 for d in range(4)]).astype(jnp.int32)
    half = out_grads.shape[1] // 2

    mine, theirs = turn(activations, core)
    other = send(activations, OTHER_COLUMN)
    got = send(theirs, SIBLING)
    rows_1 = round_x(jnp.stack([mine[:FIRST], got[:FIRST]]))
    rows_2 = jnp.stack([mine[FIRST:], got[FIRST:]])
    sibling = send(activations, SIBLING)
    grads = jnp.pad(out_grads.T, ((0, -out_grads.shape[1] % 16), (0, 0)))
    grad_mine = lax.dynamic_slice_in_dim(grads, core * half, half, 0)
    grad_theirs = lax.dynamic_slice_in_dim(grads, (1 - core) * half, half, 0)
    grad_rows = jnp.stack([grad_mine, send(grad_theirs, SIBLING)])
    grad_rows = jnp.pad(grad_rows, ((0, 0), (0, rows_2.shape[1] - half), (0, 0)))
    grad_sibling = send(grads, SIBLING)
    part = jnp.concatenate(
        [turned_product(act_basis, query_acts), turned_product(grad_basis, query_grads)], axis=0
    )
    queries = query_acts.shape[0]
    part = jnp.pad(part, ((0, -part.shape[0] % 64), (0, 0))).reshape(4, 2, -1, queries)
    largest = largest_over(
        jnp.where(
            lax.broadcasted_iota(jnp.int32, (8, 128), 0) < 4,
            jnp.max(jnp.abs(activations)).astype(jnp.float32),
            jnp.max(jnp.abs(out_grads)).astype(jnp.float32),
        ),
        lambda x, y, z, c: (x, y, z, c + 1),
        lambda x, y, z, c: (x, y, z ^ 1, c),
        lambda x, y, z, c: (x, y, z + 2, c),
        lambda x, y, z, c: (x ^ 1, y, z, c),
        lambda x, y, z, c: (x + 2, y, z, c),
    )
    n_2 = rows_2.shape[1]
    rows_2 = jnp.concatenate([rows_2, grad_rows], axis=1)
    largest, other, sibling, grads, rows_2, grad_sibling, part = lax.optimization_barrier(
        (largest, other, sibling, grads, rows_2, grad_sibling, part)
    )
    rows_2 = round_x(rows_2)
    largest = largest_over(
        largest, lambda x, y, z, c: (x, y ^ 1, z, c), lambda x, y, z, c: (x, y + 2, z, c)
    )
    act_down, act_up = scales(largest[0, 0], tokens_total)
    grad_down, grad_up = scales(largest[4, 0], tokens_total)
    columns = [activations, sibling, other, send(other, SIBLING)]
    columns, rows_1, grads, grad_sibling, part, act_down, act_up, grad_down, grad_up = (
        lax.optimization_barrier(
            (columns, rows_1, grads, grad_sibling, part, act_down, act_up, grad_down, grad_up)
        )
    )

    width, grad_width = activations.shape[1], grads.shape[0]
    down = jnp.where(jnp.arange(width + grad_width) < width, act_down, grad_down)
    one, two = {"down": act_down}, {"down": down}
    stays = y_lo == y_hi
    one["far"] = products(source, (2, 3), rows_1, FIRST, columns)
    grad_other = send(grads, OTHER_COLUMN)
    one, grad_other = lax.optimization_barrier((one, grad_other))

    one = far(one)
    part = give(part, y_hi, OTHER_COLUMN, 1)
    one["close"] = products(source, (0, 1), rows_1, FIRST, columns)
    grad_columns = [grads, grad_sibling, grad_other, send(grad_other, SIBLING)]
    one, part, grad_columns = lax.optimization_barrier((one, part, grad_columns))

    one = along(one)
    part = scatter_x(add(*part, y_hi, 1), x)
    two["far"] = products(source, (2, 3), rows_2, n_2, columns, grad_columns)
    one, two, part = lax.optimization_barrier((one, two, part))

    part = sum(part)
    part = (part, send(part, OTHER_COLUMN))
    one, two = near(one, stays), far(two)
    two["close"] = products(source, (0, 1), rows_2, n_2, columns, grad_columns)
    one, two, part = lax.optimization_barrier((one, two, part))

    part = round_x(jnp.where(y_hi == 0, jnp.stack(part), jnp.stack(part[::-1])))
    one = cross(one)
    two = along(two)
    one, two = lax.optimization_barrier((one, two))

    two = across(two, stays)
    act_cov = jnp.concatenate(
        [crossed(one, stays), result(two, stays)[:, :width]], axis=0
    )
    grad_cov = result(two, stays)[:half, width : width + out_grads.shape[1]]
    part = part.reshape(-1, queries)
    split, end = act_basis.shape[1], act_basis.shape[1] + grad_basis.shape[1]
    return (act_cov * act_up, grad_cov * grad_up, part[:split].T, part[split:end].T)


def solution(mesh):
    return jax.shard_map(
        on_device,
        mesh=mesh,
        in_specs=(
            P("dp", "block"),
            P("dp", "block"),
            P("block", "dp"),
            P("block", "dp"),
            P(None, "block"),
            P(None, "block"),
        ),
        out_specs=(P("dp", "block"), P("dp", "block"), P(None, "dp"), P(None, "dp")),
        check_vma=False,
    )
```

time: 229 us -> 220 us (0.961)
  starting transfers between devices: 50.1 us -> 36.7 us
  waiting for transfers between devices: 74.5 us -> 79 us
  other arithmetic: 33.1 us -> 30 us
    ppermute x36 -> x30, starting transfers between devices: 50 us -> 36.6 us  [send(): return lax.ppermute(value, AXES, to)]
    ppermute x36 -> x30, waiting for transfers between devices: 71 us -> 77.1 us  [send(): return lax.ppermute(value, AXES, to)]
    select_n x5 -> x3, other arithmetic: 4.26 us -> 1.96 us  [the longest x1 1.2 us: crossed(): return jnp.where(stays, own, p['m'].astype(jnp.float32))]
    pallas_call x3 -> x4, Pallas kernels: 38.9 us -> 40.5 us  [products(): pl.pallas_call(functools.partial(product_kernel, kinds, slots), out_shape...]
    convert_element_type x3 -> x2, other arithmetic: 4.83 us -> 6.38 us  [far(): return {**p, 'a': a, 'c': send((third * p['down']).astype(HALF), Z_AGAINST)}]
    convert_element_type x3 -> x2, other arithmetic: 5.27 us -> 6.35 us  [along(): return {**p, 'a': None, 'b': send(b.astype(HALF), Z_ALONG)}]
  transfers between devices with their start and end apart: 39 -> 33, of which waited for: 17 -> 16; matrix products, arithmetic and copies ran while one was open for 17% -> 13% of each run, Pallas kernels for 17% -> 19%
where the time goes in v4:
time: 220 us; the launch traced here: 217 us
  waiting for transfers between devices  79 us (36%)
  Pallas kernels  41.2 us (19%)
  starting transfers between devices  36.7 us (17%)
  other arithmetic  30 us (14%)
  between operations  16.9 us (8%)
  local copies, waits for them, and re-layouts  12 us (5%)
    ppermute x30, waiting for transfers between devices, send(): return lax.ppermute(value, AXES, to)  77.1 us
    pallas_call x4, Pallas kernels, products(): pl.pallas_call(functools.partial(product_kernel, kinds, slots), out_shape...  40.5 us
    ppermute x30, starting transfers between devices, send(): return lax.ppermute(value, AXES, to)  36.6 us
    convert_element_type x2, other arithmetic, far(): return {**p, 'a': a, 'c': send((third * p['down']).astype(HALF), Z_AGAINST)}  6.38 us
    convert_element_type x2, other arithmetic, along(): return {**p, 'a': None, 'b': send(b.astype(HALF), Z_ALONG)}  6.35 us
  transfers between devices with their start and end apart: 33, of which 16 were waited for; matrix products, arithmetic and copies ran while one was open for 13% of the time, Pallas kernels for 19%

profile of v4, /device:TPU:16, one launch (start us, length us, event | category | flops | bytes accessed | tf_op | source)
XLA Modules:
  0.0 216.6 jit_solution(13226557056928116908)
XLA Ops:
  9.7 2.4 %collective-permute-done.7 = bf16[448,1024]{1,0:T(8,128)(2,1)S(1)} collective-permute-done((bf16[448,1024]{1,0:T(8,128)(2,1)S(1)}, bf16[448,1024]{1,0:T(8,128)(2,1)S(1)}, u32[]{:S(2)}, u32[]{:S(2)}) %collective-permute-start.7) | collective-permute-done | bytes 917536 | tf_op jit(solution)/shard_map/ppermute | solution.py:45
  24.4 4.0 %collective-permute-start.2 = (f32[8,128]{1,0:T(8,128)S(1)}, f32[8,128]{1,0:T(8,128)S(1)}, u32[]{:S(2)}, u32[]{:S(2)}) collective-permute-start(f32[8,128]{1,0:T(8,128)S(1)} %fusion.16), channel_id=1, source_target_pairs={{0,64},{8,72},{32,96},{40,104},{64,0},{72,8},{96,32},{104,40},{16,... | collective-permute-start | bytes 12296 | tf_op jit(solution)/shard_map/ppermute | solution.py:45
  33.6 3.0 %collective-permute-start.4 = (f32[8,128]{1,0:T(8,128)S(1)}, f32[8,128]{1,0:T(8,128)S(1)}, u32[]{:S(2)}, u32[]{:S(2)}) collective-permute-start(f32[8,128]{1,0:T(8,128)S(1)} %max.32), channel_id=1, source_target_pairs={{0,4},{8,12},{32,36},{40,44},{64,68},{72,76},{96,100},{104,108},{1... | collective-permute-start | bytes 12296 | tf_op jit(solution)/shard_map/ppermute | solution.py:45
  41.0 17.6 %collective-permute-done.5.refs_2_ = bf16[1024,896]{1,0:T(8,128)(2,1)} collective-permute-done((bf16[1024,896]{1,0:T(8,128)(2,1)S(1)}, bf16[1024,896]{1,0:T(8,128)(2,1)}, u32[]{:S(2)}, u32[]{:S(2)}) %collective-permute-start.5) | collective-permute-done | bytes 1835040 | tf_op jit(solution)/shard_map/ppermute | solution.py:45
  60.2 2.3 %collective-permute-done.11 = f32[8,128]{1,0:T(8,128)S(1)} collective-permute-done((f32[8,128]{1,0:T(8,128)S(1)}, f32[8,128]{1,0:T(8,128)S(1)}, u32[]{:S(2)}, u32[]{:S(2)}) %collective-permute-start.11) | collective-permute-done | bytes 4128 | tf_op jit(solution)/shard_map/ppermute | solution.py:45
  62.8 4.8 %collective-permute-done.12 = f32[8,128]{1,0:T(8,128)S(1)} collective-permute-done((f32[8,128]{1,0:T(8,128)S(1)}, f32[8,128]{1,0:T(8,128)S(1)}, u32[]{:S(2)}, u32[]{:S(2)}) %collective-permute-start.12) | collective-permute-done | bytes 4128 | tf_op jit(solution)/shard_map/ppermute | solution.py:45
  72.5 10.4 %shard_map.94 = (f32[2,304,896]{2,1,0:T(8,128)}, f32[2,304,896]{2,1,0:T(8,128)}) custom-call(s32[4]{0:T(128)} %pad_add_fusion.source, bf16[4,2,304,1024]{3,2,1,0:T(8,128)(2,1)} %bitcast.65, bf16[1024,896]{1,0:T(8,128)(2,1)} %refs_0_.3, bf16[1024,896]{1,0:T(8,128)(2,1)} %collective-permute-done.6.refs_1_, bf16[1024,896]{1,0:T(8,128)(2,1)} %collective-permute-done.5.refs_2_, ...), custom_call_target="tpu_custom_call" | custom-call | flops 2231369728 | bytes 2490368 | tf_op jit(solution)/shard_map/pallas_call | solution.py:152
  83.0 4.3 %collective-permute-done.13.refs_6_ = bf16[272,1024]{1,0:T(8,128)(2,1)S(1)} collective-permute-done((bf16[272,1024]{1,0:T(8,128)(2,1)S(1)}, bf16[272,1024]{1,0:T(8,128)(2,1)S(1)}, u32[]{:S(2)}, u32[]{:S(2)}) %collective-permute-start.13) | collective-permute-done | bytes 557088 | tf_op jit(solution)/shard_map/ppermute | solution.py:45
  87.3 3.1 %multiply_convert_fusion = f16[2,304,896]{2,1,0:T(8,128)(2,1)} fusion(f32[2,304,896]{2,1,0:T(8,128)} %get-tuple-element.94, f32[]{:T(128)} %bitcast.10), kind=kLoop, calls=%fused_computation.2 | loop fusion | flops 1089536 | bytes 3268612 | tf_op jit(solution)/shard_map/convert_element_type | solution.py:183
  90.4 2.9 %collective-permute-start.15 = (f16[2,304,896]{2,1,0:T(8,128)(2,1)}, f16[2,304,896]{2,1,0:T(8,128)(2,1)S(1)}, u32[]{:S(2)}, u32[]{:S(2)}) collective-permute-start(f16[2,304,896]{2,1,0:T(8,128)(2,1)} %multiply_convert_fusion), channel_id=1, source_target_pairs={{0,96},{8,40},{32,0},{40,72},{64,32},{72,104},{96,64},{104,8},{16,... | collective-permute-start | bytes 3268616 | tf_op jit(solution)/shard_map/ppermute | solution.py:45
  96.0 10.5 %shard_map.95 = (f32[2,304,896]{2,1,0:T(8,128)}, f32[2,304,896]{2,1,0:T(8,128)}) custom-call(s32[4]{0:T(128)} %pad_add_fusion.source, bf16[4,2,304,1024]{3,2,1,0:T(8,128)(2,1)} %bitcast.66, bf16[1024,896]{1,0:T(8,128)(2,1)} %refs_0_.3, bf16[1024,896]{1,0:T(8,128)(2,1)} %collective-permute-done.6.refs_1_, bf16[1024,896]{1,0:T(8,128)(2,1)} %collective-permute-done.5.refs_2_, ...), custom_call_target="tpu_custom_call" | custom-call | flops 2231369728 | bytes 2490368 | tf_op jit(solution)/shard_map/pallas_call | solution.py:152
  106.4 6.2 %collective-permute-done.16 = f32[4,1,80,512]{3,2,1,0:T(8,128)} collective-permute-done((f32[4,1,80,512]{3,2,1,0:T(8,128)}, f32[4,1,80,512]{3,2,1,0:T(8,128)}, u32[]{:S(2)}, u32[]{:S(2)}) %collective-permute-start.16) | collective-permute-done | bytes 655392 | tf_op jit(solution)/shard_map/ppermute | solution.py:45
  112.6 4.7 %collective-permute-done.15 = f16[2,304,896]{2,1,0:T(8,128)(2,1)S(1)} collective-permute-done((f16[2,304,896]{2,1,0:T(8,128)(2,1)}, f16[2,304,896]{2,1,0:T(8,128)(2,1)S(1)}, u32[]{:S(2)}, u32[]{:S(2)}) %collective-permute-start.15) | collective-permute-done | bytes 1089568 | tf_op jit(solution)/shard_map/ppermute | solution.py:45
  117.3 3.7 %add_convert_fusion = f16[2,304,896]{2,1,0:T(8,128)(2,1)} fusion(f16[2,304,896]{2,1,0:T(8,128)(2,1)} %collective-permute-done.14, f32[2,304,896]{2,1,0:T(8,128)} %get-tuple-element.100, f32[]{:T(128)} %bitcast.10), kind=kLoop, calls=%fused_computation.1 | loop fusion | flops 2179072 | bytes 4358148 | tf_op jit(solution)/shard_map/convert_element_type | solution.py:188
  128.4 9.8 %shard_map.96 = (f32[2,144,1168]{2,1,0:T(8,128)}, f32[2,144,1168]{2,1,0:T(8,128)}) custom-call(s32[4]{0:T(128)} %pad_add_fusion.source, bf16[4,2,288,1024]{3,2,1,0:T(8,128)(2,1)} %bitcast.67, bf16[1024,896]{1,0:T(8,128)(2,1)} %refs_0_.3, bf16[1024,896]{1,0:T(8,128)(2,1)} %collective-permute-done.6.refs_1_, bf16[1024,896]{1,0:T(8,128)(2,1)} %collective-permute-done.5.refs_2_, ...), custom_call_target="tpu_custom_call" | custom-call | flops 1377828864 | bytes 1179648 | tf_op jit(solution)/shard_map/pallas_call | solution.py:152
  138.3 3.3 %multiply_convert_fusion.2 = (f16[2,144,1168]{2,1,0:T(8,128)(2,1)}, f16[2,144,1168]{2,1,0:T(8,128)(2,1)}) fusion(f32[2,144,1168]{2,1,0:T(8,128)} %get-tuple-element.121, f32[1168]{0:T(1024)S(1)} %fusion.8, f32[2,144,1168]{2,1,0:T(8,128)} %get-tuple-element.119), kind=kLoop, calls=%fused_computation.8 | loop fusion | flops 1345536 | bytes 4041280 | tf_op jit(solution)/shard_map/convert_element_type | solution.py:183
  149.3 9.8 %shard_map.97 = (f32[2,144,1168]{2,1,0:T(8,128)}, f32[2,144,1168]{2,1,0:T(8,128)}) custom-call(s32[4]{0:T(128)} %pad_add_fusion.source, bf16[4,2,288,1024]{3,2,1,0:T(8,128)(2,1)} %bitcast.68, bf16[1024,896]{1,0:T(8,128)(2,1)} %refs_0_.3, bf16[1024,896]{1,0:T(8,128)(2,1)} %collective-permute-done.6.refs_1_, bf16[1024,896]{1,0:T(8,128)(2,1)} %collective-permute-done.5.refs_2_, ...), custom_call_target="tpu_custom_call" | custom-call | flops 1377828864 | bytes 1179648 | tf_op jit(solution)/shard_map/pallas_call | solution.py:152
  159.1 4.7 %collective-permute-done.25 = f32[80,512]{1,0:T(8,128)S(1)} collective-permute-done((f32[80,512]{1,0:T(8,128)S(1)}, f32[80,512]{1,0:T(8,128)S(1)}, u32[]{:S(2)}, u32[]{:S(2)}) %collective-permute-start.25) | collective-permute-done | bytes 163872 | tf_op jit(solution)/shard_map/ppermute | solution.py:45
  163.8 2.7 %add_convert_fusion.1 = f16[2,144,1168]{2,1,0:T(8,128)(2,1)} fusion(f16[2,144,1168]{2,1,0:T(8,128)(2,1)} %collective-permute-done.23, f32[2,144,1168]{2,1,0:T(8,128)} %get-tuple-element.130, f32[1168]{0:T(1024)S(1)} %fusion.8), kind=kLoop, calls=%fused_computation.7 | loop fusion | flops 1345536 | bytes 2695744 | tf_op jit(solution)/shard_map/convert_element_type | solution.py:188
  167.7 3.0 %collective-permute-start.26 = (f16[304,896]{1,0:T(8,128)(2,1)}, f16[304,896]{1,0:T(8,128)(2,1)}, u32[]{:S(2)}, u32[]{:S(2)}) collective-permute-start(f16[304,896]{1,0:T(8,128)(2,1)} %fusion.4), channel_id=1, source_target_pairs={{16,1},{24,9},{48,33},{56,41},{80,65},{88,73},{112,97},{120,105},{... | collective-permute-start | bytes 1634312 | tf_op jit(solution)/shard_map/ppermute | solution.py:45
  171.5 11.9 %collective-permute-done.26 = f16[304,896]{1,0:T(8,128)(2,1)} collective-permute-done((f16[304,896]{1,0:T(8,128)(2,1)}, f16[304,896]{1,0:T(8,128)(2,1)}, u32[]{:S(2)}, u32[]{:S(2)}) %collective-permute-start.26) | collective-permute-done | bytes 544800 | tf_op jit(solution)/shard_map/ppermute | solution.py:45
  185.8 3.6 %collective-permute-start.29 = (f16[144,1168]{1,0:T(8,128)(2,1)S(1)}, f16[144,1168]{1,0:T(8,128)(2,1)S(1)}, u32[]{:S(2)}, u32[]{:S(2)}) collective-permute-start(f16[144,1168]{1,0:T(8,128)(2,1)S(1)} %fusion.5), channel_id=1, source_target_pairs={{16,1},{24,9},{48,33},{56,41},{80,65},{88,73},{112,97},{120,105},{... | collective-permute-start | bytes 1009160 | tf_op jit(solution)/shard_map/ppermute | solution.py:45
  190.6 5.7 %collective-permute-done.28 = f16[144,1168]{1,0:T(8,128)(2,1)S(1)} collective-permute-done((f16[144,1168]{1,0:T(8,128)(2,1)S(1)}, f16[144,1168]{1,0:T(8,128)(2,1)S(1)}, u32[]{:S(2)}, u32[]{:S(2)}) %collective-permute-start.28) | collective-permute-done | bytes 336416 | tf_op jit(solution)/shard_map/ppermute | solution.py:45
  196.3 7.8 %collective-permute-done.29 = f16[144,1168]{1,0:T(8,128)(2,1)S(1)} collective-permute-done((f16[144,1168]{1,0:T(8,128)(2,1)S(1)}, f16[144,1168]{1,0:T(8,128)(2,1)S(1)}, u32[]{:S(2)}, u32[]{:S(2)}) %collective-permute-start.29) | collective-permute-done | bytes 336416 | tf_op jit(solution)/shard_map/ppermute | solution.py:45
  (145 shorter events, 57.4 us)
Async XLA Ops:
  7.2 64.3 %all-gather.8.cloned.1.call-start = ((), (), s32[]{:S(2)}) async-start(), calls=%async_computation.1 | async-start | bytes 6225920 | tf_op jit(solution)/shard_map/all_gather | solution.py:246
  14.2 114.1 %all-gather.10.cloned.1.call-start = ((), (), s32[]{:S(2)}) async-start(), calls=%async_computation.2 | async-start | bytes 5898240 | tf_op jit(solution)/shard_map/all_gather | solution.py:246
  15.0 43.7 %collective-permute-start.5 = (bf16[1024,896]{1,0:T(8,128)(2,1)S(1)}, bf16[1024,896]{1,0:T(8,128)(2,1)}, u32[]{:S(2)}, u32[]{:S(2)}) collective-permute-start(bf16[1024,896]{1,0:T(8,128)(2,1)S(1)} %copy-done.3), channel_id=1, source_target_pairs={{0,1},{8,9},{32,33},{40,41},{64,65},{72,73},{96,97},{104,105},{16,... | collective-permute-start | bytes 5505032 | tf_op jit(solution)/shard_map/ppermute | solution.py:45
  15.2 43.4 %collective-permute-start.6 = (bf16[1024,896]{1,0:T(8,128)(2,1)S(1)}, bf16[1024,896]{1,0:T(8,128)(2,1)}, u32[]{:S(2)}, u32[]{:S(2)}) collective-permute-start(bf16[1024,896]{1,0:T(8,128)(2,1)S(1)} %copy-done.3), channel_id=1, source_target_pairs={{0,8},{8,0},{32,40},{40,32},{64,72},{72,64},{96,104},{104,96},{16,... | collective-permute-start | bytes 5505032 | tf_op jit(solution)/shard_map/ppermute | solution.py:45
  18.8 20.0 %collective-permute-start.8 = (bf16[132,1024]{1,0:T(8,128)(2,1)S(1)}, bf16[132,1024]{1,0:T(8,128)(2,1)S(1)}, u32[]{:S(2)}, u32[]{:S(2)}) collective-permute-start(bf16[132,1024]{1,0:T(8,128)(2,1)S(1)} %get-tuple-element.151), channel_id=1, source_target_pairs={{0,8},{8,0},{32,40},{40,32},{64,72},{72,64},{96,104},{104,96},{16,... | collective-permute-start | bytes 811016 | tf_op jit(solution)/shard_map/ppermute | solution.py:45
  20.1 20.9 %collective-permute-start.9 = (bf16[272,1024]{1,0:T(8,128)(2,1)S(1)}, bf16[272,1024]{1,0:T(8,128)(2,1)}, u32[]{:S(2)}, u32[]{:S(2)}) collective-permute-start(bf16[272,1024]{1,0:T(8,128)(2,1)S(1)} %pad.12.refs_4_), channel_id=1, source_target_pairs={{0,8},{8,0},{32,40},{40,32},{64,72},{72,64},{96,104},{104,96},{16,... | collective-permute-start | bytes 1671176 | tf_op jit(solution)/shard_map/ppermute | solution.py:45
  58.7 147.6 %all-gather.6.cloned.1.call-start = ((), (), s32[]{:S(2)}) async-start(), calls=%async_computation | async-start | bytes 1638400 | tf_op jit(solution)/shard_map/all_gather | solution.py:246
  58.7 10.8 %collective-permute-start.10 = (bf16[1024,896]{1,0:T(8,128)(2,1)}, bf16[1024,896]{1,0:T(8,128)(2,1)S(1)}, u32[]{:S(2)}, u32[]{:S(2)}) collective-permute-start(bf16[1024,896]{1,0:T(8,128)(2,1)} %collective-permute-done.5.refs_2_), channel_id=1, source_target_pairs={{0,8},{8,0},{32,40},{40,32},{64,72},{72,64},{96,104},{104,96},{16,... | collective-permute-start | bytes 5505032 | tf_op jit(solution)/shard_map/ppermute | solution.py:45
  71.4 15.9 %collective-permute-start.13 = (bf16[272,1024]{1,0:T(8,128)(2,1)S(1)}, bf16[272,1024]{1,0:T(8,128)(2,1)S(1)}, u32[]{:S(2)}, u32[]{:S(2)}) collective-permute-start(bf16[272,1024]{1,0:T(8,128)(2,1)S(1)} %pad.12.refs_4_), channel_id=1, source_target_pairs={{0,1},{8,9},{32,33},{40,41},{64,65},{72,73},{96,97},{104,105},{16,... | collective-permute-start | bytes 1671176 | tf_op jit(solution)/shard_map/ppermute | solution.py:45
  90.4 27.0 %collective-permute-start.15 = (f16[2,304,896]{2,1,0:T(8,128)(2,1)}, f16[2,304,896]{2,1,0:T(8,128)(2,1)S(1)}, u32[]{:S(2)}, u32[]{:S(2)}) collective-permute-start(f16[2,304,896]{2,1,0:T(8,128)(2,1)} %multiply_convert_fusion), channel_id=1, source_target_pairs={{0,96},{8,40},{32,0},{40,72},{64,32},{72,104},{96,64},{104,8},{16,... | collective-permute-start | bytes 3268616 | tf_op jit(solution)/shard_map/ppermute | solution.py:45
  94.5 22.8 %collective-permute-start.14 = (f16[2,304,896]{2,1,0:T(8,128)(2,1)}, f16[2,304,896]{2,1,0:T(8,128)(2,1)}, u32[]{:S(2)}, u32[]{:S(2)}) collective-permute-start(f16[2,304,896]{2,1,0:T(8,128)(2,1)} %multiply_convert_fusion.1), channel_id=1, source_target_pairs={{0,32},{8,104},{32,64},{40,8},{64,96},{72,40},{96,0},{104,72},{16,... | collective-permute-start | bytes 3268616 | tf_op jit(solution)/shard_map/ppermute | solution.py:45
  95.4 17.2 %collective-permute-start.16 = (f32[4,1,80,512]{3,2,1,0:T(8,128)}, f32[4,1,80,512]{3,2,1,0:T(8,128)}, u32[]{:S(2)}, u32[]{:S(2)}) collective-permute-start(f32[4,1,80,512]{3,2,1,0:T(8,128)} %constant_dynamic-slice_fusion), channel_id=1, source_target_pairs={{0,1},{8,9},{32,33},{40,41},{64,65},{72,73},{96,97},{104,105},{16,... | collective-permute-start | bytes 1966088 | tf_op jit(solution)/shard_map/ppermute | solution.py:45
  96.0 16.7 %collective-permute-start.17 = (bf16[272,1024]{1,0:T(8,128)(2,1)S(1)}, bf16[272,1024]{1,0:T(8,128)(2,1)S(1)}, u32[]{:S(2)}, u32[]{:S(2)}) collective-permute-start(bf16[272,1024]{1,0:T(8,128)(2,1)S(1)} %collective-permute-done.13.refs_6_), channel_id=1, source_target_pairs={{0,8},{8,0},{32,40},{40,32},{64,72},{72,64},{96,104},{104,96},{16,... | collective-permute-start | bytes 1671176 | tf_op jit(solution)/shard_map/ppermute | solution.py:45
  121.0 17.2 %collective-permute-start.18 = (f16[2,304,896]{2,1,0:T(8,128)(2,1)}, f16[2,304,896]{2,1,0:T(8,128)(2,1)}, u32[]{:S(2)}, u32[]{:S(2)}) collective-permute-start(f16[2,304,896]{2,1,0:T(8,128)(2,1)} %add_convert_fusion), channel_id=1, source_target_pairs={{0,32},{8,104},{32,64},{40,8},{64,96},{72,40},{96,0},{104,72},{16,... | collective-permute-start | bytes 3268616 | tf_op jit(solution)/shard_map/ppermute | solution.py:45
  123.5 14.6 %collective-permute-start.19 = (f32[80,512]{1,0:T(8,128)S(1)}, f32[80,512]{1,0:T(8,128)S(1)}, u32[]{:S(2)}, u32[]{:S(2)}) collective-permute-start(f32[80,512]{1,0:T(8,128)S(1)} %get-tuple-element.148), channel_id=1, source_target_pairs={{0,2},{8,10},{32,34},{40,42},{64,66},{72,74},{96,98},{104,106},{16... | collective-permute-start | bytes 491528 | tf_op jit(solution)/shard_map/ppermute | solution.py:45
  124.4 13.7 %collective-permute-start.20 = (f32[80,512]{1,0:T(8,128)S(1)}, f32[80,512]{1,0:T(8,128)S(1)}, u32[]{:S(2)}, u32[]{:S(2)}) collective-permute-start(f32[80,512]{1,0:T(8,128)S(1)} %get-tuple-element.147), channel_id=1, source_target_pairs={{0,4},{8,12},{32,36},{40,44},{64,68},{72,76},{96,100},{104,108},{1... | collective-permute-start | bytes 491528 | tf_op jit(solution)/shard_map/ppermute | solution.py:45
  126.8 11.4 %collective-permute-start.21 = (f32[80,512]{1,0:T(8,128)S(1)}, f32[80,512]{1,0:T(8,128)S(1)}, u32[]{:S(2)}, u32[]{:S(2)}) collective-permute-start(f32[80,512]{1,0:T(8,128)S(1)} %get-tuple-element.146), channel_id=1, source_target_pairs={{0,6},{8,14},{32,38},{40,46},{64,70},{72,78},{96,102},{104,110},{1... | collective-permute-start | bytes 491528 | tf_op jit(solution)/shard_map/ppermute | solution.py:45
  141.6 22.2 %collective-permute-start.23 = (f16[2,144,1168]{2,1,0:T(8,128)(2,1)}, f16[2,144,1168]{2,1,0:T(8,128)(2,1)}, u32[]{:S(2)}, u32[]{:S(2)}) collective-permute-start(f16[2,144,1168]{2,1,0:T(8,128)(2,1)} %get-tuple-element.153), channel_id=1, source_target_pairs={{0,32},{8,104},{32,64},{40,8},{64,96},{72,40},{96,0},{104,72},{16,... | collective-permute-start | bytes 2018312 | tf_op jit(solution)/shard_map/ppermute | solution.py:45
  143.5 20.4 %collective-permute-start.24 = (f16[2,144,1168]{2,1,0:T(8,128)(2,1)}, f16[2,144,1168]{2,1,0:T(8,128)(2,1)}, u32[]{:S(2)}, u32[]{:S(2)}) collective-permute-start(f16[2,144,1168]{2,1,0:T(8,128)(2,1)} %get-tuple-element.152), channel_id=1, source_target_pairs={{0,96},{8,40},{32,0},{40,72},{64,32},{72,104},{96,64},{104,8},{16,... | collective-permute-start | bytes 2018312 | tf_op jit(solution)/shard_map/ppermute | solution.py:45
  146.7 17.1 %collective-permute-start.22 = (f16[304,896]{1,0:T(8,128)(2,1)S(1)}, f16[304,896]{1,0:T(8,128)(2,1)S(1)}, u32[]{:S(2)}, u32[]{:S(2)}) collective-permute-start(f16[304,896]{1,0:T(8,128)(2,1)S(1)} %fusion.7), channel_id=1, source_target_pairs={{0,16},{8,24},{32,48},{40,56},{64,80},{72,88},{96,112},{104,120},{... | collective-permute-start | bytes 1634312 | tf_op jit(solution)/shard_map/ppermute | solution.py:45
  147.9 15.9 %collective-permute-start.25 = (f32[80,512]{1,0:T(8,128)S(1)}, f32[80,512]{1,0:T(8,128)S(1)}, u32[]{:S(2)}, u32[]{:S(2)}) collective-permute-start(f32[80,512]{1,0:T(8,128)S(1)} %add_add_fusion), channel_id=1, source_target_pairs={{0,1},{8,9},{32,33},{40,41},{64,65},{72,73},{96,97},{104,105},{16,... | collective-permute-start | bytes 491528 | tf_op jit(solution)/shard_map/ppermute | solution.py:45
  166.5 17.0 %collective-permute-start.27 = (f16[2,144,1168]{2,1,0:T(8,128)(2,1)}, f16[2,144,1168]{2,1,0:T(8,128)(2,1)}, u32[]{:S(2)}, u32[]{:S(2)}) collective-permute-start(f16[2,144,1168]{2,1,0:T(8,128)(2,1)} %add_convert_fusion.1), channel_id=1, source_target_pairs={{0,32},{8,104},{32,64},{40,8},{64,96},{72,40},{96,0},{104,72},{16,... | collective-permute-start | bytes 2018312 | tf_op jit(solution)/shard_map/ppermute | solution.py:45
  167.7 15.7 %collective-permute-start.26 = (f16[304,896]{1,0:T(8,128)(2,1)}, f16[304,896]{1,0:T(8,128)(2,1)}, u32[]{:S(2)}, u32[]{:S(2)}) collective-permute-start(f16[304,896]{1,0:T(8,128)(2,1)} %fusion.4), channel_id=1, source_target_pairs={{16,1},{24,9},{48,33},{56,41},{80,65},{88,73},{112,97},{120,105},{... | collective-permute-start | bytes 1634312 | tf_op jit(solution)/shard_map/ppermute | solution.py:45
  185.8 18.3 %collective-permute-start.29 = (f16[144,1168]{1,0:T(8,128)(2,1)S(1)}, f16[144,1168]{1,0:T(8,128)(2,1)S(1)}, u32[]{:S(2)}, u32[]{:S(2)}) collective-permute-start(f16[144,1168]{1,0:T(8,128)(2,1)S(1)} %fusion.5), channel_id=1, source_target_pairs={{16,1},{24,9},{48,33},{56,41},{80,65},{88,73},{112,97},{120,105},{... | collective-permute-start | bytes 1009160 | tf_op jit(solution)/shard_map/ppermute | solution.py:45
  (32 other events, 201.7 us)
Sparse Core Ops, SparseCore 0:
  14.3 57.0 all-gather.7
  73.1 53.1 all-gather.9
  171.6 25.2 all-gather.5

commit v5 on v4

--- a/solution.py
+++ b/solution.py
@@ -177,12 +177,6 @@
     return 32768.0 / most, most / (32768.0 * tokens_total)
 
 
-def far(p):
-    second, third = p.pop("far")
-    a = send((second * p["down"]).astype(HALF), Z_ALONG)
-    return {**p, "a": a, "c": send((third * p["down"]).astype(HALF), Z_AGAINST)}
-
-
 def along(p):
     b = p["close"][1] * p["down"] + p["a"].astype(jnp.float32)
     return {**p, "a": None, "b": send(b.astype(HALF), Z_ALONG)}
@@ -193,15 +187,8 @@
     return p["close"][0] * p["down"] + b + c
 
 
-def near(p, stays):
-    total = summed(p)
-    value = jnp.where(stays, total[1], total[0])
-    return {"total": total, "n": send(value.astype(HALF), Y_PARTNER)}
-
-
-def cross(p):
-    value = p["total"][1] + p["n"].astype(jnp.float32)
-    return {**p, "m": send(value.astype(HALF), Y_MIDDLE)}
+def crossing(p):
+    return (p["total"][1] + p["n"].astype(jnp.float32)).astype(HALF)
 
 
 def crossed(p, stays):
@@ -302,33 +289,39 @@
 
     width, grad_width = activations.shape[1], grads.shape[0]
     down = jnp.where(jnp.arange(width + grad_width) < width, act_down, grad_down)
-    one, two = {"down": act_down}, {"down": down}
     stays = y_lo == y_hi
-    one["far"] = products(source, (2, 3), rows_1, FIRST, columns)
+    second, third = products(source, (2, 3), rows_1, FIRST, columns)
     grad_other = send(grads, OTHER_COLUMN)
-    one, grad_other = lax.optimization_barrier((one, grad_other))
-
-    one = far(one)
+    a = send((second * act_down).astype(HALF), Z_ALONG)
+    c = send((third * act_down).astype(HALF), Z_AGAINST)
+    close = products(source, (0, 1), rows_1, FIRST, columns)
     part = give(part, y_hi, OTHER_COLUMN, 1)
-    one["close"] = products(source, (0, 1), rows_1, FIRST, columns)
     grad_columns = [grads, grad_sibling, grad_other, send(grad_other, SIBLING)]
-    one, part, grad_columns = lax.optimization_barrier((one, part, grad_columns))
-
-    one = along(one)
+    message = (close[1] * act_down + a.astype(jnp.float32)).astype(HALF)
+    message, rows_2, part = lax.optimization_barrier((message, rows_2, part))
+    one = {"close": close, "down": act_down, "b": send(message, Z_ALONG), "c": c}
+
+    second, third = products(source, (2, 3), rows_2, n_2, columns, grad_columns)
     part = scatter_x(add(*part, y_hi, 1), x)
-    two["far"] = products(source, (2, 3), rows_2, n_2, columns, grad_columns)
-    one, two, part = lax.optimization_barrier((one, two, part))
-
+    total = summed(one)
+    messages = (
+        (second * down).astype(HALF),
+        (third * down).astype(HALF),
+        jnp.where(stays, total[1], total[0]).astype(HALF),
+    )
+    messages, rows_2 = lax.optimization_barrier((messages, rows_2))
+    a, c = send(messages[0], Z_ALONG), send(messages[1], Z_AGAINST)
+    one = {"total": total, "n": send(messages[2], Y_PARTNER)}
+    two = {"close": products(source, (0, 1), rows_2, n_2, columns, grad_columns)}
+    two = {**two, "down": down, "a": a, "c": c}
     part = sum(part)
     part = (part, send(part, OTHER_COLUMN))
-    one, two = near(one, stays), far(two)
-    two["close"] = products(source, (0, 1), rows_2, n_2, columns, grad_columns)
-    one, two, part = lax.optimization_barrier((one, two, part))
-
+
+    message = crossing(one)
+    message, two = lax.optimization_barrier((message, two))
+    one["m"] = send(message, Y_MIDDLE)
+    two = along(two)
     part = round_x(jnp.where(y_hi == 0, jnp.stack(part), jnp.stack(part[::-1])))
-    one = cross(one)
-    two = along(two)
-    one, two = lax.optimization_barrier((one, two))
 
     two = across(two, stays)
     act_cov = jnp.concatenate(

time: 220 us -> 218 us (level); the launches traced: 217 us -> 217 us
  waiting for transfers between devices: 79 us -> 76.1 us
    ppermute x30, waiting for transfers between devices: 77.1 us -> 57.7 us  [send(): return lax.ppermute(value, AXES, to)]
    all_gather x3, waiting for transfers between devices: 1.87 us -> 18.4 us  [round_x(): return lax.all_gather(rows, AXES, axis_index_groups=X_RINGS)]
    convert_element_type x5 -> x6, other arithmetic: 8.64 us -> 13.2 us  [the longest x1 3.33 us: on_device(): message = (close[1] * act_down + a.astype(jnp.float32)).astype(HALF)]
    convert_element_type x2 -> x1, other arithmetic: 6.35 us -> 2.25 us  [along(): return {**p, 'a': None, 'b': send(b.astype(HALF), Z_ALONG)}]
  transfers between devices with their start and end apart: 33 -> 33, of which waited for: 16 -> 15; matrix products, arithmetic and copies ran while one was open for 13% -> 17% of each run, Pallas kernels for 19% -> 19%
where the time goes in v5:
time: 218 us; the launch traced here: 217 us
  waiting for transfers between devices  76.1 us (35%)
  Pallas kernels  41.3 us (19%)
  starting transfers between devices  38.4 us (18%)
  other arithmetic  30.8 us (14%)
  between operations  16.9 us (8%)
  local copies, waits for them, and re-layouts  12.9 us (6%)
    ppermute x30, waiting for transfers between devices, send(): return lax.ppermute(value, AXES, to)  57.7 us
    pallas_call x4, Pallas kernels, products(): pl.pallas_call(functools.partial(product_kernel, kinds, slots), out_shape...  40.6 us
    ppermute x30, starting transfers between devices, send(): return lax.ppermute(value, AXES, to)  38.3 us
    all_gather x3, waiting for transfers between devices, round_x(): return lax.all_gather(rows, AXES, axis_index_groups=X_RINGS)  18.4 us
  transfers between devices with their start and end apart: 33, of which 15 were waited for; matrix products, arithmetic and copies ran while one was open for 17% of the time, Pallas kernels for 19%

profile of v5, /device:TPU:16, one launch (start us, length us, event | category | flops | bytes accessed | tf_op | source)
XLA Modules:
  0.0 217.3 jit_solution(14227827596937729016)
XLA Ops:
  9.7 2.4 %collective-permute-done.7 = bf16[448,1024]{1,0:T(8,128)(2,1)S(1)} collective-permute-done((bf16[448,1024]{1,0:T(8,128)(2,1)S(1)}, bf16[448,1024]{1,0:T(8,128)(2,1)S(1)}, u32[]{:S(2)}, u32[]{:S(2)}) %collective-permute-start.7) | collective-permute-done | bytes 917536 | tf_op jit(solution)/shard_map/ppermute | solution.py:45
  24.4 4.0 %collective-permute-start.2 = (f32[8,128]{1,0:T(8,128)S(1)}, f32[8,128]{1,0:T(8,128)S(1)}, u32[]{:S(2)}, u32[]{:S(2)}) collective-permute-start(f32[8,128]{1,0:T(8,128)S(1)} %fusion.16), channel_id=1, source_target_pairs={{0,64},{8,72},{32,96},{40,104},{64,0},{72,8},{96,32},{104,40},{16,... | collective-permute-start | bytes 12296 | tf_op jit(solution)/shard_map/ppermute | solution.py:45
  33.6 3.0 %collective-permute-start.4 = (f32[8,128]{1,0:T(8,128)S(1)}, f32[8,128]{1,0:T(8,128)S(1)}, u32[]{:S(2)}, u32[]{:S(2)}) collective-permute-start(f32[8,128]{1,0:T(8,128)S(1)} %max.32), channel_id=1, source_target_pairs={{0,4},{8,12},{32,36},{40,44},{64,68},{72,76},{96,100},{104,108},{1... | collective-permute-start | bytes 12296 | tf_op jit(solution)/shard_map/ppermute | solution.py:45
  41.0 17.7 %collective-permute-done.5.refs_2_ = bf16[1024,896]{1,0:T(8,128)(2,1)} collective-permute-done((bf16[1024,896]{1,0:T(8,128)(2,1)S(1)}, bf16[1024,896]{1,0:T(8,128)(2,1)}, u32[]{:S(2)}, u32[]{:S(2)}) %collective-permute-start.5) | collective-permute-done | bytes 1835040 | tf_op jit(solution)/shard_map/ppermute | solution.py:45
  60.2 2.3 %collective-permute-done.11 = f32[8,128]{1,0:T(8,128)S(1)} collective-permute-done((f32[8,128]{1,0:T(8,128)S(1)}, f32[8,128]{1,0:T(8,128)S(1)}, u32[]{:S(2)}, u32[]{:S(2)}) %collective-permute-start.11) | collective-permute-done | bytes 4128 | tf_op jit(solution)/shard_map/ppermute | solution.py:45
  63.4 4.2 %collective-permute-done.12 = f32[8,128]{1,0:T(8,128)S(1)} collective-permute-done((f32[8,128]{1,0:T(8,128)S(1)}, f32[8,128]{1,0:T(8,128)S(1)}, u32[]{:S(2)}, u32[]{:S(2)}) %collective-permute-start.12) | collective-permute-done | bytes 4128 | tf_op jit(solution)/shard_map/ppermute | solution.py:45
  71.4 10.5 %shard_map.95 = (f32[2,304,896]{2,1,0:T(8,128)}, f32[2,304,896]{2,1,0:T(8,128)}) custom-call(s32[4]{0:T(128)} %pad_add_fusion.source, bf16[4,2,304,1024]{3,2,1,0:T(8,128)(2,1)} %bitcast.71, bf16[1024,896]{1,0:T(8,128)(2,1)} %refs_0_.3, bf16[1024,896]{1,0:T(8,128)(2,1)} %collective-permute-done.6.refs_1_, bf16[1024,896]{1,0:T(8,128)(2,1)} %collective-permute-done.5.refs_2_, ...), custom_call_target="tpu_custom_call" | custom-call | flops 2231369728 | bytes 2490368 | tf_op jit(solution)/shard_map/pallas_call | solution.py:152
  81.9 3.1 %multiply_convert_fusion.1 = f16[2,304,896]{2,1,0:T(8,128)(2,1)} fusion(f32[2,304,896]{2,1,0:T(8,128)} %get-tuple-element.63, f32[]{:T(128)} %bitcast.14), kind=kLoop, calls=%fused_computation.3 | loop fusion | flops 1089536 | bytes 3268612 | tf_op jit(solution)/shard_map/convert_element_type | solution.py:295
  88.1 2.9 %collective-permute-start.14 = (f32[4,1,80,512]{3,2,1,0:T(8,128)}, f32[4,1,80,512]{3,2,1,0:T(8,128)S(1)}, u32[]{:S(2)}, u32[]{:S(2)}) collective-permute-start(f32[4,1,80,512]{3,2,1,0:T(8,128)} %constant_dynamic-slice_fusion), channel_id=1, source_target_pairs={{0,1},{8,9},{32,33},{40,41},{64,65},{72,73},{96,97},{104,105},{16,... | collective-permute-start | bytes 1966088 | tf_op jit(solution)/shard_map/ppermute | solution.py:45
  91.0 2.8 %multiply_convert_fusion = f16[2,304,896]{2,1,0:T(8,128)(2,1)} fusion(f32[2,304,896]{2,1,0:T(8,128)} %get-tuple-element.67, f32[]{:T(128)} %bitcast.14), kind=kLoop, calls=%fused_computation.1 | loop fusion | flops 1089536 | bytes 3268612 | tf_op jit(solution)/shard_map/convert_element_type | solution.py:296
  95.7 10.5 %shard_map.94 = (f32[2,304,896]{2,1,0:T(8,128)}, f32[2,304,896]{2,1,0:T(8,128)}) custom-call(s32[4]{0:T(128)} %pad_add_fusion.source, bf16[4,2,304,1024]{3,2,1,0:T(8,128)(2,1)} %bitcast.72, bf16[1024,896]{1,0:T(8,128)(2,1)} %refs_0_.3, bf16[1024,896]{1,0:T(8,128)(2,1)} %collective-permute-done.6.refs_1_, bf16[1024,896]{1,0:T(8,128)(2,1)} %collective-permute-done.5.refs_2_, ...), custom_call_target="tpu_custom_call" | custom-call | flops 2231369728 | bytes 2490368 | tf_op jit(solution)/shard_map/pallas_call | solution.py:152
  106.5 3.3 %add_convert_fusion = f16[2,304,896]{2,1,0:T(8,128)(2,1)} fusion(f16[2,304,896]{2,1,0:T(8,128)(2,1)} %collective-permute-done.13, f32[2,304,896]{2,1,0:T(8,128)} %get-tuple-element.62, f32[]{:T(128)} %bitcast.14), kind=kLoop, calls=%fused_computation.2 | loop fusion | flops 2179072 | bytes 4358148 | tf_op jit(solution)/shard_map/convert_element_type | solution.py:300
  109.8 16.5 %all-gather.10.cloned.1.call-done = bf16[8,288,1024]{2,1,0:T(8,128)(2,1)} async-done(((bf16[2,288,1024]{2,1,0:T(8,128)(2,1)}), bf16[8,288,1024]{2,1,0:T(8,128)(2,1)}) %all-gather.10.cloned.1.call-update) | async-done | bytes 4718608 | tf_op jit(solution)/shard_map/all_gather | solution.py:233
  134.9 9.8 %shard_map.96 = (f32[2,144,1168]{2,1,0:T(8,128)}, f32[2,144,1168]{2,1,0:T(8,128)}) custom-call(s32[4]{0:T(128)} %pad_add_fusion.source, bf16[4,2,288,1024]{3,2,1,0:T(8,128)(2,1)} %bitcast.73, bf16[1024,896]{1,0:T(8,128)(2,1)} %refs_0_.3, bf16[1024,896]{1,0:T(8,128)(2,1)} %collective-permute-done.6.refs_1_, bf16[1024,896]{1,0:T(8,128)(2,1)} %collective-permute-done.5.refs_2_, ...), custom_call_target="tpu_custom_call" | custom-call | flops 1377828864 | bytes 1179648 | tf_op jit(solution)/shard_map/pallas_call | solution.py:152
  145.3 2.9 %multiply_convert_fusion.2 = (f16[2,144,1168]{2,1,0:T(8,128)(2,1)S(1)}, f16[2,144,1168]{2,1,0:T(8,128)(2,1)}) fusion(f32[2,144,1168]{2,1,0:T(8,128)} %get-tuple-element.73, f32[1168]{0:T(1024)S(1)} %fusion.8, f32[2,144,1168]{2,1,0:T(8,128)} %get-tuple-element.71), kind=kLoop, calls=%fused_computation.8 | loop fusion | flops 1345536 | bytes 4041280 | tf_op jit(solution)/shard_map/convert_element_type | solution.py:309
  148.3 4.3 %collective-permute-done.29 = f32[80,512]{1,0:T(8,128)S(1)} collective-permute-done((f32[80,512]{1,0:T(8,128)S(1)}, f32[80,512]{1,0:T(8,128)S(1)}, u32[]{:S(2)}, u32[]{:S(2)}) %collective-permute-start.29) | collective-permute-done | bytes 163872 | tf_op jit(solution)/shard_map/ppermute | solution.py:45
  153.3 2.6 %convert_add_fusion = f32[2,304,896]{2,1,0:T(8,128)S(1)} fusion(f16[2,304,896]{2,1,0:T(8,128)(2,1)} %collective-permute-done.16, f16[2,304,896]{2,1,0:T(8,128)(2,1)} %collective-permute-done.15, f32[2,304,896]{2,1,0:T(8,128)} %get-tuple-element.60, f32[]{:T(128)} %bitcast.14), kind=kLoop, calls=%fused_computation | loop fusion | flops 2723840 | bytes 6537220 | tf_op jit(solution)/shard_map/add | solution.py:187
  158.0 2.6 %collective-permute-start.21 = (f16[2,144,1168]{2,1,0:T(8,128)(2,1)S(1)}, f16[2,144,1168]{2,1,0:T(8,128)(2,1)}, u32[]{:S(2)}, u32[]{:S(2)}) collective-permute-start(f16[2,144,1168]{2,1,0:T(8,128)(2,1)S(1)} %get-tuple-element.76), channel_id=1, source_target_pairs={{0,96},{8,40},{32,0},{40,72},{64,32},{72,104},{96,64},{104,8},{16,... | collective-permute-start | bytes 2018312 | tf_op jit(solution)/shard_map/ppermute | solution.py:45
  160.6 9.9 %shard_map.97 = (f32[2,144,1168]{2,1,0:T(8,128)}, f32[2,144,1168]{2,1,0:T(8,128)}) custom-call(s32[4]{0:T(128)} %pad_add_fusion.source, bf16[4,2,288,1024]{3,2,1,0:T(8,128)(2,1)} %bitcast.74, bf16[1024,896]{1,0:T(8,128)(2,1)} %refs_0_.3, bf16[1024,896]{1,0:T(8,128)(2,1)} %collective-permute-done.6.refs_1_, bf16[1024,896]{1,0:T(8,128)(2,1)} %collective-permute-done.5.refs_2_, ...), custom_call_target="tpu_custom_call" | custom-call | flops 1377828864 | bytes 1179648 | tf_op jit(solution)/shard_map/pallas_call | solution.py:152
  171.4 4.6 %collective-permute-done.20 = f16[2,144,1168]{2,1,0:T(8,128)(2,1)} collective-permute-done((f16[2,144,1168]{2,1,0:T(8,128)(2,1)}, f16[2,144,1168]{2,1,0:T(8,128)(2,1)}, u32[]{:S(2)}, u32[]{:S(2)}) %collective-permute-start.20) | collective-permute-done | bytes 672800 | tf_op jit(solution)/shard_map/ppermute | solution.py:45
  183.1 8.1 %collective-permute-done.23 = f16[2,144,1168]{2,1,0:T(8,128)(2,1)S(1)} collective-permute-done((f16[2,144,1168]{2,1,0:T(8,128)(2,1)}, f16[2,144,1168]{2,1,0:T(8,128)(2,1)S(1)}, u32[]{:S(2)}, u32[]{:S(2)}) %collective-permute-start.23) | collective-permute-done | bytes 672800 | tf_op jit(solution)/shard_map/ppermute | solution.py:45
  193.7 2.4 %collective-permute-start.25 = (f16[144,1168]{1,0:T(8,128)(2,1)S(1)}, f16[144,1168]{1,0:T(8,128)(2,1)S(1)}, u32[]{:S(2)}, u32[]{:S(2)}) collective-permute-start(f16[144,1168]{1,0:T(8,128)(2,1)S(1)} %fusion.4), channel_id=1, source_target_pairs={{16,1},{24,9},{48,33},{56,41},{80,65},{88,73},{112,97},{120,105},{... | collective-permute-start | bytes 1009160 | tf_op jit(solution)/shard_map/ppermute | solution.py:45
  199.1 2.9 %collective-permute-done.24 = f16[144,1168]{1,0:T(8,128)(2,1)S(1)} collective-permute-done((f16[144,1168]{1,0:T(8,128)(2,1)S(1)}, f16[144,1168]{1,0:T(8,128)(2,1)S(1)}, u32[]{:S(2)}, u32[]{:S(2)}) %collective-permute-start.24) | collective-permute-done | bytes 336416 | tf_op jit(solution)/shard_map/ppermute | solution.py:45
  202.0 6.7 %collective-permute-done.25 = f16[144,1168]{1,0:T(8,128)(2,1)S(1)} collective-permute-done((f16[144,1168]{1,0:T(8,128)(2,1)S(1)}, f16[144,1168]{1,0:T(8,128)(2,1)S(1)}, u32[]{:S(2)}, u32[]{:S(2)}) %collective-permute-start.25) | collective-permute-done | bytes 336416 | tf_op jit(solution)/shard_map/ppermute | solution.py:45
  (135 shorter events, 60.4 us)
Async XLA Ops:
  7.2 64.3 %all-gather.8.cloned.1.call-start = ((), (), s32[]{:S(2)}) async-start(), calls=%async_computation.1 | async-start | bytes 6225920 | tf_op jit(solution)/shard_map/all_gather | solution.py:233
  14.2 112.1 %all-gather.10.cloned.1.call-start = ((), (), s32[]{:S(2)}) async-start(), calls=%async_computation.2 | async-start | bytes 5898240 | tf_op jit(solution)/shard_map/all_gather | solution.py:233
  15.0 43.7 %collective-permute-start.5 = (bf16[1024,896]{1,0:T(8,128)(2,1)S(1)}, bf16[1024,896]{1,0:T(8,128)(2,1)}, u32[]{:S(2)}, u32[]{:S(2)}) collective-permute-start(bf16[1024,896]{1,0:T(8,128)(2,1)S(1)} %copy-done.3), channel_id=1, source_target_pairs={{0,1},{8,9},{32,33},{40,41},{64,65},{72,73},{96,97},{104,105},{16,... | collective-permute-start | bytes 5505032 | tf_op jit(solution)/shard_map/ppermute | solution.py:45
  15.2 43.4 %collective-permute-start.6 = (bf16[1024,896]{1,0:T(8,128)(2,1)S(1)}, bf16[1024,896]{1,0:T(8,128)(2,1)}, u32[]{:S(2)}, u32[]{:S(2)}) collective-permute-start(bf16[1024,896]{1,0:T(8,128)(2,1)S(1)} %copy-done.3), channel_id=1, source_target_pairs={{0,8},{8,0},{32,40},{40,32},{64,72},{72,64},{96,104},{104,96},{16,... | collective-permute-start | bytes 5505032 | tf_op jit(solution)/shard_map/ppermute | solution.py:45
  18.8 20.0 %collective-permute-start.8 = (bf16[132,1024]{1,0:T(8,128)(2,1)S(1)}, bf16[132,1024]{1,0:T(8,128)(2,1)S(1)}, u32[]{:S(2)}, u32[]{:S(2)}) collective-permute-start(bf16[132,1024]{1,0:T(8,128)(2,1)S(1)} %get-tuple-element.94), channel_id=1, source_target_pairs={{0,8},{8,0},{32,40},{40,32},{64,72},{72,64},{96,104},{104,96},{16,... | collective-permute-start | bytes 811016 | tf_op jit(solution)/shard_map/ppermute | solution.py:45
  20.1 20.9 %collective-permute-start.9 = (bf16[272,1024]{1,0:T(8,128)(2,1)S(1)}, bf16[272,1024]{1,0:T(8,128)(2,1)}, u32[]{:S(2)}, u32[]{:S(2)}) collective-permute-start(bf16[272,1024]{1,0:T(8,128)(2,1)S(1)} %pad.12.refs_4_), channel_id=1, source_target_pairs={{0,8},{8,0},{32,40},{40,32},{64,72},{72,64},{96,104},{104,96},{16,... | collective-permute-start | bytes 1671176 | tf_op jit(solution)/shard_map/ppermute | solution.py:45
  58.7 122.1 %all-gather.6.cloned.1.call-start = ((), (), s32[]{:S(2)}) async-start(), calls=%async_computation | async-start | bytes 1638400 | tf_op jit(solution)/shard_map/all_gather | solution.py:233
  58.7 10.8 %collective-permute-start.10 = (bf16[1024,896]{1,0:T(8,128)(2,1)}, bf16[1024,896]{1,0:T(8,128)(2,1)S(1)}, u32[]{:S(2)}, u32[]{:S(2)}) collective-permute-start(bf16[1024,896]{1,0:T(8,128)(2,1)} %collective-permute-done.5.refs_2_), channel_id=1, source_target_pairs={{0,8},{8,0},{32,40},{40,32},{64,72},{72,64},{96,104},{104,96},{16,... | collective-permute-start | bytes 5505032 | tf_op jit(solution)/shard_map/ppermute | solution.py:45
  85.0 21.4 %collective-permute-start.13 = (f16[2,304,896]{2,1,0:T(8,128)(2,1)}, f16[2,304,896]{2,1,0:T(8,128)(2,1)}, u32[]{:S(2)}, u32[]{:S(2)}) collective-permute-start(f16[2,304,896]{2,1,0:T(8,128)(2,1)} %multiply_convert_fusion.1), channel_id=1, source_target_pairs={{0,32},{8,104},{32,64},{40,8},{64,96},{72,40},{96,0},{104,72},{16,... | collective-permute-start | bytes 3268616 | tf_op jit(solution)/shard_map/ppermute | solution.py:45
  86.6 19.6 %collective-permute-start.17 = (bf16[272,1024]{1,0:T(8,128)(2,1)S(1)}, bf16[272,1024]{1,0:T(8,128)(2,1)S(1)}, u32[]{:S(2)}, u32[]{:S(2)}) collective-permute-start(bf16[272,1024]{1,0:T(8,128)(2,1)S(1)} %pad.12.refs_4_), channel_id=1, source_target_pairs={{0,1},{8,9},{32,33},{40,41},{64,65},{72,73},{96,97},{104,105},{16,... | collective-permute-start | bytes 1671176 | tf_op jit(solution)/shard_map/ppermute | solution.py:45
  88.1 38.2 %collective-permute-start.14 = (f32[4,1,80,512]{3,2,1,0:T(8,128)}, f32[4,1,80,512]{3,2,1,0:T(8,128)S(1)}, u32[]{:S(2)}, u32[]{:S(2)}) collective-permute-start(f32[4,1,80,512]{3,2,1,0:T(8,128)} %constant_dynamic-slice_fusion), channel_id=1, source_target_pairs={{0,1},{8,9},{32,33},{40,41},{64,65},{72,73},{96,97},{104,105},{16,... | collective-permute-start | bytes 1966088 | tf_op jit(solution)/shard_map/ppermute | solution.py:45
  93.9 59.5 %collective-permute-start.16 = (f16[2,304,896]{2,1,0:T(8,128)(2,1)}, f16[2,304,896]{2,1,0:T(8,128)(2,1)}, u32[]{:S(2)}, u32[]{:S(2)}) collective-permute-start(f16[2,304,896]{2,1,0:T(8,128)(2,1)} %multiply_convert_fusion), channel_id=1, source_target_pairs={{0,96},{8,40},{32,0},{40,72},{64,32},{72,104},{96,64},{104,8},{16,... | collective-permute-start | bytes 3268616 | tf_op jit(solution)/shard_map/ppermute | solution.py:45
  106.2 27.0 %collective-permute-start.18 = (bf16[272,1024]{1,0:T(8,128)(2,1)S(1)}, bf16[272,1024]{1,0:T(8,128)(2,1)S(1)}, u32[]{:S(2)}, u32[]{:S(2)}) collective-permute-start(bf16[272,1024]{1,0:T(8,128)(2,1)S(1)} %collective-permute-done.17.refs_6_), channel_id=1, source_target_pairs={{0,8},{8,0},{32,40},{40,32},{64,72},{72,64},{96,104},{104,96},{16,... | collective-permute-start | bytes 1671176 | tf_op jit(solution)/shard_map/ppermute | solution.py:45
  128.4 16.3 %collective-permute-start.26 = (f32[80,512]{1,0:T(8,128)S(1)}, f32[80,512]{1,0:T(8,128)S(1)}, u32[]{:S(2)}, u32[]{:S(2)}) collective-permute-start(f32[80,512]{1,0:T(8,128)S(1)} %get-tuple-element.90), channel_id=1, source_target_pairs={{0,2},{8,10},{32,34},{40,42},{64,66},{72,74},{96,98},{104,106},{16... | collective-permute-start | bytes 491528 | tf_op jit(solution)/shard_map/ppermute | solution.py:45
  129.4 15.3 %collective-permute-start.27 = (f32[80,512]{1,0:T(8,128)S(1)}, f32[80,512]{1,0:T(8,128)S(1)}, u32[]{:S(2)}, u32[]{:S(2)}) collective-permute-start(f32[80,512]{1,0:T(8,128)S(1)} %get-tuple-element.92), channel_id=1, source_target_pairs={{0,4},{8,12},{32,36},{40,44},{64,68},{72,76},{96,100},{104,108},{1... | collective-permute-start | bytes 491528 | tf_op jit(solution)/shard_map/ppermute | solution.py:45
  131.1 13.5 %collective-permute-start.28 = (f32[80,512]{1,0:T(8,128)S(1)}, f32[80,512]{1,0:T(8,128)S(1)}, u32[]{:S(2)}, u32[]{:S(2)}) collective-permute-start(f32[80,512]{1,0:T(8,128)S(1)} %get-tuple-element.91), channel_id=1, source_target_pairs={{0,6},{8,14},{32,38},{40,46},{64,70},{72,78},{96,102},{104,110},{1... | collective-permute-start | bytes 491528 | tf_op jit(solution)/shard_map/ppermute | solution.py:45
  133.2 20.1 %collective-permute-start.15 = (f16[2,304,896]{2,1,0:T(8,128)(2,1)}, f16[2,304,896]{2,1,0:T(8,128)(2,1)}, u32[]{:S(2)}, u32[]{:S(2)}) collective-permute-start(f16[2,304,896]{2,1,0:T(8,128)(2,1)} %add_convert_fusion), channel_id=1, source_target_pairs={{0,32},{8,104},{32,64},{40,8},{64,96},{72,40},{96,0},{104,72},{16,... | collective-permute-start | bytes 3268616 | tf_op jit(solution)/shard_map/ppermute | solution.py:45
  156.1 14.4 %collective-permute-start.19 = (f16[304,896]{1,0:T(8,128)(2,1)S(1)}, f16[304,896]{1,0:T(8,128)(2,1)S(1)}, u32[]{:S(2)}, u32[]{:S(2)}) collective-permute-start(f16[304,896]{1,0:T(8,128)(2,1)S(1)} %select_convert_fusion), channel_id=1, source_target_pairs={{0,16},{8,24},{32,48},{40,56},{64,80},{72,88},{96,112},{104,120},{... | collective-permute-start | bytes 1634312 | tf_op jit(solution)/shard_map/ppermute | solution.py:45
  157.4 18.7 %collective-permute-start.20 = (f16[2,144,1168]{2,1,0:T(8,128)(2,1)}, f16[2,144,1168]{2,1,0:T(8,128)(2,1)}, u32[]{:S(2)}, u32[]{:S(2)}) collective-permute-start(f16[2,144,1168]{2,1,0:T(8,128)(2,1)} %get-tuple-element.75), channel_id=1, source_target_pairs={{0,32},{8,104},{32,64},{40,8},{64,96},{72,40},{96,0},{104,72},{16,... | collective-permute-start | bytes 2018312 | tf_op jit(solution)/shard_map/ppermute | solution.py:45
  158.0 18.0 %collective-permute-start.21 = (f16[2,144,1168]{2,1,0:T(8,128)(2,1)S(1)}, f16[2,144,1168]{2,1,0:T(8,128)(2,1)}, u32[]{:S(2)}, u32[]{:S(2)}) collective-permute-start(f16[2,144,1168]{2,1,0:T(8,128)(2,1)S(1)} %get-tuple-element.76), channel_id=1, source_target_pairs={{0,96},{8,40},{32,0},{40,72},{64,32},{72,104},{96,64},{104,8},{16,... | collective-permute-start | bytes 2018312 | tf_op jit(solution)/shard_map/ppermute | solution.py:45
  178.3 12.9 %collective-permute-start.23 = (f16[2,144,1168]{2,1,0:T(8,128)(2,1)}, f16[2,144,1168]{2,1,0:T(8,128)(2,1)S(1)}, u32[]{:S(2)}, u32[]{:S(2)}) collective-permute-start(f16[2,144,1168]{2,1,0:T(8,128)(2,1)} %add_convert_fusion.1), channel_id=1, source_target_pairs={{0,32},{8,104},{32,64},{40,8},{64,96},{72,40},{96,0},{104,72},{16,... | collective-permute-start | bytes 2018312 | tf_op jit(solution)/shard_map/ppermute | solution.py:45
  178.8 19.0 %collective-permute-start.22 = (f16[304,896]{1,0:T(8,128)(2,1)}, f16[304,896]{1,0:T(8,128)(2,1)}, u32[]{:S(2)}, u32[]{:S(2)}) collective-permute-start(f16[304,896]{1,0:T(8,128)(2,1)} %fusion.3), channel_id=1, source_target_pairs={{16,1},{24,9},{48,33},{56,41},{80,65},{88,73},{112,97},{120,105},{... | collective-permute-start | bytes 1634312 | tf_op jit(solution)/shard_map/ppermute | solution.py:45
  192.8 9.2 %collective-permute-start.24 = (f16[144,1168]{1,0:T(8,128)(2,1)S(1)}, f16[144,1168]{1,0:T(8,128)(2,1)S(1)}, u32[]{:S(2)}, u32[]{:S(2)}) collective-permute-start(f16[144,1168]{1,0:T(8,128)(2,1)S(1)} %select_convert_fusion.1), channel_id=1, source_target_pairs={{0,1},{8,9},{32,33},{40,41},{64,65},{72,73},{96,97},{104,105},{16,... | collective-permute-start | bytes 1009160 | tf_op jit(solution)/shard_map/ppermute | solution.py:45
  193.7 14.9 %collective-permute-start.25 = (f16[144,1168]{1,0:T(8,128)(2,1)S(1)}, f16[144,1168]{1,0:T(8,128)(2,1)S(1)}, u32[]{:S(2)}, u32[]{:S(2)}) collective-permute-start(f16[144,1168]{1,0:T(8,128)(2,1)S(1)} %fusion.4), channel_id=1, source_target_pairs={{16,1},{24,9},{48,33},{56,41},{80,65},{88,73},{112,97},{120,105},{... | collective-permute-start | bytes 1009160 | tf_op jit(solution)/shard_map/ppermute | solution.py:45
  (27 other events, 183.1 us)
Sparse Core Ops, SparseCore 0:
  14.4 57.0 all-gather.7
  73.1 53.1 all-gather.9
  153.4 23.3 all-gather.5

commit v6 on v5

--- a/solution.py
+++ b/solution.py
@@ -174,7 +174,11 @@
 def scales(largest, tokens_total):
     largest = jnp.maximum(largest, 1e-18)
     most = largest * largest * tokens_total
-    return 32768.0 / most, most / (32768.0 * tokens_total)
+    return 32768.0 / most, most
+
+
+def mean(scaled, most, tokens_total):
+    return scaled * (1.0 / (32768.0 * tokens_total)) * most
 
 
 def along(p):
@@ -278,12 +282,12 @@
     largest = largest_over(
         largest, lambda x, y, z, c: (x, y ^ 1, z, c), lambda x, y, z, c: (x, y + 2, z, c)
     )
-    act_down, act_up = scales(largest[0, 0], tokens_total)
-    grad_down, grad_up = scales(largest[4, 0], tokens_total)
+    act_down, act_most = scales(largest[0, 0], tokens_total)
+    grad_down, grad_most = scales(largest[4, 0], tokens_total)
     columns = [activations, sibling, other, send(other, SIBLING)]
-    columns, rows_1, grads, grad_sibling, part, act_down, act_up, grad_down, grad_up = (
+    columns, rows_1, grads, grad_sibling, part, act_down, act_most, grad_down, grad_most = (
         lax.optimization_barrier(
-            (columns, rows_1, grads, grad_sibling, part, act_down, act_up, grad_down, grad_up)
+            (columns, rows_1, grads, grad_sibling, part, act_down, act_most, grad_down, grad_most)
         )
     )
 
@@ -330,7 +334,7 @@
     grad_cov = result(two, stays)[:half, width : width + out_grads.shape[1]]
     part = part.reshape(-1, queries)
     split, end = act_basis.shape[1], act_basis.shape[1] + grad_basis.shape[1]
-    return (act_cov * act_up, grad_cov * grad_up, part[:split].T, part[split:end].T)
+    return (mean(act_cov, act_most, tokens_total), mean(grad_cov, grad_most, tokens_total), part[:split].T, part[split:end].T)
 
 
 def solution(mesh):

time: 218 us -> 218 us (level)
  no operation moved by 1% of the time
where the time goes in v6:
time: 218 us; the launch traced here: 217 us
  waiting for transfers between devices  76.1 us (35%)
  Pallas kernels  41.3 us (19%)
  starting transfers between devices  38.4 us (18%)
  other arithmetic  30.8 us (14%)
  between operations  16.9 us (8%)
  local copies, waits for them, and re-layouts  12.9 us (6%)
    ppermute x30, waiting for transfers between devices, send(): return lax.ppermute(value, AXES, to)  57.7 us
    pallas_call x4, Pallas kernels, products(): pl.pallas_call(functools.partial(product_kernel, kinds, slots), out_shape...  40.6 us
    ppermute x30, starting transfers between devices, send(): return lax.ppermute(value, AXES, to)  38.3 us
    all_gather x3, waiting for transfers between devices, round_x(): return lax.all_gather(rows, AXES, axis_index_groups=X_RINGS)  18.4 us
  transfers between devices with their start and end apart: 33, of which 15 were waited for; matrix products, arithmetic and copies ran while one was open for 17% of the time, Pallas kernels for 19%

profile of v6, /device:TPU:16, one launch (start us, length us, event | category | flops | bytes accessed | tf_op | source)
XLA Modules:
  0.0 217.3 jit_solution(244592515627386151)
XLA Ops:
  9.7 2.4 %collective-permute-done.7 = bf16[448,1024]{1,0:T(8,128)(2,1)S(1)} collective-permute-done((bf16[448,1024]{1,0:T(8,128)(2,1)S(1)}, bf16[448,1024]{1,0:T(8,128)(2,1)S(1)}, u32[]{:S(2)}, u32[]{:S(2)}) %collective-permute-start.7) | collective-permute-done | bytes 917536 | tf_op jit(solution)/shard_map/ppermute | solution.py:45
  24.4 4.0 %collective-permute-start.2 = (f32[8,128]{1,0:T(8,128)S(1)}, f32[8,128]{1,0:T(8,128)S(1)}, u32[]{:S(2)}, u32[]{:S(2)}) collective-permute-start(f32[8,128]{1,0:T(8,128)S(1)} %fusion.16), channel_id=1, source_target_pairs={{0,64},{8,72},{32,96},{40,104},{64,0},{72,8},{96,32},{104,40},{16,... | collective-permute-start | bytes 12296 | tf_op jit(solution)/shard_map/ppermute | solution.py:45
  33.6 3.0 %collective-permute-start.4 = (f32[8,128]{1,0:T(8,128)S(1)}, f32[8,128]{1,0:T(8,128)S(1)}, u32[]{:S(2)}, u32[]{:S(2)}) collective-permute-start(f32[8,128]{1,0:T(8,128)S(1)} %max.32), channel_id=1, source_target_pairs={{0,4},{8,12},{32,36},{40,44},{64,68},{72,76},{96,100},{104,108},{1... | collective-permute-start | bytes 12296 | tf_op jit(solution)/shard_map/ppermute | solution.py:45
  41.0 17.7 %collective-permute-done.5.refs_2_ = bf16[1024,896]{1,0:T(8,128)(2,1)} collective-permute-done((bf16[1024,896]{1,0:T(8,128)(2,1)S(1)}, bf16[1024,896]{1,0:T(8,128)(2,1)}, u32[]{:S(2)}, u32[]{:S(2)}) %collective-permute-start.5) | collective-permute-done | bytes 1835040 | tf_op jit(solution)/shard_map/ppermute | solution.py:45
  60.2 2.3 %collective-permute-done.11 = f32[8,128]{1,0:T(8,128)S(1)} collective-permute-done((f32[8,128]{1,0:T(8,128)S(1)}, f32[8,128]{1,0:T(8,128)S(1)}, u32[]{:S(2)}, u32[]{:S(2)}) %collective-permute-start.11) | collective-permute-done | bytes 4128 | tf_op jit(solution)/shard_map/ppermute | solution.py:45
  63.4 4.2 %collective-permute-done.12 = f32[8,128]{1,0:T(8,128)S(1)} collective-permute-done((f32[8,128]{1,0:T(8,128)S(1)}, f32[8,128]{1,0:T(8,128)S(1)}, u32[]{:S(2)}, u32[]{:S(2)}) %collective-permute-start.12) | collective-permute-done | bytes 4128 | tf_op jit(solution)/shard_map/ppermute | solution.py:45
  71.4 10.5 %shard_map.95 = (f32[2,304,896]{2,1,0:T(8,128)}, f32[2,304,896]{2,1,0:T(8,128)}) custom-call(s32[4]{0:T(128)} %pad_add_fusion.source, bf16[4,2,304,1024]{3,2,1,0:T(8,128)(2,1)} %bitcast.69, bf16[1024,896]{1,0:T(8,128)(2,1)} %refs_0_.3, bf16[1024,896]{1,0:T(8,128)(2,1)} %collective-permute-done.6.refs_1_, bf16[1024,896]{1,0:T(8,128)(2,1)} %collective-permute-done.5.refs_2_, ...), custom_call_target="tpu_custom_call" | custom-call | flops 2231369728 | bytes 2490368 | tf_op jit(solution)/shard_map/pallas_call | solution.py:152
  81.9 3.1 %multiply_convert_fusion.1 = f16[2,304,896]{2,1,0:T(8,128)(2,1)} fusion(f32[2,304,896]{2,1,0:T(8,128)} %get-tuple-element.63, f32[]{:T(128)S(6)} %div.34), kind=kLoop, calls=%fused_computation.3 | loop fusion | flops 1089536 | bytes 3268612 | tf_op jit(solution)/shard_map/convert_element_type | solution.py:299
  88.1 2.9 %collective-permute-start.14 = (f32[4,1,80,512]{3,2,1,0:T(8,128)}, f32[4,1,80,512]{3,2,1,0:T(8,128)S(1)}, u32[]{:S(2)}, u32[]{:S(2)}) collective-permute-start(f32[4,1,80,512]{3,2,1,0:T(8,128)} %constant_dynamic-slice_fusion), channel_id=1, source_target_pairs={{0,1},{8,9},{32,33},{40,41},{64,65},{72,73},{96,97},{104,105},{16,... | collective-permute-start | bytes 1966088 | tf_op jit(solution)/shard_map/ppermute | solution.py:45
  91.0 2.8 %multiply_convert_fusion = f16[2,304,896]{2,1,0:T(8,128)(2,1)} fusion(f32[2,304,896]{2,1,0:T(8,128)} %get-tuple-element.67, f32[]{:T(128)S(6)} %div.34), kind=kLoop, calls=%fused_computation.1 | loop fusion | flops 1089536 | bytes 3268612 | tf_op jit(solution)/shard_map/convert_element_type | solution.py:300
  95.7 10.5 %shard_map.94 = (f32[2,304,896]{2,1,0:T(8,128)}, f32[2,304,896]{2,1,0:T(8,128)}) custom-call(s32[4]{0:T(128)} %pad_add_fusion.source, bf16[4,2,304,1024]{3,2,1,0:T(8,128)(2,1)} %bitcast.70, bf16[1024,896]{1,0:T(8,128)(2,1)} %refs_0_.3, bf16[1024,896]{1,0:T(8,128)(2,1)} %collective-permute-done.6.refs_1_, bf16[1024,896]{1,0:T(8,128)(2,1)} %collective-permute-done.5.refs_2_, ...), custom_call_target="tpu_custom_call" | custom-call | flops 2231369728 | bytes 2490368 | tf_op jit(solution)/shard_map/pallas_call | solution.py:152
  106.5 3.3 %add_convert_fusion = f16[2,304,896]{2,1,0:T(8,128)(2,1)} fusion(f16[2,304,896]{2,1,0:T(8,128)(2,1)} %collective-permute-done.13, f32[2,304,896]{2,1,0:T(8,128)} %get-tuple-element.62, f32[]{:T(128)S(6)} %div.34), kind=kLoop, calls=%fused_computation.2 | loop fusion | flops 2179072 | bytes 4358148 | tf_op jit(solution)/shard_map/convert_element_type | solution.py:304
  109.8 16.5 %all-gather.10.cloned.1.call-done = bf16[8,288,1024]{2,1,0:T(8,128)(2,1)} async-done(((bf16[2,288,1024]{2,1,0:T(8,128)(2,1)}), bf16[8,288,1024]{2,1,0:T(8,128)(2,1)}) %all-gather.10.cloned.1.call-update) | async-done | bytes 4718608 | tf_op jit(solution)/shard_map/all_gather | solution.py:237
  134.9 9.8 %shard_map.96 = (f32[2,144,1168]{2,1,0:T(8,128)}, f32[2,144,1168]{2,1,0:T(8,128)}) custom-call(s32[4]{0:T(128)} %pad_add_fusion.source, bf16[4,2,288,1024]{3,2,1,0:T(8,128)(2,1)} %bitcast.71, bf16[1024,896]{1,0:T(8,128)(2,1)} %refs_0_.3, bf16[1024,896]{1,0:T(8,128)(2,1)} %collective-permute-done.6.refs_1_, bf16[1024,896]{1,0:T(8,128)(2,1)} %collective-permute-done.5.refs_2_, ...), custom_call_target="tpu_custom_call" | custom-call | flops 1377828864 | bytes 1179648 | tf_op jit(solution)/shard_map/pallas_call | solution.py:152
  145.3 2.9 %multiply_convert_fusion.2 = (f16[2,144,1168]{2,1,0:T(8,128)(2,1)S(1)}, f16[2,144,1168]{2,1,0:T(8,128)(2,1)}) fusion(f32[2,144,1168]{2,1,0:T(8,128)} %get-tuple-element.73, f32[1168]{0:T(1024)S(1)} %fusion.8, f32[2,144,1168]{2,1,0:T(8,128)} %get-tuple-element.71), kind=kLoop, calls=%fused_computation.8 | loop fusion | flops 1345536 | bytes 4041280 | tf_op jit(solution)/shard_map/convert_element_type | solution.py:313
  148.3 4.3 %collective-permute-done.29 = f32[80,512]{1,0:T(8,128)S(1)} collective-permute-done((f32[80,512]{1,0:T(8,128)S(1)}, f32[80,512]{1,0:T(8,128)S(1)}, u32[]{:S(2)}, u32[]{:S(2)}) %collective-permute-start.29) | collective-permute-done | bytes 163872 | tf_op jit(solution)/shard_map/ppermute | solution.py:45
  153.3 2.6 %convert_add_fusion = f32[2,304,896]{2,1,0:T(8,128)S(1)} fusion(f16[2,304,896]{2,1,0:T(8,128)(2,1)} %collective-permute-done.16, f16[2,304,896]{2,1,0:T(8,128)(2,1)} %collective-permute-done.15, f32[2,304,896]{2,1,0:T(8,128)} %get-tuple-element.60, f32[]{:T(128)S(6)} %div.34), kind=kLoop, calls=%fused_computation | loop fusion | flops 2723840 | bytes 6537220 | tf_op jit(solution)/shard_map/add | solution.py:191
  158.0 2.6 %collective-permute-start.21 = (f16[2,144,1168]{2,1,0:T(8,128)(2,1)S(1)}, f16[2,144,1168]{2,1,0:T(8,128)(2,1)}, u32[]{:S(2)}, u32[]{:S(2)}) collective-permute-start(f16[2,144,1168]{2,1,0:T(8,128)(2,1)S(1)} %get-tuple-element.76), channel_id=1, source_target_pairs={{0,96},{8,40},{32,0},{40,72},{64,32},{72,104},{96,64},{104,8},{16,... | collective-permute-start | bytes 2018312 | tf_op jit(solution)/shard_map/ppermute | solution.py:45
  160.6 9.9 %shard_map.97 = (f32[2,144,1168]{2,1,0:T(8,128)}, f32[2,144,1168]{2,1,0:T(8,128)}) custom-call(s32[4]{0:T(128)} %pad_add_fusion.source, bf16[4,2,288,1024]{3,2,1,0:T(8,128)(2,1)} %bitcast.72, bf16[1024,896]{1,0:T(8,128)(2,1)} %refs_0_.3, bf16[1024,896]{1,0:T(8,128)(2,1)} %collective-permute-done.6.refs_1_, bf16[1024,896]{1,0:T(8,128)(2,1)} %collective-permute-done.5.refs_2_, ...), custom_call_target="tpu_custom_call" | custom-call | flops 1377828864 | bytes 1179648 | tf_op jit(solution)/shard_map/pallas_call | solution.py:152
  171.4 4.6 %collective-permute-done.20 = f16[2,144,1168]{2,1,0:T(8,128)(2,1)} collective-permute-done((f16[2,144,1168]{2,1,0:T(8,128)(2,1)}, f16[2,144,1168]{2,1,0:T(8,128)(2,1)}, u32[]{:S(2)}, u32[]{:S(2)}) %collective-permute-start.20) | collective-permute-done | bytes 672800 | tf_op jit(solution)/shard_map/ppermute | solution.py:45
  183.1 8.1 %collective-permute-done.23 = f16[2,144,1168]{2,1,0:T(8,128)(2,1)S(1)} collective-permute-done((f16[2,144,1168]{2,1,0:T(8,128)(2,1)}, f16[2,144,1168]{2,1,0:T(8,128)(2,1)S(1)}, u32[]{:S(2)}, u32[]{:S(2)}) %collective-permute-start.23) | collective-permute-done | bytes 672800 | tf_op jit(solution)/shard_map/ppermute | solution.py:45
  193.7 2.4 %collective-permute-start.25 = (f16[144,1168]{1,0:T(8,128)(2,1)S(1)}, f16[144,1168]{1,0:T(8,128)(2,1)S(1)}, u32[]{:S(2)}, u32[]{:S(2)}) collective-permute-start(f16[144,1168]{1,0:T(8,128)(2,1)S(1)} %fusion.4), channel_id=1, source_target_pairs={{16,1},{24,9},{48,33},{56,41},{80,65},{88,73},{112,97},{120,105},{... | collective-permute-start | bytes 1009160 | tf_op jit(solution)/shard_map/ppermute | solution.py:45
  199.1 2.9 %collective-permute-done.24 = f16[144,1168]{1,0:T(8,128)(2,1)S(1)} collective-permute-done((f16[144,1168]{1,0:T(8,128)(2,1)S(1)}, f16[144,1168]{1,0:T(8,128)(2,1)S(1)}, u32[]{:S(2)}, u32[]{:S(2)}) %collective-permute-start.24) | collective-permute-done | bytes 336416 | tf_op jit(solution)/shard_map/ppermute | solution.py:45
  202.0 6.7 %collective-permute-done.25 = f16[144,1168]{1,0:T(8,128)(2,1)S(1)} collective-permute-done((f16[144,1168]{1,0:T(8,128)(2,1)S(1)}, f16[144,1168]{1,0:T(8,128)(2,1)S(1)}, u32[]{:S(2)}, u32[]{:S(2)}) %collective-permute-start.25) | collective-permute-done | bytes 336416 | tf_op jit(solution)/shard_map/ppermute | solution.py:45
  (135 shorter events, 60.4 us)
Async XLA Ops:
  7.2 64.3 %all-gather.8.cloned.1.call-start = ((), (), s32[]{:S(2)}) async-start(), calls=%async_computation.1 | async-start | bytes 6225920 | tf_op jit(solution)/shard_map/all_gather | solution.py:237
  14.2 112.1 %all-gather.10.cloned.1.call-start = ((), (), s32[]{:S(2)}) async-start(), calls=%async_computation.2 | async-start | bytes 5898240 | tf_op jit(solution)/shard_map/all_gather | solution.py:237
  15.0 43.7 %collective-permute-start.5 = (bf16[1024,896]{1,0:T(8,128)(2,1)S(1)}, bf16[1024,896]{1,0:T(8,128)(2,1)}, u32[]{:S(2)}, u32[]{:S(2)}) collective-permute-start(bf16[1024,896]{1,0:T(8,128)(2,1)S(1)} %copy-done.3), channel_id=1, source_target_pairs={{0,1},{8,9},{32,33},{40,41},{64,65},{72,73},{96,97},{104,105},{16,... | collective-permute-start | bytes 5505032 | tf_op jit(solution)/shard_map/ppermute | solution.py:45
  15.2 43.4 %collective-permute-start.6 = (bf16[1024,896]{1,0:T(8,128)(2,1)S(1)}, bf16[1024,896]{1,0:T(8,128)(2,1)}, u32[]{:S(2)}, u32[]{:S(2)}) collective-permute-start(bf16[1024,896]{1,0:T(8,128)(2,1)S(1)} %copy-done.3), channel_id=1, source_target_pairs={{0,8},{8,0},{32,40},{40,32},{64,72},{72,64},{96,104},{104,96},{16,... | collective-permute-start | bytes 5505032 | tf_op jit(solution)/shard_map/ppermute | solution.py:45
  18.8 20.0 %collective-permute-start.8 = (bf16[132,1024]{1,0:T(8,128)(2,1)S(1)}, bf16[132,1024]{1,0:T(8,128)(2,1)S(1)}, u32[]{:S(2)}, u32[]{:S(2)}) collective-permute-start(bf16[132,1024]{1,0:T(8,128)(2,1)S(1)} %get-tuple-element.94), channel_id=1, source_target_pairs={{0,8},{8,0},{32,40},{40,32},{64,72},{72,64},{96,104},{104,96},{16,... | collective-permute-start | bytes 811016 | tf_op jit(solution)/shard_map/ppermute | solution.py:45
  20.1 20.9 %collective-permute-start.9 = (bf16[272,1024]{1,0:T(8,128)(2,1)S(1)}, bf16[272,1024]{1,0:T(8,128)(2,1)}, u32[]{:S(2)}, u32[]{:S(2)}) collective-permute-start(bf16[272,1024]{1,0:T(8,128)(2,1)S(1)} %pad.12.refs_4_), channel_id=1, source_target_pairs={{0,8},{8,0},{32,40},{40,32},{64,72},{72,64},{96,104},{104,96},{16,... | collective-permute-start | bytes 1671176 | tf_op jit(solution)/shard_map/ppermute | solution.py:45
  58.7 122.1 %all-gather.6.cloned.1.call-start = ((), (), s32[]{:S(2)}) async-start(), calls=%async_computation | async-start | bytes 1638400 | tf_op jit(solution)/shard_map/all_gather | solution.py:237
  58.7 10.8 %collective-permute-start.10 = (bf16[1024,896]{1,0:T(8,128)(2,1)}, bf16[1024,896]{1,0:T(8,128)(2,1)S(1)}, u32[]{:S(2)}, u32[]{:S(2)}) collective-permute-start(bf16[1024,896]{1,0:T(8,128)(2,1)} %collective-permute-done.5.refs_2_), channel_id=1, source_target_pairs={{0,8},{8,0},{32,40},{40,32},{64,72},{72,64},{96,104},{104,96},{16,... | collective-permute-start | bytes 5505032 | tf_op jit(solution)/shard_map/ppermute | solution.py:45
  85.0 21.4 %collective-permute-start.13 = (f16[2,304,896]{2,1,0:T(8,128)(2,1)}, f16[2,304,896]{2,1,0:T(8,128)(2,1)}, u32[]{:S(2)}, u32[]{:S(2)}) collective-permute-start(f16[2,304,896]{2,1,0:T(8,128)(2,1)} %multiply_convert_fusion.1), channel_id=1, source_target_pairs={{0,32},{8,104},{32,64},{40,8},{64,96},{72,40},{96,0},{104,72},{16,... | collective-permute-start | bytes 3268616 | tf_op jit(solution)/shard_map/ppermute | solution.py:45
  86.6 19.6 %collective-permute-start.17 = (bf16[272,1024]{1,0:T(8,128)(2,1)S(1)}, bf16[272,1024]{1,0:T(8,128)(2,1)S(1)}, u32[]{:S(2)}, u32[]{:S(2)}) collective-permute-start(bf16[272,1024]{1,0:T(8,128)(2,1)S(1)} %pad.12.refs_4_), channel_id=1, source_target_pairs={{0,1},{8,9},{32,33},{40,41},{64,65},{72,73},{96,97},{104,105},{16,... | collective-permute-start | bytes 1671176 | tf_op jit(solution)/shard_map/ppermute | solution.py:45
  88.1 38.2 %collective-permute-start.14 = (f32[4,1,80,512]{3,2,1,0:T(8,128)}, f32[4,1,80,512]{3,2,1,0:T(8,128)S(1)}, u32[]{:S(2)}, u32[]{:S(2)}) collective-permute-start(f32[4,1,80,512]{3,2,1,0:T(8,128)} %constant_dynamic-slice_fusion), channel_id=1, source_target_pairs={{0,1},{8,9},{32,33},{40,41},{64,65},{72,73},{96,97},{104,105},{16,... | collective-permute-start | bytes 1966088 | tf_op jit(solution)/shard_map/ppermute | solution.py:45
  93.9 59.5 %collective-permute-start.16 = (f16[2,304,896]{2,1,0:T(8,128)(2,1)}, f16[2,304,896]{2,1,0:T(8,128)(2,1)}, u32[]{:S(2)}, u32[]{:S(2)}) collective-permute-start(f16[2,304,896]{2,1,0:T(8,128)(2,1)} %multiply_convert_fusion), channel_id=1, source_target_pairs={{0,96},{8,40},{32,0},{40,72},{64,32},{72,104},{96,64},{104,8},{16,... | collective-permute-start | bytes 3268616 | tf_op jit(solution)/shard_map/ppermute | solution.py:45
  106.2 27.0 %collective-permute-start.18 = (bf16[272,1024]{1,0:T(8,128)(2,1)S(1)}, bf16[272,1024]{1,0:T(8,128)(2,1)S(1)}, u32[]{:S(2)}, u32[]{:S(2)}) collective-permute-start(bf16[272,1024]{1,0:T(8,128)(2,1)S(1)} %collective-permute-done.17.refs_6_), channel_id=1, source_target_pairs={{0,8},{8,0},{32,40},{40,32},{64,72},{72,64},{96,104},{104,96},{16,... | collective-permute-start | bytes 1671176 | tf_op jit(solution)/shard_map/ppermute | solution.py:45
  128.4 16.3 %collective-permute-start.26 = (f32[80,512]{1,0:T(8,128)S(1)}, f32[80,512]{1,0:T(8,128)S(1)}, u32[]{:S(2)}, u32[]{:S(2)}) collective-permute-start(f32[80,512]{1,0:T(8,128)S(1)} %get-tuple-element.90), channel_id=1, source_target_pairs={{0,2},{8,10},{32,34},{40,42},{64,66},{72,74},{96,98},{104,106},{16... | collective-permute-start | bytes 491528 | tf_op jit(solution)/shard_map/ppermute | solution.py:45
  129.4 15.3 %collective-permute-start.27 = (f32[80,512]{1,0:T(8,128)S(1)}, f32[80,512]{1,0:T(8,128)S(1)}, u32[]{:S(2)}, u32[]{:S(2)}) collective-permute-start(f32[80,512]{1,0:T(8,128)S(1)} %get-tuple-element.92), channel_id=1, source_target_pairs={{0,4},{8,12},{32,36},{40,44},{64,68},{72,76},{96,100},{104,108},{1... | collective-permute-start | bytes 491528 | tf_op jit(solution)/shard_map/ppermute | solution.py:45
  131.1 13.5 %collective-permute-start.28 = (f32[80,512]{1,0:T(8,128)S(1)}, f32[80,512]{1,0:T(8,128)S(1)}, u32[]{:S(2)}, u32[]{:S(2)}) collective-permute-start(f32[80,512]{1,0:T(8,128)S(1)} %get-tuple-element.91), channel_id=1, source_target_pairs={{0,6},{8,14},{32,38},{40,46},{64,70},{72,78},{96,102},{104,110},{1... | collective-permute-start | bytes 491528 | tf_op jit(solution)/shard_map/ppermute | solution.py:45
  133.2 20.1 %collective-permute-start.15 = (f16[2,304,896]{2,1,0:T(8,128)(2,1)}, f16[2,304,896]{2,1,0:T(8,128)(2,1)}, u32[]{:S(2)}, u32[]{:S(2)}) collective-permute-start(f16[2,304,896]{2,1,0:T(8,128)(2,1)} %add_convert_fusion), channel_id=1, source_target_pairs={{0,32},{8,104},{32,64},{40,8},{64,96},{72,40},{96,0},{104,72},{16,... | collective-permute-start | bytes 3268616 | tf_op jit(solution)/shard_map/ppermute | solution.py:45
  156.1 14.4 %collective-permute-start.19 = (f16[304,896]{1,0:T(8,128)(2,1)S(1)}, f16[304,896]{1,0:T(8,128)(2,1)S(1)}, u32[]{:S(2)}, u32[]{:S(2)}) collective-permute-start(f16[304,896]{1,0:T(8,128)(2,1)S(1)} %select_convert_fusion), channel_id=1, source_target_pairs={{0,16},{8,24},{32,48},{40,56},{64,80},{72,88},{96,112},{104,120},{... | collective-permute-start | bytes 1634312 | tf_op jit(solution)/shard_map/ppermute | solution.py:45
  157.4 18.7 %collective-permute-start.20 = (f16[2,144,1168]{2,1,0:T(8,128)(2,1)}, f16[2,144,1168]{2,1,0:T(8,128)(2,1)}, u32[]{:S(2)}, u32[]{:S(2)}) collective-permute-start(f16[2,144,1168]{2,1,0:T(8,128)(2,1)} %get-tuple-element.75), channel_id=1, source_target_pairs={{0,32},{8,104},{32,64},{40,8},{64,96},{72,40},{96,0},{104,72},{16,... | collective-permute-start | bytes 2018312 | tf_op jit(solution)/shard_map/ppermute | solution.py:45
  158.0 18.0 %collective-permute-start.21 = (f16[2,144,1168]{2,1,0:T(8,128)(2,1)S(1)}, f16[2,144,1168]{2,1,0:T(8,128)(2,1)}, u32[]{:S(2)}, u32[]{:S(2)}) collective-permute-start(f16[2,144,1168]{2,1,0:T(8,128)(2,1)S(1)} %get-tuple-element.76), channel_id=1, source_target_pairs={{0,96},{8,40},{32,0},{40,72},{64,32},{72,104},{96,64},{104,8},{16,... | collective-permute-start | bytes 2018312 | tf_op jit(solution)/shard_map/ppermute | solution.py:45
  178.3 12.9 %collective-permute-start.23 = (f16[2,144,1168]{2,1,0:T(8,128)(2,1)}, f16[2,144,1168]{2,1,0:T(8,128)(2,1)S(1)}, u32[]{:S(2)}, u32[]{:S(2)}) collective-permute-start(f16[2,144,1168]{2,1,0:T(8,128)(2,1)} %add_convert_fusion.1), channel_id=1, source_target_pairs={{0,32},{8,104},{32,64},{40,8},{64,96},{72,40},{96,0},{104,72},{16,... | collective-permute-start | bytes 2018312 | tf_op jit(solution)/shard_map/ppermute | solution.py:45
  178.8 19.0 %collective-permute-start.22 = (f16[304,896]{1,0:T(8,128)(2,1)}, f16[304,896]{1,0:T(8,128)(2,1)}, u32[]{:S(2)}, u32[]{:S(2)}) collective-permute-start(f16[304,896]{1,0:T(8,128)(2,1)} %fusion.3), channel_id=1, source_target_pairs={{16,1},{24,9},{48,33},{56,41},{80,65},{88,73},{112,97},{120,105},{... | collective-permute-start | bytes 1634312 | tf_op jit(solution)/shard_map/ppermute | solution.py:45
  192.8 9.2 %collective-permute-start.24 = (f16[144,1168]{1,0:T(8,128)(2,1)S(1)}, f16[144,1168]{1,0:T(8,128)(2,1)S(1)}, u32[]{:S(2)}, u32[]{:S(2)}) collective-permute-start(f16[144,1168]{1,0:T(8,128)(2,1)S(1)} %select_convert_fusion.1), channel_id=1, source_target_pairs={{0,1},{8,9},{32,33},{40,41},{64,65},{72,73},{96,97},{104,105},{16,... | collective-permute-start | bytes 1009160 | tf_op jit(solution)/shard_map/ppermute | solution.py:45
  193.7 14.9 %collective-permute-start.25 = (f16[144,1168]{1,0:T(8,128)(2,1)S(1)}, f16[144,1168]{1,0:T(8,128)(2,1)S(1)}, u32[]{:S(2)}, u32[]{:S(2)}) collective-permute-start(f16[144,1168]{1,0:T(8,128)(2,1)S(1)} %fusion.4), channel_id=1, source_target_pairs={{16,1},{24,9},{48,33},{56,41},{80,65},{88,73},{112,97},{120,105},{... | collective-permute-start | bytes 1009160 | tf_op jit(solution)/shard_map/ppermute | solution.py:45
  (27 other events, 183.1 us)
Sparse Core Ops, SparseCore 0:
  14.4 57.0 all-gather.7
  73.1 53.1 all-gather.9
  153.4 23.3 all-gather.5

commit v7 on v6

--- a/solution.py
+++ b/solution.py
@@ -322,9 +322,10 @@
     part = (part, send(part, OTHER_COLUMN))
 
     message = crossing(one)
-    message, two = lax.optimization_barrier((message, two))
+    message, two["close"] = lax.optimization_barrier((message, two["close"]))
     one["m"] = send(message, Y_MIDDLE)
     two = along(two)
+    one, two = lax.optimization_barrier((one, two))
     part = round_x(jnp.where(y_hi == 0, jnp.stack(part), jnp.stack(part[::-1])))
 
     two = across(two, stays)

time: 218 us -> 219 us (level)
  transfers between devices with their start and end apart: 33 -> 33, of which waited for: 15 -> 15; matrix products, arithmetic and copies ran while one was open for 17% -> 16% of each run, Pallas kernels for 19% -> 19%
where the time goes in v7:
time: 219 us; the launch traced here: 217 us
  waiting for transfers between devices  75.8 us (35%)
  Pallas kernels  41.3 us (19%)
  starting transfers between devices  38.3 us (17%)
  other arithmetic  31 us (14%)
  between operations  16.9 us (8%)
  local copies, waits for them, and re-layouts  12.9 us (6%)
    ppermute x30, waiting for transfers between devices, send(): return lax.ppermute(value, AXES, to)  57.4 us
    pallas_call x4, Pallas kernels, products(): pl.pallas_call(functools.partial(product_kernel, kinds, slots), out_shape...  40.6 us
    ppermute x30, starting transfers between devices, send(): return lax.ppermute(value, AXES, to)  38.2 us
    all_gather x3, waiting for transfers between devices, round_x(): return lax.all_gather(rows, AXES, axis_index_groups=X_RINGS)  18.4 us
  transfers between devices with their start and end apart: 33, of which 15 were waited for; matrix products, arithmetic and copies ran while one was open for 16% of the time, Pallas kernels for 19%

profile of v7, /device:TPU:16, one launch (start us, length us, event | category | flops | bytes accessed | tf_op | source)
XLA Modules:
  0.0 217.0 jit_solution(14243793227263526405)
XLA Ops:
  9.7 2.4 %collective-permute-done.7 = bf16[448,1024]{1,0:T(8,128)(2,1)S(1)} collective-permute-done((bf16[448,1024]{1,0:T(8,128)(2,1)S(1)}, bf16[448,1024]{1,0:T(8,128)(2,1)S(1)}, u32[]{:S(2)}, u32[]{:S(2)}) %collective-permute-start.7) | collective-permute-done | bytes 917536 | tf_op jit(solution)/shard_map/ppermute | solution.py:45
  24.4 4.0 %collective-permute-start.2 = (f32[8,128]{1,0:T(8,128)S(1)}, f32[8,128]{1,0:T(8,128)S(1)}, u32[]{:S(2)}, u32[]{:S(2)}) collective-permute-start(f32[8,128]{1,0:T(8,128)S(1)} %fusion.17), channel_id=1, source_target_pairs={{0,64},{8,72},{32,96},{40,104},{64,0},{72,8},{96,32},{104,40},{16,... | collective-permute-start | bytes 12296 | tf_op jit(solution)/shard_map/ppermute | solution.py:45
  33.6 3.0 %collective-permute-start.4 = (f32[8,128]{1,0:T(8,128)S(1)}, f32[8,128]{1,0:T(8,128)S(1)}, u32[]{:S(2)}, u32[]{:S(2)}) collective-permute-start(f32[8,128]{1,0:T(8,128)S(1)} %max.32), channel_id=1, source_target_pairs={{0,4},{8,12},{32,36},{40,44},{64,68},{72,76},{96,100},{104,108},{1... | collective-permute-start | bytes 12296 | tf_op jit(solution)/shard_map/ppermute | solution.py:45
  41.0 17.7 %collective-permute-done.5.refs_2_ = bf16[1024,896]{1,0:T(8,128)(2,1)} collective-permute-done((bf16[1024,896]{1,0:T(8,128)(2,1)S(1)}, bf16[1024,896]{1,0:T(8,128)(2,1)}, u32[]{:S(2)}, u32[]{:S(2)}) %collective-permute-start.5) | collective-permute-done | bytes 1835040 | tf_op jit(solution)/shard_map/ppermute | solution.py:45
  60.2 2.3 %collective-permute-done.11 = f32[8,128]{1,0:T(8,128)S(1)} collective-permute-done((f32[8,128]{1,0:T(8,128)S(1)}, f32[8,128]{1,0:T(8,128)S(1)}, u32[]{:S(2)}, u32[]{:S(2)}) %collective-permute-start.11) | collective-permute-done | bytes 4128 | tf_op jit(solution)/shard_map/ppermute | solution.py:45
  63.4 4.2 %collective-permute-done.12 = f32[8,128]{1,0:T(8,128)S(1)} collective-permute-done((f32[8,128]{1,0:T(8,128)S(1)}, f32[8,128]{1,0:T(8,128)S(1)}, u32[]{:S(2)}, u32[]{:S(2)}) %collective-permute-start.12) | collective-permute-done | bytes 4128 | tf_op jit(solution)/shard_map/ppermute | solution.py:45
  71.4 10.5 %shard_map.95 = (f32[2,304,896]{2,1,0:T(8,128)}, f32[2,304,896]{2,1,0:T(8,128)}) custom-call(s32[4]{0:T(128)} %pad_add_fusion.source, bf16[4,2,304,1024]{3,2,1,0:T(8,128)(2,1)} %bitcast.73, bf16[1024,896]{1,0:T(8,128)(2,1)} %refs_0_.3, bf16[1024,896]{1,0:T(8,128)(2,1)} %collective-permute-done.6.refs_1_, bf16[1024,896]{1,0:T(8,128)(2,1)} %collective-permute-done.5.refs_2_, ...), custom_call_target="tpu_custom_call" | custom-call | flops 2231369728 | bytes 2490368 | tf_op jit(solution)/shard_map/pallas_call | solution.py:152
  81.9 3.1 %multiply_convert_fusion.1 = f16[2,304,896]{2,1,0:T(8,128)(2,1)} fusion(f32[2,304,896]{2,1,0:T(8,128)} %get-tuple-element.67, f32[]{:T(128)S(6)} %div.34), kind=kLoop, calls=%fused_computation.3 | loop fusion | flops 1089536 | bytes 3268612 | tf_op jit(solution)/shard_map/convert_element_type | solution.py:299
  88.1 2.9 %collective-permute-start.14 = (f32[4,1,80,512]{3,2,1,0:T(8,128)}, f32[4,1,80,512]{3,2,1,0:T(8,128)S(1)}, u32[]{:S(2)}, u32[]{:S(2)}) collective-permute-start(f32[4,1,80,512]{3,2,1,0:T(8,128)} %constant_dynamic-slice_fusion), channel_id=1, source_target_pairs={{0,1},{8,9},{32,33},{40,41},{64,65},{72,73},{96,97},{104,105},{16,... | collective-permute-start | bytes 1966088 | tf_op jit(solution)/shard_map/ppermute | solution.py:45
  91.0 2.8 %multiply_convert_fusion = f16[2,304,896]{2,1,0:T(8,128)(2,1)} fusion(f32[2,304,896]{2,1,0:T(8,128)} %get-tuple-element.71, f32[]{:T(128)S(6)} %div.34), kind=kLoop, calls=%fused_computation.1 | loop fusion | flops 1089536 | bytes 3268612 | tf_op jit(solution)/shard_map/convert_element_type | solution.py:300
  95.7 10.5 %shard_map.94 = (f32[2,304,896]{2,1,0:T(8,128)}, f32[2,304,896]{2,1,0:T(8,128)}) custom-call(s32[4]{0:T(128)} %pad_add_fusion.source, bf16[4,2,304,1024]{3,2,1,0:T(8,128)(2,1)} %bitcast.74, bf16[1024,896]{1,0:T(8,128)(2,1)} %refs_0_.3, bf16[1024,896]{1,0:T(8,128)(2,1)} %collective-permute-done.6.refs_1_, bf16[1024,896]{1,0:T(8,128)(2,1)} %collective-permute-done.5.refs_2_, ...), custom_call_target="tpu_custom_call" | custom-call | flops 2231369728 | bytes 2490368 | tf_op jit(solution)/shard_map/pallas_call | solution.py:152
  106.5 3.3 %add_convert_fusion = f16[2,304,896]{2,1,0:T(8,128)(2,1)} fusion(f16[2,304,896]{2,1,0:T(8,128)(2,1)} %collective-permute-done.13, f32[2,304,896]{2,1,0:T(8,128)} %get-tuple-element.66, f32[]{:T(128)S(6)} %div.34), kind=kLoop, calls=%fused_computation.2 | loop fusion | flops 2179072 | bytes 4358148 | tf_op jit(solution)/shard_map/convert_element_type | solution.py:304
  109.8 16.5 %all-gather.10.cloned.1.call-done = bf16[8,288,1024]{2,1,0:T(8,128)(2,1)} async-done(((bf16[2,288,1024]{2,1,0:T(8,128)(2,1)}), bf16[8,288,1024]{2,1,0:T(8,128)(2,1)}) %all-gather.10.cloned.1.call-update) | async-done | bytes 4718608 | tf_op jit(solution)/shard_map/all_gather | solution.py:237
  134.9 9.8 %shard_map.96 = (f32[2,144,1168]{2,1,0:T(8,128)}, f32[2,144,1168]{2,1,0:T(8,128)}) custom-call(s32[4]{0:T(128)} %pad_add_fusion.source, bf16[4,2,288,1024]{3,2,1,0:T(8,128)(2,1)} %bitcast.75, bf16[1024,896]{1,0:T(8,128)(2,1)} %refs_0_.3, bf16[1024,896]{1,0:T(8,128)(2,1)} %collective-permute-done.6.refs_1_, bf16[1024,896]{1,0:T(8,128)(2,1)} %collective-permute-done.5.refs_2_, ...), custom_call_target="tpu_custom_call" | custom-call | flops 1377828864 | bytes 1179648 | tf_op jit(solution)/shard_map/pallas_call | solution.py:152
  145.3 2.9 %multiply_convert_fusion.2 = (f16[2,144,1168]{2,1,0:T(8,128)(2,1)S(1)}, f16[2,144,1168]{2,1,0:T(8,128)(2,1)}) fusion(f32[2,144,1168]{2,1,0:T(8,128)} %get-tuple-element.77, f32[1168]{0:T(1024)S(1)} %fusion.9, f32[2,144,1168]{2,1,0:T(8,128)} %get-tuple-element.75), kind=kLoop, calls=%fused_computation.8 | loop fusion | flops 1345536 | bytes 4041280 | tf_op jit(solution)/shard_map/convert_element_type | solution.py:313
  148.3 4.3 %collective-permute-done.29 = f32[80,512]{1,0:T(8,128)S(1)} collective-permute-done((f32[80,512]{1,0:T(8,128)S(1)}, f32[80,512]{1,0:T(8,128)S(1)}, u32[]{:S(2)}, u32[]{:S(2)}) %collective-permute-start.29) | collective-permute-done | bytes 163872 | tf_op jit(solution)/shard_map/ppermute | solution.py:45
  153.3 2.6 %convert_add_fusion = f32[2,304,896]{2,1,0:T(8,128)S(1)} fusion(f16[2,304,896]{2,1,0:T(8,128)(2,1)} %collective-permute-done.16, f16[2,304,896]{2,1,0:T(8,128)(2,1)} %collective-permute-done.15, f32[2,304,896]{2,1,0:T(8,128)} %get-tuple-element.64, f32[]{:T(128)S(6)} %div.34), kind=kLoop, calls=%fused_computation | loop fusion | flops 2723840 | bytes 6537220 | tf_op jit(solution)/shard_map/add | solution.py:191
  158.0 2.6 %collective-permute-start.23 = (f16[2,144,1168]{2,1,0:T(8,128)(2,1)S(1)}, f16[2,144,1168]{2,1,0:T(8,128)(2,1)}, u32[]{:S(2)}, u32[]{:S(2)}) collective-permute-start(f16[2,144,1168]{2,1,0:T(8,128)(2,1)S(1)} %get-tuple-element.85), channel_id=1, source_target_pairs={{0,96},{8,40},{32,0},{40,72},{64,32},{72,104},{96,64},{104,8},{16,... | collective-permute-start | bytes 2018312 | tf_op jit(solution)/shard_map/ppermute | solution.py:45
  160.6 9.9 %shard_map.97 = (f32[2,144,1168]{2,1,0:T(8,128)}, f32[2,144,1168]{2,1,0:T(8,128)}) custom-call(s32[4]{0:T(128)} %pad_add_fusion.source, bf16[4,2,288,1024]{3,2,1,0:T(8,128)(2,1)} %bitcast.76, bf16[1024,896]{1,0:T(8,128)(2,1)} %refs_0_.3, bf16[1024,896]{1,0:T(8,128)(2,1)} %collective-permute-done.6.refs_1_, bf16[1024,896]{1,0:T(8,128)(2,1)} %collective-permute-done.5.refs_2_, ...), custom_call_target="tpu_custom_call" | custom-call | flops 1377828864 | bytes 1179648 | tf_op jit(solution)/shard_map/pallas_call | solution.py:152
  171.4 4.6 %collective-permute-done.21 = f16[2,144,1168]{2,1,0:T(8,128)(2,1)} collective-permute-done((f16[2,144,1168]{2,1,0:T(8,128)(2,1)}, f16[2,144,1168]{2,1,0:T(8,128)(2,1)}, u32[]{:S(2)}, u32[]{:S(2)}) %collective-permute-start.21) | collective-permute-done | bytes 672800 | tf_op jit(solution)/shard_map/ppermute | solution.py:45
  183.1 8.3 %collective-permute-done.20 = f16[304,896]{1,0:T(8,128)(2,1)} collective-permute-done((f16[304,896]{1,0:T(8,128)(2,1)}, f16[304,896]{1,0:T(8,128)(2,1)}, u32[]{:S(2)}, u32[]{:S(2)}) %collective-permute-start.20) | collective-permute-done | bytes 544800 | tf_op jit(solution)/shard_map/ppermute | solution.py:45
  194.0 2.4 %collective-permute-start.25 = (f16[144,1168]{1,0:T(8,128)(2,1)S(1)}, f16[144,1168]{1,0:T(8,128)(2,1)S(1)}, u32[]{:S(2)}, u32[]{:S(2)}) collective-permute-start(f16[144,1168]{1,0:T(8,128)(2,1)S(1)} %fusion.5), channel_id=1, source_target_pairs={{16,1},{24,9},{48,33},{56,41},{80,65},{88,73},{112,97},{120,105},{... | collective-permute-start | bytes 1009160 | tf_op jit(solution)/shard_map/ppermute | solution.py:45
  199.3 3.1 %collective-permute-done.24 = f16[144,1168]{1,0:T(8,128)(2,1)S(1)} collective-permute-done((f16[144,1168]{1,0:T(8,128)(2,1)S(1)}, f16[144,1168]{1,0:T(8,128)(2,1)S(1)}, u32[]{:S(2)}, u32[]{:S(2)}) %collective-permute-start.24) | collective-permute-done | bytes 336416 | tf_op jit(solution)/shard_map/ppermute | solution.py:45
  202.4 5.9 %collective-permute-done.25 = f16[144,1168]{1,0:T(8,128)(2,1)S(1)} collective-permute-done((f16[144,1168]{1,0:T(8,128)(2,1)S(1)}, f16[144,1168]{1,0:T(8,128)(2,1)S(1)}, u32[]{:S(2)}, u32[]{:S(2)}) %collective-permute-start.25) | collective-permute-done | bytes 336416 | tf_op jit(solution)/shard_map/ppermute | solution.py:45
  (135 shorter events, 60.5 us)
Async XLA Ops:
  7.2 64.3 %all-gather.8.cloned.1.call-start = ((), (), s32[]{:S(2)}) async-start(), calls=%async_computation.1 | async-start | bytes 6225920 | tf_op jit(solution)/shard_map/all_gather | solution.py:237
  14.2 112.1 %all-gather.10.cloned.1.call-start = ((), (), s32[]{:S(2)}) async-start(), calls=%async_computation.2 | async-start | bytes 5898240 | tf_op jit(solution)/shard_map/all_gather | solution.py:237
  15.0 43.7 %collective-permute-start.5 = (bf16[1024,896]{1,0:T(8,128)(2,1)S(1)}, bf16[1024,896]{1,0:T(8,128)(2,1)}, u32[]{:S(2)}, u32[]{:S(2)}) collective-permute-start(bf16[1024,896]{1,0:T(8,128)(2,1)S(1)} %copy-done.3), channel_id=1, source_target_pairs={{0,1},{8,9},{32,33},{40,41},{64,65},{72,73},{96,97},{104,105},{16,... | collective-permute-start | bytes 5505032 | tf_op jit(solution)/shard_map/ppermute | solution.py:45
  15.2 43.4 %collective-permute-start.6 = (bf16[1024,896]{1,0:T(8,128)(2,1)S(1)}, bf16[1024,896]{1,0:T(8,128)(2,1)}, u32[]{:S(2)}, u32[]{:S(2)}) collective-permute-start(bf16[1024,896]{1,0:T(8,128)(2,1)S(1)} %copy-done.3), channel_id=1, source_target_pairs={{0,8},{8,0},{32,40},{40,32},{64,72},{72,64},{96,104},{104,96},{16,... | collective-permute-start | bytes 5505032 | tf_op jit(solution)/shard_map/ppermute | solution.py:45
  18.8 20.0 %collective-permute-start.8 = (bf16[132,1024]{1,0:T(8,128)(2,1)S(1)}, bf16[132,1024]{1,0:T(8,128)(2,1)S(1)}, u32[]{:S(2)}, u32[]{:S(2)}) collective-permute-start(bf16[132,1024]{1,0:T(8,128)(2,1)S(1)} %get-tuple-element.102), channel_id=1, source_target_pairs={{0,8},{8,0},{32,40},{40,32},{64,72},{72,64},{96,104},{104,96},{16,... | collective-permute-start | bytes 811016 | tf_op jit(solution)/shard_map/ppermute | solution.py:45
  20.1 20.9 %collective-permute-start.9 = (bf16[272,1024]{1,0:T(8,128)(2,1)S(1)}, bf16[272,1024]{1,0:T(8,128)(2,1)}, u32[]{:S(2)}, u32[]{:S(2)}) collective-permute-start(bf16[272,1024]{1,0:T(8,128)(2,1)S(1)} %pad.12.refs_4_), channel_id=1, source_target_pairs={{0,8},{8,0},{32,40},{40,32},{64,72},{72,64},{96,104},{104,96},{16,... | collective-permute-start | bytes 1671176 | tf_op jit(solution)/shard_map/ppermute | solution.py:45
  58.7 122.1 %all-gather.6.cloned.1.call-start = ((), (), s32[]{:S(2)}) async-start(), calls=%async_computation | async-start | bytes 1638400 | tf_op jit(solution)/shard_map/all_gather | solution.py:237
  58.7 10.8 %collective-permute-start.10 = (bf16[1024,896]{1,0:T(8,128)(2,1)}, bf16[1024,896]{1,0:T(8,128)(2,1)S(1)}, u32[]{:S(2)}, u32[]{:S(2)}) collective-permute-start(bf16[1024,896]{1,0:T(8,128)(2,1)} %collective-permute-done.5.refs_2_), channel_id=1, source_target_pairs={{0,8},{8,0},{32,40},{40,32},{64,72},{72,64},{96,104},{104,96},{16,... | collective-permute-start | bytes 5505032 | tf_op jit(solution)/shard_map/ppermute | solution.py:45
  85.0 21.4 %collective-permute-start.13 = (f16[2,304,896]{2,1,0:T(8,128)(2,1)}, f16[2,304,896]{2,1,0:T(8,128)(2,1)}, u32[]{:S(2)}, u32[]{:S(2)}) collective-permute-start(f16[2,304,896]{2,1,0:T(8,128)(2,1)} %multiply_convert_fusion.1), channel_id=1, source_target_pairs={{0,32},{8,104},{32,64},{40,8},{64,96},{72,40},{96,0},{104,72},{16,... | collective-permute-start | bytes 3268616 | tf_op jit(solution)/shard_map/ppermute | solution.py:45
  86.6 19.6 %collective-permute-start.17 = (bf16[272,1024]{1,0:T(8,128)(2,1)S(1)}, bf16[272,1024]{1,0:T(8,128)(2,1)S(1)}, u32[]{:S(2)}, u32[]{:S(2)}) collective-permute-start(bf16[272,1024]{1,0:T(8,128)(2,1)S(1)} %pad.12.refs_4_), channel_id=1, source_target_pairs={{0,1},{8,9},{32,33},{40,41},{64,65},{72,73},{96,97},{104,105},{16,... | collective-permute-start | bytes 1671176 | tf_op jit(solution)/shard_map/ppermute | solution.py:45
  88.1 38.2 %collective-permute-start.14 = (f32[4,1,80,512]{3,2,1,0:T(8,128)}, f32[4,1,80,512]{3,2,1,0:T(8,128)S(1)}, u32[]{:S(2)}, u32[]{:S(2)}) collective-permute-start(f32[4,1,80,512]{3,2,1,0:T(8,128)} %constant_dynamic-slice_fusion), channel_id=1, source_target_pairs={{0,1},{8,9},{32,33},{40,41},{64,65},{72,73},{96,97},{104,105},{16,... | collective-permute-start | bytes 1966088 | tf_op jit(solution)/shard_map/ppermute | solution.py:45
  93.9 59.5 %collective-permute-start.16 = (f16[2,304,896]{2,1,0:T(8,128)(2,1)}, f16[2,304,896]{2,1,0:T(8,128)(2,1)}, u32[]{:S(2)}, u32[]{:S(2)}) collective-permute-start(f16[2,304,896]{2,1,0:T(8,128)(2,1)} %multiply_convert_fusion), channel_id=1, source_target_pairs={{0,96},{8,40},{32,0},{40,72},{64,32},{72,104},{96,64},{104,8},{16,... | collective-permute-start | bytes 3268616 | tf_op jit(solution)/shard_map/ppermute | solution.py:45
  106.2 27.0 %collective-permute-start.18 = (bf16[272,1024]{1,0:T(8,128)(2,1)S(1)}, bf16[272,1024]{1,0:T(8,128)(2,1)S(1)}, u32[]{:S(2)}, u32[]{:S(2)}) collective-permute-start(bf16[272,1024]{1,0:T(8,128)(2,1)S(1)} %collective-permute-done.17.refs_6_), channel_id=1, source_target_pairs={{0,8},{8,0},{32,40},{40,32},{64,72},{72,64},{96,104},{104,96},{16,... | collective-permute-start | bytes 1671176 | tf_op jit(solution)/shard_map/ppermute | solution.py:45
  128.4 16.3 %collective-permute-start.26 = (f32[80,512]{1,0:T(8,128)S(1)}, f32[80,512]{1,0:T(8,128)S(1)}, u32[]{:S(2)}, u32[]{:S(2)}) collective-permute-start(f32[80,512]{1,0:T(8,128)S(1)} %get-tuple-element.98), channel_id=1, source_target_pairs={{0,2},{8,10},{32,34},{40,42},{64,66},{72,74},{96,98},{104,106},{16... | collective-permute-start | bytes 491528 | tf_op jit(solution)/shard_map/ppermute | solution.py:45
  129.4 15.3 %collective-permute-start.27 = (f32[80,512]{1,0:T(8,128)S(1)}, f32[80,512]{1,0:T(8,128)S(1)}, u32[]{:S(2)}, u32[]{:S(2)}) collective-permute-start(f32[80,512]{1,0:T(8,128)S(1)} %get-tuple-element.100), channel_id=1, source_target_pairs={{0,4},{8,12},{32,36},{40,44},{64,68},{72,76},{96,100},{104,108},{1... | collective-permute-start | bytes 491528 | tf_op jit(solution)/shard_map/ppermute | solution.py:45
  131.1 13.5 %collective-permute-start.28 = (f32[80,512]{1,0:T(8,128)S(1)}, f32[80,512]{1,0:T(8,128)S(1)}, u32[]{:S(2)}, u32[]{:S(2)}) collective-permute-start(f32[80,512]{1,0:T(8,128)S(1)} %get-tuple-element.99), channel_id=1, source_target_pairs={{0,6},{8,14},{32,38},{40,46},{64,70},{72,78},{96,102},{104,110},{1... | collective-permute-start | bytes 491528 | tf_op jit(solution)/shard_map/ppermute | solution.py:45
  133.2 20.1 %collective-permute-start.15 = (f16[2,304,896]{2,1,0:T(8,128)(2,1)}, f16[2,304,896]{2,1,0:T(8,128)(2,1)}, u32[]{:S(2)}, u32[]{:S(2)}) collective-permute-start(f16[2,304,896]{2,1,0:T(8,128)(2,1)} %add_convert_fusion), channel_id=1, source_target_pairs={{0,32},{8,104},{32,64},{40,8},{64,96},{72,40},{96,0},{104,72},{16,... | collective-permute-start | bytes 3268616 | tf_op jit(solution)/shard_map/ppermute | solution.py:45
  156.1 14.4 %collective-permute-start.19 = (f16[304,896]{1,0:T(8,128)(2,1)S(1)}, f16[304,896]{1,0:T(8,128)(2,1)S(1)}, u32[]{:S(2)}, u32[]{:S(2)}) collective-permute-start(f16[304,896]{1,0:T(8,128)(2,1)S(1)} %fusion.3), channel_id=1, source_target_pairs={{0,16},{8,24},{32,48},{40,56},{64,80},{72,88},{96,112},{104,120},{... | collective-permute-start | bytes 1634312 | tf_op jit(solution)/shard_map/ppermute | solution.py:45
  157.4 18.7 %collective-permute-start.21 = (f16[2,144,1168]{2,1,0:T(8,128)(2,1)}, f16[2,144,1168]{2,1,0:T(8,128)(2,1)}, u32[]{:S(2)}, u32[]{:S(2)}) collective-permute-start(f16[2,144,1168]{2,1,0:T(8,128)(2,1)} %get-tuple-element.84), channel_id=1, source_target_pairs={{0,32},{8,104},{32,64},{40,8},{64,96},{72,40},{96,0},{104,72},{16,... | collective-permute-start | bytes 2018312 | tf_op jit(solution)/shard_map/ppermute | solution.py:45
  158.0 25.1 %collective-permute-start.23 = (f16[2,144,1168]{2,1,0:T(8,128)(2,1)S(1)}, f16[2,144,1168]{2,1,0:T(8,128)(2,1)}, u32[]{:S(2)}, u32[]{:S(2)}) collective-permute-start(f16[2,144,1168]{2,1,0:T(8,128)(2,1)S(1)} %get-tuple-element.85), channel_id=1, source_target_pairs={{0,96},{8,40},{32,0},{40,72},{64,32},{72,104},{96,64},{104,8},{16,... | collective-permute-start | bytes 2018312 | tf_op jit(solution)/shard_map/ppermute | solution.py:45
  178.3 13.1 %collective-permute-start.22 = (f16[2,144,1168]{2,1,0:T(8,128)(2,1)}, f16[2,144,1168]{2,1,0:T(8,128)(2,1)}, u32[]{:S(2)}, u32[]{:S(2)}) collective-permute-start(f16[2,144,1168]{2,1,0:T(8,128)(2,1)} %add_convert_fusion.1), channel_id=1, source_target_pairs={{0,32},{8,104},{32,64},{40,8},{64,96},{72,40},{96,0},{104,72},{16,... | collective-permute-start | bytes 2018312 | tf_op jit(solution)/shard_map/ppermute | solution.py:45
  178.8 12.6 %collective-permute-start.20 = (f16[304,896]{1,0:T(8,128)(2,1)}, f16[304,896]{1,0:T(8,128)(2,1)}, u32[]{:S(2)}, u32[]{:S(2)}) collective-permute-start(f16[304,896]{1,0:T(8,128)(2,1)} %add_convert_fusion.2), channel_id=1, source_target_pairs={{16,1},{24,9},{48,33},{56,41},{80,65},{88,73},{112,97},{120,105},{... | collective-permute-start | bytes 1634312 | tf_op jit(solution)/shard_map/ppermute | solution.py:45
  193.2 9.2 %collective-permute-start.24 = (f16[144,1168]{1,0:T(8,128)(2,1)S(1)}, f16[144,1168]{1,0:T(8,128)(2,1)S(1)}, u32[]{:S(2)}, u32[]{:S(2)}) collective-permute-start(f16[144,1168]{1,0:T(8,128)(2,1)S(1)} %select_convert_fusion), channel_id=1, source_target_pairs={{0,1},{8,9},{32,33},{40,41},{64,65},{72,73},{96,97},{104,105},{16,... | collective-permute-start | bytes 1009160 | tf_op jit(solution)/shard_map/ppermute | solution.py:45
  194.0 14.3 %collective-permute-start.25 = (f16[144,1168]{1,0:T(8,128)(2,1)S(1)}, f16[144,1168]{1,0:T(8,128)(2,1)S(1)}, u32[]{:S(2)}, u32[]{:S(2)}) collective-permute-start(f16[144,1168]{1,0:T(8,128)(2,1)S(1)} %fusion.5), channel_id=1, source_target_pairs={{16,1},{24,9},{48,33},{56,41},{80,65},{88,73},{112,97},{120,105},{... | collective-permute-start | bytes 1009160 | tf_op jit(solution)/shard_map/ppermute | solution.py:45
  (27 other events, 183.3 us)
Sparse Core Ops, SparseCore 0:
  14.4 57.0 all-gather.7
  73.1 53.1 all-gather.9
  153.4 23.3 all-gather.5
